TPU v7x, 32 devices: a whole 2x2x4 slice. The times are simulated.
32 devices in a mesh: dp: 4 (over y, x), blk: 8 (over z, core).
Axes of the slice: x: 2, y: 2, z: 4, core: 2. Of those that a mesh axis runs over, the one named last changes fastest.
Arguments:
- tokens: bfloat16 [16, 2048, 512], P('dp', 'blk'), may hold values from -6 to 6
- teacher_tokens: bfloat16 [16, 2048, 512], P('dp', 'blk'), may hold values from -6 to 6
- segment_ids: int32 [16, 2048], P('dp', 'blk'), may hold values from 0 to 510, as said below
- cotangent: bfloat16 [16, 2048, 512], P('dp', 'blk'), may hold values from -6 to 6
- latent_qkv: bfloat16 [3, 512, 512], replicated, may hold values from -0.375 to 0.375
- latent_out: bfloat16 [512, 512], replicated, may hold values from -1.5 to 1.5
- latent_up: bfloat16 [512, 2048], replicated, may hold values from -0.25 to 0.25
- latent_down: bfloat16 [2048, 512], replicated, may hold values from -0.125 to 0.125
- student_gain: float32 [2, 512], replicated, may hold values from 0.25 to 1.75
- student_bias: float32 [6, 512], replicated, may hold values from -3 to 3
- student_up_bias: float32 [2048], replicated, may hold values from -3 to 3
- teacher_qkv: bfloat16 [3, 512, 512], P(None, 'dp'), may hold values from -0.375 to 0.375
- teacher_out: bfloat16 [512, 512], P('dp'), may hold values from -1.5 to 1.5
- teacher_up: bfloat16 [512, 2048], P('dp'), may hold values from -0.25 to 0.25
- teacher_down: bfloat16 [2048, 512], P('dp'), may hold values from -0.125 to 0.125
- teacher_gain: float32 [2, 512], replicated, may hold values from 0.25 to 1.75
- teacher_bias: float32 [6, 512], replicated, may hold values from -3 to 3
- teacher_up_bias: float32 [2048], replicated, may hold values from -3 to 3
Outputs:
- output: bfloat16 [16, 2048, 512], P('dp', 'blk')
- grad_tokens: bfloat16 [16, 2048, 512], P('dp', 'blk')
- grad_latent_qkv: float32 [3, 512, 512], replicated
- grad_latent_out: float32 [512, 512], replicated
- grad_latent_up: float32 [512, 2048], replicated
- grad_latent_down: float32 [2048, 512], replicated
- grad_student_gain: float32 [2, 512], replicated
- grad_student_bias: float32 [6, 512], replicated
- grad_student_up_bias: float32 [2048], replicated
Inputs may be any that keep to these rules, and one draw needn't show every extreme that they name: `segment_ids`: in each stream the ids start at 0 and never fall; one document of every stream begins within its first 256 tokens and ends within its last 256 tokens.
All inputs are finite; a program needn't handle non-finite values.
Results may differ from a plain program's by a relative error of at most 0.014.
Values may be sent and summed in bfloat16 or wider, within the bound.
A program may use at most 384 MiB of HBM per device.

v0:
```python
import jax
import jax.numpy as jnp
from jax import lax
from jax.sharding import PartitionSpec as P

HEADS = 8


clip_level = 2.5
masked_score = -1e30


def shifted(block, axis, distance):
    devices = range(lax.axis_size(axis))
    route = [((i - distance) % len(devices), i) for i in devices]
    return lax.ppermute(block, axis, route)


def squash(tensor):
    return clip_level * jnp.tanh(tensor / clip_level)


def squash_slope(tensor):
    bent = jnp.tanh(tensor / clip_level)
    return 1.0 - bent * bent


def gelu(tensor):
    return 0.5 * tensor * (1.0 + lax.erf(tensor * 0.7071067811865476))


def gelu_slope(tensor):
    return (
        0.5 * (1.0 + lax.erf(tensor * 0.7071067811865476))
        + tensor * jnp.exp(-0.5 * tensor * tensor) * 0.3989422804014327
    )


def binarize(matrix):
    column_scale = jnp.sqrt(jnp.mean(matrix * matrix, axis=-2, keepdims=True) + 1e-06)
    return column_scale * jnp.tanh(2.0 * matrix / column_scale)


def layer_norm(tensor, gain_row, shift_row):
    centre = tensor - jnp.mean(tensor, axis=-1, keepdims=True)
    inverse_std = lax.rsqrt(jnp.mean(centre * centre, axis=-1, keepdims=True) + 1e-05)
    normed = centre * inverse_std
    return (normed * gain_row + shift_row, normed, inverse_std)


def norm_back(upstream, gain_row, normed, inverse_std):
    scaled = upstream * gain_row
    return inverse_std * (
        scaled
        - jnp.mean(scaled, axis=-1, keepdims=True)
        - normed * jnp.mean(scaled * normed, axis=-1, keepdims=True)
    )


def row_total(tensor):
    return jnp.sum(tensor.astype(jnp.float32), axis=(0, 1))


def heads_of(tensor):
    return tensor.reshape(tensor.shape[0], tensor.shape[1], HEADS, tensor.shape[2] // HEADS)


def project(tensor, matrix):
    return jnp.einsum("bsd,de->bse", tensor, matrix, preferred_element_type=jnp.float32)


def online_step(state, queries, key_rows, value_rows, same_doc):
    row_max, row_sum, weighted = state
    scores = (
        jnp.einsum("bqhd,bkhd->bhqk", queries, key_rows, preferred_element_type=jnp.float32) * 0.125
    )
    scores = jnp.where(same_doc, scores, masked_score)
    new_max = jnp.maximum(row_max, jnp.max(scores, axis=-1))
    numerators = jnp.where(same_doc, jnp.exp(scores - new_max[..., None]), 0.0)
    row_sum = jnp.sum(numerators, axis=-1)
    weighted = jnp.einsum(
        "bhqk,bkhd->bqhd",
        numerators.astype(jnp.bfloat16),
        value_rows,
        preferred_element_type=jnp.float32,
    )
    return (new_max, row_sum, weighted)


def latent_grad(latent, binary_grad):
    unused, pullback = jax.vjp(binarize, latent.astype(jnp.float32))
    return pullback(binary_grad)[0]


def shards(
    tokens,
    teacher_tokens,
    segment_ids,
    cotangent,
    latent_qkv,
    latent_out,
    latent_up,
    latent_down,
    student_gain,
    student_bias,
    student_up_bias,
    teacher_qkv,
    teacher_out,
    teacher_up,
    teacher_down,
    teacher_gain,
    teacher_bias,
    teacher_up_bias,
):
    streams, shard_len, model_width = tokens.shape
    head_dim = model_width // HEADS
    seq_total = shard_len * lax.axis_size("blk")
    float_tokens = tokens.astype(jnp.float32)
    bin_qkv = binarize(latent_qkv.astype(jnp.float32)).astype(jnp.bfloat16)
    bin_out = binarize(latent_out.astype(jnp.float32)).astype(jnp.bfloat16)
    bin_up = binarize(latent_up.astype(jnp.float32)).astype(jnp.bfloat16)
    bin_down = binarize(latent_down.astype(jnp.float32)).astype(jnp.bfloat16)
    full_qkv, full_out, full_up, full_down = (
        lax.all_gather(teacher_qkv, "dp", axis=1, tiled=True),
        lax.all_gather(teacher_out, "dp", axis=0, tiled=True),
        lax.all_gather(teacher_up, "dp", axis=0, tiled=True),
        lax.all_gather(teacher_down, "dp", axis=0, tiled=True),
    )
    teacher_proj = jnp.einsum(
        "bsd,kde->kbse", teacher_tokens, full_qkv, preferred_element_type=jnp.float32
    )
    teacher_queries = (teacher_proj[0] + teacher_bias[0]).astype(jnp.bfloat16)
    teacher_keys = teacher_proj[1].astype(jnp.bfloat16)
    teacher_values = (teacher_proj[2] + teacher_bias[1]).astype(jnp.bfloat16)
    active = squash(float_tokens).astype(jnp.bfloat16)
    projected = jnp.einsum("bsd,kde->kbse", active, bin_qkv, preferred_element_type=jnp.float32)
    queries = (projected[0] + student_bias[0]).astype(jnp.bfloat16)
    key_rows = projected[1].astype(jnp.bfloat16)
    value_rows = (projected[2] + student_bias[1]).astype(jnp.bfloat16)
    query_heads = heads_of(queries)
    teacher_heads = heads_of(teacher_queries)
    start_max = jnp.full((streams, HEADS, shard_len), masked_score, jnp.float32)
    start_sum = jnp.zeros((streams, HEADS, shard_len), jnp.float32)
    start_acc = jnp.zeros((streams, shard_len, HEADS, head_dim), jnp.float32)
    folded = ((start_max, start_sum, start_acc), (start_max, start_sum, start_acc))
    piece_keys = lax.all_gather(key_rows, "blk", axis=1, tiled=True)
    piece_values = lax.all_gather(value_rows, "blk", axis=1, tiled=True)
    piece_tkeys = lax.all_gather(teacher_keys, "blk", axis=1, tiled=True)
    piece_tvalues = lax.all_gather(teacher_values, "blk", axis=1, tiled=True)
    piece_docs = lax.all_gather(segment_ids, "blk", axis=1, tiled=True)
    same_doc = segment_ids[:, None, :, None] == piece_docs[:, None, None, :]
    student_state = online_step(
        folded[0], query_heads, heads_of(piece_keys), heads_of(piece_values), same_doc
    )
    teacher_state = online_step(
        folded[1], teacher_heads, heads_of(piece_tkeys), heads_of(piece_tvalues), same_doc
    )
    student_state, teacher_state = (student_state, teacher_state)
    context_heads = student_state[2] / jnp.transpose(student_state[1], (0, 2, 1))[..., None]
    log_total = student_state[0] + jnp.log(student_state[1])
    teacher_context = (
        teacher_state[2] / jnp.transpose(teacher_state[1], (0, 2, 1))[..., None]
    ).reshape(streams, shard_len, model_width)
    context = context_heads.reshape(streams, shard_len, model_width)
    teacher_attended = project(teacher_context.astype(jnp.bfloat16), full_out) + teacher_bias[2]
    teacher_hidden, unused_one, unused_two = layer_norm(
        teacher_tokens.astype(jnp.float32) + teacher_attended, teacher_gain[0], teacher_bias[3]
    )
    teacher_inner = gelu(project(teacher_hidden.astype(jnp.bfloat16), full_up) + teacher_up_bias)
    teacher_output, unused_three, unused_four = layer_norm(
        teacher_hidden + project(teacher_inner.astype(jnp.bfloat16), full_down) + teacher_bias[4],
        teacher_gain[1],
        teacher_bias[5],
    )
    context_active = squash(context).astype(jnp.bfloat16)
    attended = project(context_active, bin_out) + student_bias[2]
    hidden, normed_one, inverse_one = layer_norm(
        float_tokens + attended, student_gain[0], student_bias[3]
    )
    hidden_active = squash(hidden).astype(jnp.bfloat16)
    inner_pre = project(hidden_active, bin_up) + student_up_bias
    inner_act = gelu(inner_pre)
    inner_active = squash(inner_act).astype(jnp.bfloat16)
    branch = project(inner_active, bin_down) + student_bias[4]
    output, normed_two, inverse_two = layer_norm(hidden + branch, student_gain[1], student_bias[5])
    upstream = cotangent.astype(jnp.float32) + 0.5 * (output - teacher_output)
    d_resid_two = norm_back(upstream, student_gain[1], normed_two, inverse_two)
    d_branch = d_resid_two.astype(jnp.bfloat16)
    grad_down_bin = jnp.einsum(
        "bsf,bsd->fd", inner_active, d_branch, preferred_element_type=jnp.float32
    )
    d_inner = (
        jnp.einsum("bsd,fd->bsf", d_branch, bin_down, preferred_element_type=jnp.float32)
        * squash_slope(inner_act)
        * gelu_slope(inner_pre)
    ).astype(jnp.bfloat16)
    grad_up_bin = jnp.einsum(
        "bsd,bsf->df", hidden_active, d_inner, preferred_element_type=jnp.float32
    )
    d_hidden = d_resid_two + jnp.einsum(
        "bsf,df->bsd", d_inner, bin_up, preferred_element_type=jnp.float32
    ) * squash_slope(hidden)
    d_resid_one = norm_back(d_hidden, student_gain[0], normed_one, inverse_one)
    d_attended = d_resid_one.astype(jnp.bfloat16)
    grad_out_bin = jnp.einsum(
        "bsd,bse->de", context_active, d_attended, preferred_element_type=jnp.float32
    )
    d_context = (
        jnp.einsum("bse,de->bsd", d_attended, bin_out, preferred_element_type=jnp.float32)
        * squash_slope(context)
    ).astype(jnp.bfloat16)
    d_context_heads = heads_of(d_context)
    delta_rows = jnp.transpose(
        jnp.sum(d_context_heads.astype(jnp.float32) * context_heads, axis=-1), (0, 2, 1)
    )

    def key_terms(piece_keys, piece_values, piece_tkeys, piece_docs):
        same_doc = segment_ids[:, None, :, None] == piece_docs[:, None, None, :]
        key_heads = heads_of(piece_keys)
        scores = (
            jnp.einsum(
                "bqhd,bkhd->bhqk", query_heads, key_heads, preferred_element_type=jnp.float32
            )
            * 0.125
        )
        teacher_scores = (
            jnp.einsum(
                "bqhd,bkhd->bhqk",
                teacher_heads,
                heads_of(piece_tkeys),
                preferred_element_type=jnp.float32,
            )
            * 0.125
        )
        attn_probs = jnp.where(same_doc, jnp.exp(scores - log_total[..., None]), 0.0)
        d_probs = jnp.einsum(
            "bqhd,bkhd->bhqk",
            d_context_heads,
            heads_of(piece_values),
            preferred_element_type=jnp.float32,
        )
        d_scores = attn_probs * (d_probs - delta_rows[..., None]) + jnp.where(
            same_doc, (scores - teacher_scores) / seq_total, 0.0
        )
        d_scores = d_scores.astype(jnp.bfloat16)
        part_query = (
            jnp.einsum("bhqk,bkhd->bqhd", d_scores, key_heads, preferred_element_type=jnp.float32)
            * 0.125
        )
        part_key = (
            jnp.einsum("bhqk,bqhd->bkhd", d_scores, query_heads, preferred_element_type=jnp.float32)
            * 0.125
        )
        part_value = jnp.einsum(
            "bhqk,bqhd->bkhd",
            attn_probs.astype(jnp.bfloat16),
            d_context_heads,
            preferred_element_type=jnp.float32,
        )
        key_shape = (piece_keys.shape[0], piece_keys.shape[1], model_width)
        return (part_query, part_key.reshape(key_shape), part_value.reshape(key_shape))

    zeros_query = jnp.zeros((streams, shard_len, HEADS, head_dim), jnp.float32)
    zeros_keys = jnp.zeros((streams, shard_len, model_width), jnp.float32)

    def cycle_turn(turn_index, folded):
        cycle_keys, cycle_values, cycle_tkeys, cycle_docs, key_grad, value_grad, query_grad = folded
        part_query, part_key, part_value = key_terms(
            cycle_keys, cycle_values, cycle_tkeys, cycle_docs
        )
        cycle_keys, cycle_values, cycle_tkeys, cycle_docs = shifted(
            (cycle_keys, cycle_values, cycle_tkeys, cycle_docs), "blk", 1
        )
        key_grad, value_grad = (
            shifted((key_grad + part_key).astype(jnp.bfloat16), "blk", 1).astype(jnp.float32),
            shifted((value_grad + part_value).astype(jnp.bfloat16), "blk", 1).astype(jnp.float32),
        )
        return (
            cycle_keys,
            cycle_values,
            cycle_tkeys,
            cycle_docs,
            key_grad,
            value_grad,
            query_grad + part_query,
        )

    result = lax.fori_loop(
        0,
        lax.axis_size("blk"),
        cycle_turn,
        (key_rows, value_rows, teacher_keys, segment_ids, zeros_keys, zeros_keys, zeros_query),
    )
    query_grad, key_grad, value_grad = (result[6], result[4], result[5])
    d_queries = query_grad.reshape(streams, shard_len, model_width).astype(jnp.bfloat16)
    d_keys = key_grad.astype(jnp.bfloat16)
    d_values = value_grad.astype(jnp.bfloat16)
    d_qkv = jnp.stack([d_queries, d_keys, d_values])
    grad_qkv_bin = jnp.einsum("bsd,kbse->kde", active, d_qkv, preferred_element_type=jnp.float32)
    d_active = jnp.einsum("kbse,kde->bsd", d_qkv, bin_qkv, preferred_element_type=jnp.float32)
    grad_tokens = (d_resid_one + d_active * squash_slope(float_tokens)).astype(jnp.bfloat16)
    grad_gain = jnp.stack([row_total(d_hidden * normed_one), row_total(upstream * normed_two)])
    grad_bias = jnp.stack(
        [
            row_total(d_queries),
            row_total(d_values),
            row_total(d_attended),
            row_total(d_hidden),
            row_total(d_branch),
            row_total(upstream),
        ]
    )
    grad_up_shift = row_total(d_inner)
    partials = (
        grad_qkv_bin,
        grad_out_bin,
        grad_up_bin,
        grad_down_bin,
        grad_gain,
        grad_bias,
        grad_up_shift,
    )
    summed = lax.psum(
        (partials[0], partials[1], partials[2], partials[3], partials[4], partials[5], partials[6]),
        ("dp", "blk"),
    )
    return (
        output.astype(jnp.bfloat16),
        grad_tokens,
        latent_grad(latent_qkv, summed[0]),
        latent_grad(latent_out, summed[1]),
        latent_grad(latent_up, summed[2]),
        latent_grad(latent_down, summed[3]),
        summed[4],
        summed[5],
        summed[6],
    )


def solution(mesh):
    return jax.shard_map(
        shards,
        mesh=mesh,
        in_specs=(
            P("dp", "blk", None),
            P("dp", "blk", None),
            P("dp", "blk"),
            P("dp", "blk", None),
            P(),
            P(),
            P(),
            P(),
            P(),
            P(),
            P(),
            P(None, "dp", None),
            P("dp", None),
            P("dp", None),
            P("dp", None),
            P(),
            P(),
            P(),
        ),
        out_specs=(P("dp", "blk", None), P("dp", "blk", None), P(), P(), P(), P(), P(), P(), P()),
        check_vma=False,
    )
```

profile of v0, /device:TPU:0, one launch (start us, length us, event | category | flops | bytes accessed | tf_op | source)
XLA Modules:
  0.0 1503.4 jit_solution(4287829762037666849)
XLA Ops:
  18.0 26.0 %all-gather.12.cloned.1.call-done = bf16[3,512,512]{1,2,0:T(8,128)(2,1)} async-done(((bf16[3,128,512]{1,2,0:T(8,128)(2,1)}), bf16[3,512,512]{1,2,0:T(8,128)(2,1)}) %all-gather.12.cloned.1.call-update) | async-done | bytes 1572880 | tf_op jit(solution)/shard_map/all_gather | solution.py:124
  64.7 19.8 %all_gather.28 = s32[4,2048]{1,0:T(4,128)S(1)} all-gather(s32[4,256]{1,0:T(4,128)S(1)} %copy-done.30), channel_id=1, replica_groups=mesh['dp'=4,'blk'=8] {'blk'}, dimensions={1}, use_global_device_ids=true | all-gather | bytes 36864 | tf_op jit(solution)/shard_map/all_gather | solution.py:150
  86.6 10.8 all_gather.33
  111.6 17.3 %all-gather.20.cloned.1.call-done = bf16[1,4,2048,512]{2,3,1,0:T(8,128)(2,1)} async-done(((bf16[1,4,256,512]{2,3,1,0:T(8,128)(2,1)}), bf16[1,4,2048,512]{2,3,1,0:T(8,128)(2,1)}) %all-gather.20.cloned.1.call-update) | async-done | bytes 8388624 | tf_op jit(solution)/shard_map/all_gather | solution.py:146
  128.9 27.8 %fusion.154 = f32[4,8,256,2048]{3,2,1,0:T(8,128)} fusion(bf16[4,256,8,64]{1,3,2,0:T(8,128)(2,1)S(1)} %add_convert_fusion.2, bf16[4,2048,8,64]{1,3,2,0:T(8,128)(2,1)} %bitcast.230), kind=kOutput, calls=%fused_computation.247 | convolution fusion | flops 2147483648 | bytes 76546048 | tf_op jit(solution)/shard_map/bqhd,bkhd->bhqk/dot_general | solution.py:75
  156.7 55.1 %all-gather.22.cloned.1.call-done = bf16[1,4,2048,512]{2,3,1,0:T(8,128)(2,1)} async-done(((bf16[1,4,256,512]{2,3,1,0:T(8,128)(2,1)}), bf16[1,4,2048,512]{2,3,1,0:T(8,128)(2,1)}) %all-gather.22.cloned.1.call-update) | async-done | bytes 8388624 | tf_op jit(solution)/shard_map/all_gather | solution.py:148
  211.8 54.0 %fusion.12 = (f32[4,8,256]{2,1,0:T(8,128)S(1)}, f32[4,8,256]{2,1,0:T(8,128)S(1)}, f32[4,8,256,2048]{3,2,1,0:T(8,128)}) fusion(pred[4,256,2048]{2,1,0:T(8,128)(4,1)S(1)} %broadcast_compare_fusion.1, f32[4,8,256,2048]{3,2,1,0:T(8,128)} %fusion.154, bf16[4,256,8,64]{1,3,2,0:T(8,128)(2,1)} %add_convert_fusion.1, bf16[4,2048,8,64]{1,3,2,0:T(8,128)(2,1)} %bitcast.231), kind=kOutput, calls=%fused_computation.22 | convolution fusion | flops 2248130560 | bytes 145817600 | tf_op jit(solution)/shard_map/bqhd,bkhd->bhqk/dot_general | solution.py:75
  265.9 43.2 %fusion.15 = (f32[4,8,256]{2,1,0:T(8,128)S(1)}, f32[4,8,256]{2,1,0:T(8,128)S(1)}) fusion(f32[4,8,256,2048]{3,2,1,0:T(8,128)} %get-tuple-element.238, f32[4,8,256]{2,1,0:T(8,128)S(1)} %broadcast_maximum_fusion, pred[4,256,2048]{2,1,0:T(8,128)(4,1)S(1)} %broadcast_compare_fusion.1, f32[4,8,256]{2,1,0:T(8,128)S(1)} %broadcast_maximum_fusion.1, ...), kind=kLoop, calls=%fused_computation.25 | loop fusion | flops 167755776 | bytes 136445952 | tf_op jit(solution)/shard_map/reduce_sum | solution.py:80
  309.2 29.3 %fusion.62 = bf16[4,256,8,64]{1,3,2,0:T(8,128)(2,1)} fusion(bf16[4,2048,8,64]{1,3,2,0:T(8,128)(2,1)} %bitcast.275, f32[4,8,256,2048]{3,2,1,0:T(8,128)} %get-tuple-element.238, f32[4,8,256]{2,1,0:T(8,128)S(1)} %broadcast_maximum_fusion, pred[4,256,2048]{2,1,0:T(8,128)(4,1)S(1)} %broadcast_compare_fusion.1, f32[4,256,8]{1,2,0:T(8,128)S(1)} %bitcast.242), kind=kOutput, calls=%fused_computation.110 | convolution fusion | flops 2232418304 | bytes 78708736 | tf_op jit(solution)/shard_map/bhqk,bkhd->bqhd/dot_general | solution.py:81
  342.8 24.1 %all-gather.18.cloned.1.call-done = bf16[2048,512]{1,0:T(8,128)(2,1)} async-done(((bf16[512,512]{1,0:T(8,128)(2,1)}), bf16[2048,512]{1,0:T(8,128)(2,1)}) %all-gather.18.cloned.1.call-update) | async-done | bytes 2097168 | tf_op jit(solution)/shard_map/all_gather | solution.py:127
  366.9 9.8 fusion.147
  379.1 71.9 %all-gather.10.cloned.1.call-done = bf16[4,2048,512]{1,2,0:T(8,128)(2,1)} async-done(((bf16[4,256,512]{1,2,0:T(8,128)(2,1)}), bf16[4,2048,512]{1,2,0:T(8,128)(2,1)}) %all-gather.10.cloned.1.call-update) | async-done | bytes 8388624 | tf_op jit(solution)/shard_map/all_gather | solution.py:147
  451.0 30.0 %multiply_subtract_fusion = (f32[4,256,8,64]{1,3,2,0:T(8,128)}, bf16[4,256,8,64]{1,3,2,0:T(8,128)(2,1)}, f32[4,256,8,64]{1,3,2,0:T(8,128)}) fusion(f32[4,256,8]{1,2,0:T(8,128)S(1)} %bitcast.240, bf16[4,2048,8,64]{1,3,2,0:T(8,128)(2,1)} %bitcast.274, f32[4,8,256,2048]{3,2,1,0:T(8,128)} %fusion.154, f32[4,8,256]{2,1,0:T(8,128)S(1)} %broadcast_maximum_fusion.1, ...), kind=kOutput, calls=%fused_computation.120 | convolution fusion | flops 2234515456 | bytes 82903040 | tf_op jit(solution)/shard_map/bhqk,bkhd->bqhd/dot_general | solution.py:81
  484.3 4.5 multiply_convert_fusion.1
  498.1 4.5 convolution_bitcast_fusion
  502.6 8.2 convert_reduce_fusion
  510.8 5.7 multiply_reduce_fusion.4
  516.5 4.7 convolution_bitcast_fusion.1
  534.3 691.4 %while.23 = (s32[]{:T(128)}, bf16[4,256,512]{1,2,0:T(8,128)(2,1)}, bf16[4,256,512]{1,2,0:T(8,128)(2,1)}, bf16[4,256,512]{1,2,0:T(8,128)(2,1)}, s32[4,256]{1,0:T(...) while((s32[]{:T(128)}, bf16[4,256,512]{1,2,0:T(8,128)(2,1)}, ...), condition=%wide.region_22.23_spmd.clone, body=%wide.region_21.22_spmd.clone.sunk | while | flops 1648623616 | bytes 197001776 | solution.py:288
  541.6 4.4 fusion.212
  546.2 6.9 add_convert_fusion.4
  559.5 4.9 fusion.215
  567.2 8.2 collective-permute-done.4
  581.0 5.6 collective-permute-done.5
  589.4 31.0 %collective-permute-done.3 = s32[4,256]{1,0:T(4,128)S(1)} collective-permute-done((s32[4,256]{1,0:T(4,128)S(1)}, s32[4,256]{1,0:T(4,128)S(1)}, u32[]{:S(2)}, u32[]{:S(2)}) %collective-permute-start.3) | collective-permute-done | bytes 4128 | tf_op jit(solution)/shard_map/while/body/eval_jaxpr/ppermute | solution.py:16
  627.4 4.4 fusion.212
  632.1 6.9 add_convert_fusion.4
  645.8 4.9 fusion.215
  652.1 9.8 collective-permute-done.4
  675.9 31.0 %collective-permute-done.3 = s32[4,256]{1,0:T(4,128)S(1)} collective-permute-done((s32[4,256]{1,0:T(4,128)S(1)}, s32[4,256]{1,0:T(4,128)S(1)}, u32[]{:S(2)}, u32[]{:S(2)}) %collective-permute-start.3) | collective-permute-done | bytes 4128 | tf_op jit(solution)/shard_map/while/body/eval_jaxpr/ppermute | solution.py:16
  713.9 4.4 fusion.212
  718.6 6.9 add_convert_fusion.4
  732.3 4.9 fusion.215
  738.5 9.8 collective-permute-done.4
  762.4 31.0 %collective-permute-done.3 = s32[4,256]{1,0:T(4,128)S(1)} collective-permute-done((s32[4,256]{1,0:T(4,128)S(1)}, s32[4,256]{1,0:T(4,128)S(1)}, u32[]{:S(2)}, u32[]{:S(2)}) %collective-permute-start.3) | collective-permute-done | bytes 4128 | tf_op jit(solution)/shard_map/while/body/eval_jaxpr/ppermute | solution.py:16
  800.4 4.4 fusion.212
  805.0 6.9 add_convert_fusion.4
  818.7 4.9 fusion.215
  825.0 9.8 collective-permute-done.4
  848.8 31.0 %collective-permute-done.3 = s32[4,256]{1,0:T(4,128)S(1)} collective-permute-done((s32[4,256]{1,0:T(4,128)S(1)}, s32[4,256]{1,0:T(4,128)S(1)}, u32[]{:S(2)}, u32[]{:S(2)}) %collective-permute-start.3) | collective-permute-done | bytes 4128 | tf_op jit(solution)/shard_map/while/body/eval_jaxpr/ppermute | solution.py:16
  886.9 4.4 fusion.212
  891.5 6.9 add_convert_fusion.4
  905.2 4.9 fusion.215
  911.5 9.8 collective-permute-done.4
  935.3 31.0 %collective-permute-done.3 = s32[4,256]{1,0:T(4,128)S(1)} collective-permute-done((s32[4,256]{1,0:T(4,128)S(1)}, s32[4,256]{1,0:T(4,128)S(1)}, u32[]{:S(2)}, u32[]{:S(2)}) %collective-permute-start.3) | collective-permute-done | bytes 4128 | tf_op jit(solution)/shard_map/while/body/eval_jaxpr/ppermute | solution.py:16
  973.4 4.4 fusion.212
  978.0 6.9 add_convert_fusion.4
  991.7 4.9 fusion.215
  998.0 9.8 collective-permute-done.4
  1021.8 31.0 %collective-permute-done.3 = s32[4,256]{1,0:T(4,128)S(1)} collective-permute-done((s32[4,256]{1,0:T(4,128)S(1)}, s32[4,256]{1,0:T(4,128)S(1)}, u32[]{:S(2)}, u32[]{:S(2)}) %collective-permute-start.3) | collective-permute-done | bytes 4128 | tf_op jit(solution)/shard_map/while/body/eval_jaxpr/ppermute | solution.py:16
  1059.8 4.4 fusion.212
  1064.5 6.9 add_convert_fusion.4
  1078.2 4.9 fusion.215
  1084.4 9.8 collective-permute-done.4
  1108.3 31.0 %collective-permute-done.3 = s32[4,256]{1,0:T(4,128)S(1)} collective-permute-done((s32[4,256]{1,0:T(4,128)S(1)}, s32[4,256]{1,0:T(4,128)S(1)}, u32[]{:S(2)}, u32[]{:S(2)}) %collective-permute-start.3) | collective-permute-done | bytes 4128 | tf_op jit(solution)/shard_map/while/body/eval_jaxpr/ppermute | solution.py:16
  1146.3 4.4 fusion.212
  1150.9 6.9 add_convert_fusion.4
  1164.6 4.9 fusion.215
  1170.9 9.8 collective-permute-done.4
  1194.7 31.0 %collective-permute-done.3 = s32[4,256]{1,0:T(4,128)S(1)} collective-permute-done((s32[4,256]{1,0:T(4,128)S(1)}, s32[4,256]{1,0:T(4,128)S(1)}, u32[]{:S(2)}, u32[]{:S(2)}) %collective-permute-start.3) | collective-permute-done | bytes 4128 | tf_op jit(solution)/shard_map/while/body/eval_jaxpr/ppermute | solution.py:16
  1234.0 5.4 convolution_bitcast_fusion.4
  1240.2 40.3 %all-reduce = (f32[2,512]{1,0:T(2,128)}, f32[6,512]{1,0:T(8,128)}, f32[2048]{0:T(1024)}) all-reduce(f32[2,512]{1,0:T(2,128)S(1)} %pad_maximum_fusion.3, f32[6,512]{1,0:T(8,128)S(1)} %stack.52, f32[2048]{0:T(1024)S(1)} %copy-done.70), channel_id=1, replica_groups=mesh['dp'=4,'blk'=8] {'dp','blk'}, use_global_device_ids=true, to_apply=%region_37.38 | all-reduce | flops 6144 | bytes 49152 | tf_op jit(solution)/shard_map/psum | solution.py:323
  1280.6 6.8 fusion.52
  1287.4 184.0 %all-reduce.4.cloned.1.call-done = (f32[3,512,512]{1,2,0:T(8,128)}, f32[512,512]{1,0:T(8,128)}, f32[512,2048]{1,0:T(8,128)}, f32[2048,512]{1,0:T(8,128)}) async-done(((f32[3,512,512]{1,2,0:T(8,128)}, f32[512,512]{1,0:T(8,128)}, f32[512,2048]{1,0:T(8,128)}, f32[2048,512]{1,0:T(8,128)}), (f32[3,512,512]{1,2,0:T(8,128)}, f32[512,512]{1,0:T(8,128)}, f32[512,2048]{1,0:T(8,128)}, ...) | async-done | bytes 12582928 | tf_op jit(solution)/shard_map/psum | solution.py:323
  (529 shorter events, 343.6 us)
Async XLA Ops:
  7.2 36.8 %all-gather.12.cloned.1.call-start = ((), (), s32[]{:S(2)}) async-start(), calls=%async_computation.1 | async-start | bytes 1966080 | tf_op jit(solution)/shard_map/all_gather | solution.py:124
  9.3 119.7 %all-gather.20.cloned.1.call-start = ((), (), s32[]{:S(2)}) async-start(), calls=%async_computation.5 | async-start | bytes 9437184 | tf_op jit(solution)/shard_map/all_gather | solution.py:146
  18.0 193.9 %all-gather.22.cloned.1.call-start = ((), (), s32[]{:S(2)}) async-start(), calls=%async_computation.6 | async-start | bytes 9437184 | tf_op jit(solution)/shard_map/all_gather | solution.py:148
  51.1 258.0 %all-gather.14.cloned.1.call-start = ((), (), s32[]{:S(2)}) async-start(), calls=%async_computation.2 | async-start | bytes 9437184 | tf_op jit(solution)/shard_map/all_gather | solution.py:149
  54.7 288.0 %all-gather.16.cloned.1.call-start = ((), (), s32[]{:S(2)}) async-start(), calls=%async_computation.3 | async-start | bytes 2621440 | tf_op jit(solution)/shard_map/all_gather | solution.py:126
  55.3 311.5 %all-gather.18.cloned.1.call-start = ((), (), s32[]{:S(2)}) async-start(), calls=%async_computation.4 | async-start | bytes 2621440 | tf_op jit(solution)/shard_map/all_gather | solution.py:127
  55.9 395.1 %all-gather.10.cloned.1.call-start = ((), (), s32[]{:S(2)}) async-start(), calls=%async_computation | async-start | bytes 9437184 | tf_op jit(solution)/shard_map/all_gather | solution.py:147
  58.8 1412.6 %all-reduce.4.cloned.1.call-start = ((), (), s32[]{:S(2)}) async-start(), calls=%async_computation.7 | async-start | bytes 25165824 | tf_op jit(solution)/shard_map/psum | solution.py:323
  107.2 49.5 %copy-start.3 = (bf16[4,256,8,64]{1,3,2,0:T(8,128)(2,1)}, bf16[4,256,8,64]{1,3,2,0:T(8,128)(2,1)S(1)}, u32[]{:S(2)}) copy-start(bf16[4,256,8,64]{1,3,2,0:T(8,128)(2,1)S(1)} %add_convert_fusion.2) | copy-start | bytes 3145732
  559.2 16.2 %collective-permute-start.4 = (bf16[4,256,512]{1,2,0:T(8,128)(2,1)S(1)}, bf16[4,256,512]{1,2,0:T(8,128)(2,1)}, u32[]{:S(2)}, u32[]{:S(2)}) collective-permute-start(bf16[4,256,512]{1,2,0:T(8,128)(2,1)S(1)} %fusion.214), channel_id=1, source_target_pairs={{7,0},{0,1},{1,2},{2,3},{3,4},{4,5},{5,6},{6,7},{15,8},{8,9},{9,10... | collective-permute-start | bytes 3145736 | tf_op jit(solution)/shard_map/while/body/eval_jaxpr/ppermute | solution.py:16
  565.8 20.9 %collective-permute-start.5 = (bf16[4,256,512]{1,2,0:T(8,128)(2,1)}, bf16[4,256,512]{1,2,0:T(8,128)(2,1)}, u32[]{:S(2)}, u32[]{:S(2)}) collective-permute-start(bf16[4,256,512]{1,2,0:T(8,128)(2,1)} %fusion.216), channel_id=1, source_target_pairs={{7,0},{0,1},{1,2},{2,3},{3,4},{4,5},{5,6},{6,7},{15,8},{8,9},{9,10... | collective-permute-start | bytes 3145736 | tf_op jit(solution)/shard_map/while/body/eval_jaxpr/ppermute | solution.py:16
  565.8 54.6 %collective-permute-start = (bf16[4,256,512]{1,2,0:T(8,128)(2,1)S(1)}, bf16[4,256,512]{1,2,0:T(8,128)(2,1)}, u32[]{:S(2)}, u32[]{:S(2)}) collective-permute-start(bf16[4,256,512]{1,2,0:T(8,128)(2,1)S(1)} %copy.75), channel_id=1, source_target_pairs={{7,0},{0,1},{1,2},{2,3},{3,4},{4,5},{5,6},{6,7},{15,8},{8,9},{9,10... | collective-permute-start | bytes 3145736 | tf_op jit(solution)/shard_map/while/body/eval_jaxpr/ppermute | solution.py:16
  565.8 54.6 %collective-permute-start.1 = (bf16[4,256,512]{1,2,0:T(8,128)(2,1)}, bf16[4,256,512]{1,2,0:T(8,128)(2,1)}, u32[]{:S(2)}, u32[]{:S(2)}) collective-permute-start(bf16[4,256,512]{1,2,0:T(8,128)(2,1)} %copy.76), channel_id=1, source_target_pairs={{7,0},{0,1},{1,2},{2,3},{3,4},{4,5},{5,6},{6,7},{15,8},{8,9},{9,10... | collective-permute-start | bytes 3145736 | tf_op jit(solution)/shard_map/while/body/eval_jaxpr/ppermute | solution.py:16
  566.8 53.6 %collective-permute-start.2 = (bf16[4,256,512]{1,2,0:T(8,128)(2,1)}, bf16[4,256,512]{1,2,0:T(8,128)(2,1)}, u32[]{:S(2)}, u32[]{:S(2)}) collective-permute-start(bf16[4,256,512]{1,2,0:T(8,128)(2,1)} %copy.77), channel_id=1, source_target_pairs={{7,0},{0,1},{1,2},{2,3},{3,4},{4,5},{5,6},{6,7},{15,8},{8,9},{9,10... | collective-permute-start | bytes 3145736 | tf_op jit(solution)/shard_map/while/body/eval_jaxpr/ppermute | solution.py:16
  575.4 44.9 %collective-permute-start.3 = (s32[4,256]{1,0:T(4,128)S(1)}, s32[4,256]{1,0:T(4,128)S(1)}, u32[]{:S(2)}, u32[]{:S(2)}) collective-permute-start(s32[4,256]{1,0:T(4,128)S(1)} %copy.78), channel_id=1, source_target_pairs={{7,0},{0,1},{1,2},{2,3},{3,4},{4,5},{5,6},{6,7},{15,8},{8,9},{9,10... | collective-permute-start | bytes 12296 | tf_op jit(solution)/shard_map/while/body/eval_jaxpr/ppermute | solution.py:16
  578.2 42.2 %copy-start.5 = (bf16[4,256,8,64]{1,3,2,0:T(8,128)(2,1)S(1)}, bf16[4,256,8,64]{1,3,2,0:T(8,128)(2,1)}, u32[]{:S(2)}) copy-start(bf16[4,256,8,64]{1,3,2,0:T(8,128)(2,1)} %get-tuple-element.424) | copy-start | bytes 3145732 | tf_op jit(solution)/shard_map/while
  645.7 16.2 %collective-permute-start.4 = (bf16[4,256,512]{1,2,0:T(8,128)(2,1)S(1)}, bf16[4,256,512]{1,2,0:T(8,128)(2,1)}, u32[]{:S(2)}, u32[]{:S(2)}) collective-permute-start(bf16[4,256,512]{1,2,0:T(8,128)(2,1)S(1)} %fusion.214), channel_id=1, source_target_pairs={{7,0},{0,1},{1,2},{2,3},{3,4},{4,5},{5,6},{6,7},{15,8},{8,9},{9,10... | collective-permute-start | bytes 3145736 | tf_op jit(solution)/shard_map/while/body/eval_jaxpr/ppermute | solution.py:16
  652.0 21.2 %collective-permute-start.5 = (bf16[4,256,512]{1,2,0:T(8,128)(2,1)}, bf16[4,256,512]{1,2,0:T(8,128)(2,1)}, u32[]{:S(2)}, u32[]{:S(2)}) collective-permute-start(bf16[4,256,512]{1,2,0:T(8,128)(2,1)} %fusion.216), channel_id=1, source_target_pairs={{7,0},{0,1},{1,2},{2,3},{3,4},{4,5},{5,6},{6,7},{15,8},{8,9},{9,10... | collective-permute-start | bytes 3145736 | tf_op jit(solution)/shard_map/while/body/eval_jaxpr/ppermute | solution.py:16
  652.0 54.9 %collective-permute-start = (bf16[4,256,512]{1,2,0:T(8,128)(2,1)S(1)}, bf16[4,256,512]{1,2,0:T(8,128)(2,1)}, u32[]{:S(2)}, u32[]{:S(2)}) collective-permute-start(bf16[4,256,512]{1,2,0:T(8,128)(2,1)S(1)} %copy.75), channel_id=1, source_target_pairs={{7,0},{0,1},{1,2},{2,3},{3,4},{4,5},{5,6},{6,7},{15,8},{8,9},{9,10... | collective-permute-start | bytes 3145736 | tf_op jit(solution)/shard_map/while/body/eval_jaxpr/ppermute | solution.py:16
  652.0 54.9 %collective-permute-start.1 = (bf16[4,256,512]{1,2,0:T(8,128)(2,1)}, bf16[4,256,512]{1,2,0:T(8,128)(2,1)}, u32[]{:S(2)}, u32[]{:S(2)}) collective-permute-start(bf16[4,256,512]{1,2,0:T(8,128)(2,1)} %copy.76), channel_id=1, source_target_pairs={{7,0},{0,1},{1,2},{2,3},{3,4},{4,5},{5,6},{6,7},{15,8},{8,9},{9,10... | collective-permute-start | bytes 3145736 | tf_op jit(solution)/shard_map/while/body/eval_jaxpr/ppermute | solution.py:16
  652.0 54.9 %collective-permute-start.2 = (bf16[4,256,512]{1,2,0:T(8,128)(2,1)}, bf16[4,256,512]{1,2,0:T(8,128)(2,1)}, u32[]{:S(2)}, u32[]{:S(2)}) collective-permute-start(bf16[4,256,512]{1,2,0:T(8,128)(2,1)} %copy.77), channel_id=1, source_target_pairs={{7,0},{0,1},{1,2},{2,3},{3,4},{4,5},{5,6},{6,7},{15,8},{8,9},{9,10... | collective-permute-start | bytes 3145736 | tf_op jit(solution)/shard_map/while/body/eval_jaxpr/ppermute | solution.py:16
  661.9 44.9 %collective-permute-start.3 = (s32[4,256]{1,0:T(4,128)S(1)}, s32[4,256]{1,0:T(4,128)S(1)}, u32[]{:S(2)}, u32[]{:S(2)}) collective-permute-start(s32[4,256]{1,0:T(4,128)S(1)} %copy.78), channel_id=1, source_target_pairs={{7,0},{0,1},{1,2},{2,3},{3,4},{4,5},{5,6},{6,7},{15,8},{8,9},{9,10... | collective-permute-start | bytes 12296 | tf_op jit(solution)/shard_map/while/body/eval_jaxpr/ppermute | solution.py:16
  732.2 16.2 %collective-permute-start.4 = (bf16[4,256,512]{1,2,0:T(8,128)(2,1)S(1)}, bf16[4,256,512]{1,2,0:T(8,128)(2,1)}, u32[]{:S(2)}, u32[]{:S(2)}) collective-permute-start(bf16[4,256,512]{1,2,0:T(8,128)(2,1)S(1)} %fusion.214), channel_id=1, source_target_pairs={{7,0},{0,1},{1,2},{2,3},{3,4},{4,5},{5,6},{6,7},{15,8},{8,9},{9,10... | collective-permute-start | bytes 3145736 | tf_op jit(solution)/shard_map/while/body/eval_jaxpr/ppermute | solution.py:16
  738.5 21.2 %collective-permute-start.5 = (bf16[4,256,512]{1,2,0:T(8,128)(2,1)}, bf16[4,256,512]{1,2,0:T(8,128)(2,1)}, u32[]{:S(2)}, u32[]{:S(2)}) collective-permute-start(bf16[4,256,512]{1,2,0:T(8,128)(2,1)} %fusion.216), channel_id=1, source_target_pairs={{7,0},{0,1},{1,2},{2,3},{3,4},{4,5},{5,6},{6,7},{15,8},{8,9},{9,10... | collective-permute-start | bytes 3145736 | tf_op jit(solution)/shard_map/while/body/eval_jaxpr/ppermute | solution.py:16
  738.5 54.9 %collective-permute-start = (bf16[4,256,512]{1,2,0:T(8,128)(2,1)S(1)}, bf16[4,256,512]{1,2,0:T(8,128)(2,1)}, u32[]{:S(2)}, u32[]{:S(2)}) collective-permute-start(bf16[4,256,512]{1,2,0:T(8,128)(2,1)S(1)} %copy.75), channel_id=1, source_target_pairs={{7,0},{0,1},{1,2},{2,3},{3,4},{4,5},{5,6},{6,7},{15,8},{8,9},{9,10... | collective-permute-start | bytes 3145736 | tf_op jit(solution)/shard_map/while/body/eval_jaxpr/ppermute | solution.py:16
  738.5 54.9 %collective-permute-start.1 = (bf16[4,256,512]{1,2,0:T(8,128)(2,1)}, bf16[4,256,512]{1,2,0:T(8,128)(2,1)}, u32[]{:S(2)}, u32[]{:S(2)}) collective-permute-start(bf16[4,256,512]{1,2,0:T(8,128)(2,1)} %copy.76), channel_id=1, source_target_pairs={{7,0},{0,1},{1,2},{2,3},{3,4},{4,5},{5,6},{6,7},{15,8},{8,9},{9,10... | collective-permute-start | bytes 3145736 | tf_op jit(solution)/shard_map/while/body/eval_jaxpr/ppermute | solution.py:16
  738.5 54.9 %collective-permute-start.2 = (bf16[4,256,512]{1,2,0:T(8,128)(2,1)}, bf16[4,256,512]{1,2,0:T(8,128)(2,1)}, u32[]{:S(2)}, u32[]{:S(2)}) collective-permute-start(bf16[4,256,512]{1,2,0:T(8,128)(2,1)} %copy.77), channel_id=1, source_target_pairs={{7,0},{0,1},{1,2},{2,3},{3,4},{4,5},{5,6},{6,7},{15,8},{8,9},{9,10... | collective-permute-start | bytes 3145736 | tf_op jit(solution)/shard_map/while/body/eval_jaxpr/ppermute | solution.py:16
  748.4 44.9 %collective-permute-start.3 = (s32[4,256]{1,0:T(4,128)S(1)}, s32[4,256]{1,0:T(4,128)S(1)}, u32[]{:S(2)}, u32[]{:S(2)}) collective-permute-start(s32[4,256]{1,0:T(4,128)S(1)} %copy.78), channel_id=1, source_target_pairs={{7,0},{0,1},{1,2},{2,3},{3,4},{4,5},{5,6},{6,7},{15,8},{8,9},{9,10... | collective-permute-start | bytes 12296 | tf_op jit(solution)/shard_map/while/body/eval_jaxpr/ppermute | solution.py:16
  818.7 16.2 %collective-permute-start.4 = (bf16[4,256,512]{1,2,0:T(8,128)(2,1)S(1)}, bf16[4,256,512]{1,2,0:T(8,128)(2,1)}, u32[]{:S(2)}, u32[]{:S(2)}) collective-permute-start(bf16[4,256,512]{1,2,0:T(8,128)(2,1)S(1)} %fusion.214), channel_id=1, source_target_pairs={{7,0},{0,1},{1,2},{2,3},{3,4},{4,5},{5,6},{6,7},{15,8},{8,9},{9,10... | collective-permute-start | bytes 3145736 | tf_op jit(solution)/shard_map/while/body/eval_jaxpr/ppermute | solution.py:16
  824.9 21.2 %collective-permute-start.5 = (bf16[4,256,512]{1,2,0:T(8,128)(2,1)}, bf16[4,256,512]{1,2,0:T(8,128)(2,1)}, u32[]{:S(2)}, u32[]{:S(2)}) collective-permute-start(bf16[4,256,512]{1,2,0:T(8,128)(2,1)} %fusion.216), channel_id=1, source_target_pairs={{7,0},{0,1},{1,2},{2,3},{3,4},{4,5},{5,6},{6,7},{15,8},{8,9},{9,10... | collective-permute-start | bytes 3145736 | tf_op jit(solution)/shard_map/while/body/eval_jaxpr/ppermute | solution.py:16
  824.9 54.9 %collective-permute-start = (bf16[4,256,512]{1,2,0:T(8,128)(2,1)S(1)}, bf16[4,256,512]{1,2,0:T(8,128)(2,1)}, u32[]{:S(2)}, u32[]{:S(2)}) collective-permute-start(bf16[4,256,512]{1,2,0:T(8,128)(2,1)S(1)} %copy.75), channel_id=1, source_target_pairs={{7,0},{0,1},{1,2},{2,3},{3,4},{4,5},{5,6},{6,7},{15,8},{8,9},{9,10... | collective-permute-start | bytes 3145736 | tf_op jit(solution)/shard_map/while/body/eval_jaxpr/ppermute | solution.py:16
  824.9 54.9 %collective-permute-start.1 = (bf16[4,256,512]{1,2,0:T(8,128)(2,1)}, bf16[4,256,512]{1,2,0:T(8,128)(2,1)}, u32[]{:S(2)}, u32[]{:S(2)}) collective-permute-start(bf16[4,256,512]{1,2,0:T(8,128)(2,1)} %copy.76), channel_id=1, source_target_pairs={{7,0},{0,1},{1,2},{2,3},{3,4},{4,5},{5,6},{6,7},{15,8},{8,9},{9,10... | collective-permute-start | bytes 3145736 | tf_op jit(solution)/shard_map/while/body/eval_jaxpr/ppermute | solution.py:16
  824.9 54.9 %collective-permute-start.2 = (bf16[4,256,512]{1,2,0:T(8,128)(2,1)}, bf16[4,256,512]{1,2,0:T(8,128)(2,1)}, u32[]{:S(2)}, u32[]{:S(2)}) collective-permute-start(bf16[4,256,512]{1,2,0:T(8,128)(2,1)} %copy.77), channel_id=1, source_target_pairs={{7,0},{0,1},{1,2},{2,3},{3,4},{4,5},{5,6},{6,7},{15,8},{8,9},{9,10... | collective-permute-start | bytes 3145736 | tf_op jit(solution)/shard_map/while/body/eval_jaxpr/ppermute | solution.py:16
  834.9 44.9 %collective-permute-start.3 = (s32[4,256]{1,0:T(4,128)S(1)}, s32[4,256]{1,0:T(4,128)S(1)}, u32[]{:S(2)}, u32[]{:S(2)}) collective-permute-start(s32[4,256]{1,0:T(4,128)S(1)} %copy.78), channel_id=1, source_target_pairs={{7,0},{0,1},{1,2},{2,3},{3,4},{4,5},{5,6},{6,7},{15,8},{8,9},{9,10... | collective-permute-start | bytes 12296 | tf_op jit(solution)/shard_map/while/body/eval_jaxpr/ppermute | solution.py:16
  905.1 16.2 %collective-permute-start.4 = (bf16[4,256,512]{1,2,0:T(8,128)(2,1)S(1)}, bf16[4,256,512]{1,2,0:T(8,128)(2,1)}, u32[]{:S(2)}, u32[]{:S(2)}) collective-permute-start(bf16[4,256,512]{1,2,0:T(8,128)(2,1)S(1)} %fusion.214), channel_id=1, source_target_pairs={{7,0},{0,1},{1,2},{2,3},{3,4},{4,5},{5,6},{6,7},{15,8},{8,9},{9,10... | collective-permute-start | bytes 3145736 | tf_op jit(solution)/shard_map/while/body/eval_jaxpr/ppermute | solution.py:16
  911.4 21.2 %collective-permute-start.5 = (bf16[4,256,512]{1,2,0:T(8,128)(2,1)}, bf16[4,256,512]{1,2,0:T(8,128)(2,1)}, u32[]{:S(2)}, u32[]{:S(2)}) collective-permute-start(bf16[4,256,512]{1,2,0:T(8,128)(2,1)} %fusion.216), channel_id=1, source_target_pairs={{7,0},{0,1},{1,2},{2,3},{3,4},{4,5},{5,6},{6,7},{15,8},{8,9},{9,10... | collective-permute-start | bytes 3145736 | tf_op jit(solution)/shard_map/while/body/eval_jaxpr/ppermute | solution.py:16
  911.4 54.9 %collective-permute-start = (bf16[4,256,512]{1,2,0:T(8,128)(2,1)S(1)}, bf16[4,256,512]{1,2,0:T(8,128)(2,1)}, u32[]{:S(2)}, u32[]{:S(2)}) collective-permute-start(bf16[4,256,512]{1,2,0:T(8,128)(2,1)S(1)} %copy.75), channel_id=1, source_target_pairs={{7,0},{0,1},{1,2},{2,3},{3,4},{4,5},{5,6},{6,7},{15,8},{8,9},{9,10... | collective-permute-start | bytes 3145736 | tf_op jit(solution)/shard_map/while/body/eval_jaxpr/ppermute | solution.py:16
  911.4 54.9 %collective-permute-start.1 = (bf16[4,256,512]{1,2,0:T(8,128)(2,1)}, bf16[4,256,512]{1,2,0:T(8,128)(2,1)}, u32[]{:S(2)}, u32[]{:S(2)}) collective-permute-start(bf16[4,256,512]{1,2,0:T(8,128)(2,1)} %copy.76), channel_id=1, source_target_pairs={{7,0},{0,1},{1,2},{2,3},{3,4},{4,5},{5,6},{6,7},{15,8},{8,9},{9,10... | collective-permute-start | bytes 3145736 | tf_op jit(solution)/shard_map/while/body/eval_jaxpr/ppermute | solution.py:16
  911.4 54.9 %collective-permute-start.2 = (bf16[4,256,512]{1,2,0:T(8,128)(2,1)}, bf16[4,256,512]{1,2,0:T(8,128)(2,1)}, u32[]{:S(2)}, u32[]{:S(2)}) collective-permute-start(bf16[4,256,512]{1,2,0:T(8,128)(2,1)} %copy.77), channel_id=1, source_target_pairs={{7,0},{0,1},{1,2},{2,3},{3,4},{4,5},{5,6},{6,7},{15,8},{8,9},{9,10... | collective-permute-start | bytes 3145736 | tf_op jit(solution)/shard_map/while/body/eval_jaxpr/ppermute | solution.py:16
  921.3 44.9 %collective-permute-start.3 = (s32[4,256]{1,0:T(4,128)S(1)}, s32[4,256]{1,0:T(4,128)S(1)}, u32[]{:S(2)}, u32[]{:S(2)}) collective-permute-start(s32[4,256]{1,0:T(4,128)S(1)} %copy.78), channel_id=1, source_target_pairs={{7,0},{0,1},{1,2},{2,3},{3,4},{4,5},{5,6},{6,7},{15,8},{8,9},{9,10... | collective-permute-start | bytes 12296 | tf_op jit(solution)/shard_map/while/body/eval_jaxpr/ppermute | solution.py:16
  991.6 16.2 %collective-permute-start.4 = (bf16[4,256,512]{1,2,0:T(8,128)(2,1)S(1)}, bf16[4,256,512]{1,2,0:T(8,128)(2,1)}, u32[]{:S(2)}, u32[]{:S(2)}) collective-permute-start(bf16[4,256,512]{1,2,0:T(8,128)(2,1)S(1)} %fusion.214), channel_id=1, source_target_pairs={{7,0},{0,1},{1,2},{2,3},{3,4},{4,5},{5,6},{6,7},{15,8},{8,9},{9,10... | collective-permute-start | bytes 3145736 | tf_op jit(solution)/shard_map/while/body/eval_jaxpr/ppermute | solution.py:16
  997.9 21.2 %collective-permute-start.5 = (bf16[4,256,512]{1,2,0:T(8,128)(2,1)}, bf16[4,256,512]{1,2,0:T(8,128)(2,1)}, u32[]{:S(2)}, u32[]{:S(2)}) collective-permute-start(bf16[4,256,512]{1,2,0:T(8,128)(2,1)} %fusion.216), channel_id=1, source_target_pairs={{7,0},{0,1},{1,2},{2,3},{3,4},{4,5},{5,6},{6,7},{15,8},{8,9},{9,10... | collective-permute-start | bytes 3145736 | tf_op jit(solution)/shard_map/while/body/eval_jaxpr/ppermute | solution.py:16
  997.9 54.9 %collective-permute-start = (bf16[4,256,512]{1,2,0:T(8,128)(2,1)S(1)}, bf16[4,256,512]{1,2,0:T(8,128)(2,1)}, u32[]{:S(2)}, u32[]{:S(2)}) collective-permute-start(bf16[4,256,512]{1,2,0:T(8,128)(2,1)S(1)} %copy.75), channel_id=1, source_target_pairs={{7,0},{0,1},{1,2},{2,3},{3,4},{4,5},{5,6},{6,7},{15,8},{8,9},{9,10... | collective-permute-start | bytes 3145736 | tf_op jit(solution)/shard_map/while/body/eval_jaxpr/ppermute | solution.py:16
  997.9 54.9 %collective-permute-start.1 = (bf16[4,256,512]{1,2,0:T(8,128)(2,1)}, bf16[4,256,512]{1,2,0:T(8,128)(2,1)}, u32[]{:S(2)}, u32[]{:S(2)}) collective-permute-start(bf16[4,256,512]{1,2,0:T(8,128)(2,1)} %copy.76), channel_id=1, source_target_pairs={{7,0},{0,1},{1,2},{2,3},{3,4},{4,5},{5,6},{6,7},{15,8},{8,9},{9,10... | collective-permute-start | bytes 3145736 | tf_op jit(solution)/shard_map/while/body/eval_jaxpr/ppermute | solution.py:16
  997.9 54.9 %collective-permute-start.2 = (bf16[4,256,512]{1,2,0:T(8,128)(2,1)}, bf16[4,256,512]{1,2,0:T(8,128)(2,1)}, u32[]{:S(2)}, u32[]{:S(2)}) collective-permute-start(bf16[4,256,512]{1,2,0:T(8,128)(2,1)} %copy.77), channel_id=1, source_target_pairs={{7,0},{0,1},{1,2},{2,3},{3,4},{4,5},{5,6},{6,7},{15,8},{8,9},{9,10... | collective-permute-start | bytes 3145736 | tf_op jit(solution)/shard_map/while/body/eval_jaxpr/ppermute | solution.py:16
  1007.8 44.9 %collective-permute-start.3 = (s32[4,256]{1,0:T(4,128)S(1)}, s32[4,256]{1,0:T(4,128)S(1)}, u32[]{:S(2)}, u32[]{:S(2)}) collective-permute-start(s32[4,256]{1,0:T(4,128)S(1)} %copy.78), channel_id=1, source_target_pairs={{7,0},{0,1},{1,2},{2,3},{3,4},{4,5},{5,6},{6,7},{15,8},{8,9},{9,10... | collective-permute-start | bytes 12296 | tf_op jit(solution)/shard_map/while/body/eval_jaxpr/ppermute | solution.py:16
  1078.1 16.2 %collective-permute-start.4 = (bf16[4,256,512]{1,2,0:T(8,128)(2,1)S(1)}, bf16[4,256,512]{1,2,0:T(8,128)(2,1)}, u32[]{:S(2)}, u32[]{:S(2)}) collective-permute-start(bf16[4,256,512]{1,2,0:T(8,128)(2,1)S(1)} %fusion.214), channel_id=1, source_target_pairs={{7,0},{0,1},{1,2},{2,3},{3,4},{4,5},{5,6},{6,7},{15,8},{8,9},{9,10... | collective-permute-start | bytes 3145736 | tf_op jit(solution)/shard_map/while/body/eval_jaxpr/ppermute | solution.py:16
  1084.4 21.2 %collective-permute-start.5 = (bf16[4,256,512]{1,2,0:T(8,128)(2,1)}, bf16[4,256,512]{1,2,0:T(8,128)(2,1)}, u32[]{:S(2)}, u32[]{:S(2)}) collective-permute-start(bf16[4,256,512]{1,2,0:T(8,128)(2,1)} %fusion.216), channel_id=1, source_target_pairs={{7,0},{0,1},{1,2},{2,3},{3,4},{4,5},{5,6},{6,7},{15,8},{8,9},{9,10... | collective-permute-start | bytes 3145736 | tf_op jit(solution)/shard_map/while/body/eval_jaxpr/ppermute | solution.py:16
  1084.4 54.9 %collective-permute-start = (bf16[4,256,512]{1,2,0:T(8,128)(2,1)S(1)}, bf16[4,256,512]{1,2,0:T(8,128)(2,1)}, u32[]{:S(2)}, u32[]{:S(2)}) collective-permute-start(bf16[4,256,512]{1,2,0:T(8,128)(2,1)S(1)} %copy.75), channel_id=1, source_target_pairs={{7,0},{0,1},{1,2},{2,3},{3,4},{4,5},{5,6},{6,7},{15,8},{8,9},{9,10... | collective-permute-start | bytes 3145736 | tf_op jit(solution)/shard_map/while/body/eval_jaxpr/ppermute | solution.py:16
  1084.4 54.9 %collective-permute-start.1 = (bf16[4,256,512]{1,2,0:T(8,128)(2,1)}, bf16[4,256,512]{1,2,0:T(8,128)(2,1)}, u32[]{:S(2)}, u32[]{:S(2)}) collective-permute-start(bf16[4,256,512]{1,2,0:T(8,128)(2,1)} %copy.76), channel_id=1, source_target_pairs={{7,0},{0,1},{1,2},{2,3},{3,4},{4,5},{5,6},{6,7},{15,8},{8,9},{9,10... | collective-permute-start | bytes 3145736 | tf_op jit(solution)/shard_map/while/body/eval_jaxpr/ppermute | solution.py:16
  1084.4 54.9 %collective-permute-start.2 = (bf16[4,256,512]{1,2,0:T(8,128)(2,1)}, bf16[4,256,512]{1,2,0:T(8,128)(2,1)}, u32[]{:S(2)}, u32[]{:S(2)}) collective-permute-start(bf16[4,256,512]{1,2,0:T(8,128)(2,1)} %copy.77), channel_id=1, source_target_pairs={{7,0},{0,1},{1,2},{2,3},{3,4},{4,5},{5,6},{6,7},{15,8},{8,9},{9,10... | collective-permute-start | bytes 3145736 | tf_op jit(solution)/shard_map/while/body/eval_jaxpr/ppermute | solution.py:16
  1094.3 44.9 %collective-permute-start.3 = (s32[4,256]{1,0:T(4,128)S(1)}, s32[4,256]{1,0:T(4,128)S(1)}, u32[]{:S(2)}, u32[]{:S(2)}) collective-permute-start(s32[4,256]{1,0:T(4,128)S(1)} %copy.78), channel_id=1, source_target_pairs={{7,0},{0,1},{1,2},{2,3},{3,4},{4,5},{5,6},{6,7},{15,8},{8,9},{9,10... | collective-permute-start | bytes 12296 | tf_op jit(solution)/shard_map/while/body/eval_jaxpr/ppermute | solution.py:16
  1164.6 16.2 %collective-permute-start.4 = (bf16[4,256,512]{1,2,0:T(8,128)(2,1)S(1)}, bf16[4,256,512]{1,2,0:T(8,128)(2,1)}, u32[]{:S(2)}, u32[]{:S(2)}) collective-permute-start(bf16[4,256,512]{1,2,0:T(8,128)(2,1)S(1)} %fusion.214), channel_id=1, source_target_pairs={{7,0},{0,1},{1,2},{2,3},{3,4},{4,5},{5,6},{6,7},{15,8},{8,9},{9,10... | collective-permute-start | bytes 3145736 | tf_op jit(solution)/shard_map/while/body/eval_jaxpr/ppermute | solution.py:16
  1170.8 21.2 %collective-permute-start.5 = (bf16[4,256,512]{1,2,0:T(8,128)(2,1)}, bf16[4,256,512]{1,2,0:T(8,128)(2,1)}, u32[]{:S(2)}, u32[]{:S(2)}) collective-permute-start(bf16[4,256,512]{1,2,0:T(8,128)(2,1)} %fusion.216), channel_id=1, source_target_pairs={{7,0},{0,1},{1,2},{2,3},{3,4},{4,5},{5,6},{6,7},{15,8},{8,9},{9,10... | collective-permute-start | bytes 3145736 | tf_op jit(solution)/shard_map/while/body/eval_jaxpr/ppermute | solution.py:16
  1170.8 54.9 %collective-permute-start = (bf16[4,256,512]{1,2,0:T(8,128)(2,1)S(1)}, bf16[4,256,512]{1,2,0:T(8,128)(2,1)}, u32[]{:S(2)}, u32[]{:S(2)}) collective-permute-start(bf16[4,256,512]{1,2,0:T(8,128)(2,1)S(1)} %copy.75), channel_id=1, source_target_pairs={{7,0},{0,1},{1,2},{2,3},{3,4},{4,5},{5,6},{6,7},{15,8},{8,9},{9,10... | collective-permute-start | bytes 3145736 | tf_op jit(solution)/shard_map/while/body/eval_jaxpr/ppermute | solution.py:16
  1170.8 54.9 %collective-permute-start.1 = (bf16[4,256,512]{1,2,0:T(8,128)(2,1)}, bf16[4,256,512]{1,2,0:T(8,128)(2,1)}, u32[]{:S(2)}, u32[]{:S(2)}) collective-permute-start(bf16[4,256,512]{1,2,0:T(8,128)(2,1)} %copy.76), channel_id=1, source_target_pairs={{7,0},{0,1},{1,2},{2,3},{3,4},{4,5},{5,6},{6,7},{15,8},{8,9},{9,10... | collective-permute-start | bytes 3145736 | tf_op jit(solution)/shard_map/while/body/eval_jaxpr/ppermute | solution.py:16
  1170.9 54.9 %collective-permute-start.2 = (bf16[4,256,512]{1,2,0:T(8,128)(2,1)}, bf16[4,256,512]{1,2,0:T(8,128)(2,1)}, u32[]{:S(2)}, u32[]{:S(2)}) collective-permute-start(bf16[4,256,512]{1,2,0:T(8,128)(2,1)} %copy.77), channel_id=1, source_target_pairs={{7,0},{0,1},{1,2},{2,3},{3,4},{4,5},{5,6},{6,7},{15,8},{8,9},{9,10... | collective-permute-start | bytes 3145736 | tf_op jit(solution)/shard_map/while/body/eval_jaxpr/ppermute | solution.py:16
  1180.8 44.9 %collective-permute-start.3 = (s32[4,256]{1,0:T(4,128)S(1)}, s32[4,256]{1,0:T(4,128)S(1)}, u32[]{:S(2)}, u32[]{:S(2)}) collective-permute-start(s32[4,256]{1,0:T(4,128)S(1)} %copy.78), channel_id=1, source_target_pairs={{7,0},{0,1},{1,2},{2,3},{3,4},{4,5},{5,6},{6,7},{15,8},{8,9},{9,10... | collective-permute-start | bytes 12296 | tf_op jit(solution)/shard_map/while/body/eval_jaxpr/ppermute | solution.py:16
  1239.5 41.0 %copy-start.9 = (bf16[3,512,512]{1,2,0:T(8,128)(2,1)S(1)}, bf16[3,512,512]{1,2,0:T(8,128)(2,1)}, u32[]{:S(2)}) copy-start(bf16[3,512,512]{1,2,0:T(8,128)(2,1)} %copy-done.8) | copy-start | bytes 4718596
  1239.5 41.0 %copy-start.33 = (f32[4,256]{1,0:T(4,128)S(1)}, f32[4,256]{1,0:T(4,128)}, u32[]{:S(2)}) copy-start(f32[4,256]{1,0:T(4,128)} %copy-done.32) | copy-start | bytes 12292
  1239.5 41.0 %copy-start.36 = (f32[4,256]{1,0:T(4,128)S(1)}, f32[4,256]{1,0:T(4,128)}, u32[]{:S(2)}) copy-start(f32[4,256]{1,0:T(4,128)} %copy-done.35) | copy-start | bytes 12292
  1239.5 41.0 %copy-start.45 = (f32[3,512]{1,0:T(4,128)S(1)}, f32[3,512]{1,0:T(4,128)}, u32[]{:S(2)}) copy-start(f32[3,512]{1,0:T(4,128)} %copy-done.44) | copy-start | bytes 18436
  1280.5 190.8 %copy-start.53 = (f32[512]{0:T(512)S(1)}, f32[512]{0:T(512)}, u32[]{:S(2)}) copy-start(f32[512]{0:T(512)} %get-tuple-element.235) | copy-start | bytes 6148
  1280.5 190.8 %copy-start.69 = (f32[512]{0:T(512)S(1)}, f32[512]{0:T(512)}, u32[]{:S(2)}) copy-start(f32[512]{0:T(512)} %get-tuple-element.234) | copy-start | bytes 6148
  (119 other events, 1310.0 us)
Sparse Core Ops, SparseCore 0:
  10.4 33.5 all-gather.11
  46.1 82.7 all-gather.19
  131.1 80.6 all-gather.21
  213.9 80.6 all-gather.13
  296.3 33.4 all-gather.15
  331.5 35.2 all-gather.17
  368.4 82.4 all-gather.9
  1239.7 231.6 all-reduce.3
where the time goes:
time: 1510 us; the launch traced here: 1500 us
  waiting for transfers between devices  738 us (49%)
  matrix products  414 us (27%)
  other arithmetic  172 us (11%)
  local copies, waits for them, and re-layouts  88.7 us (6%)
  blocking collectives  71 us (5%)
  between operations  15.3 us (1%)
    ppermute x48, waiting for transfers between devices, shifted(): return lax.ppermute(block, axis, route)  358 us
    psum x1, waiting for transfers between devices, shards(): lax.psum((partials[0], partials[1], partials[2], partials[3], partials[4]...  184 us
    dot_general x2, matrix products, online_step(): jnp.einsum('bqhd,bkhd->bhqk', queries, key_rows, preferred_element_type=j...  81.8 us
    all_gather x1, waiting for transfers between devices, shards(): piece_values = lax.all_gather(value_rows, 'blk', axis=1, tiled=True)  71.9 us
    dot_general x2, matrix products, online_step(): jnp.einsum('bhqk,bkhd->bqhd', numerators.astype(jnp.bfloat16), value_rows...  59.4 us
    dot_general x8, matrix products, key_terms(): jnp.einsum('bqhd,bkhd->bhqk', teacher_heads, heads_of(piece_tkeys), prefe...  55.2 us
    all_gather x1, waiting for transfers between devices, shards(): piece_tkeys = lax.all_gather(teacher_keys, 'blk', axis=1, tiled=True)  55.1 us
    while x112, local copies, waits for them, and re-layouts  46.1 us
  transfers between devices with their start and end apart: 56, of which 30 were waited for; matrix products, arithmetic and copies ran while one was open for 23% of the time, Pallas kernels for 0%

commit v1 on v0

v1 whole, which is shorter than its diff:
```python
import functools

import jax
import jax.numpy as jnp
from jax import lax
from jax.experimental import pallas as pl
from jax.experimental.pallas import tpu as pltpu
from jax.sharding import PartitionSpec as P

HEADS = 8
BF = jnp.bfloat16
F32 = jnp.float32
LOG2E = 1.4426950408889634
clip_level = 2.5
masked_score = -1e30
VMEM_BYTES = 56 << 20
MESH = pl.DeviceIdType.MESH
NT = (((1,), (1,)), ((), ()))
TN = (((0,), (0,)), ((), ()))


def squash(tensor):
    return clip_level * jnp.tanh(tensor * (1.0 / clip_level))


def gelu_parts(tensor):
    phi = 0.5 * (1.0 + lax.erf(tensor * 0.7071067811865476))
    return tensor * phi, phi


def binarize(matrix):
    column_scale = jnp.sqrt(jnp.mean(matrix * matrix, axis=-2, keepdims=True) + 1e-06)
    return column_scale * jnp.tanh(2.0 * matrix / column_scale)


def layer_norm(tensor, gain_row, shift_row):
    centre = tensor - jnp.mean(tensor, axis=-1, keepdims=True)
    inverse_std = lax.rsqrt(jnp.mean(centre * centre, axis=-1, keepdims=True) + 1e-05)
    normed = centre * inverse_std
    return (normed * gain_row + shift_row, normed, inverse_std)


def norm_back(upstream, gain_row, normed, inverse_std):
    scaled = upstream * gain_row
    return inverse_std * (
        scaled
        - jnp.mean(scaled, axis=-1, keepdims=True)
        - normed * jnp.mean(scaled * normed, axis=-1, keepdims=True)
    )


def dot(a, b, dims=(((1,), (0,)), ((), ()))):
    return lax.dot_general(a, b, dims, preferred_element_type=F32)


def latent_grad(latent, binary_grad):
    matrix = latent.astype(F32)
    unused, pullback = jax.vjp(binarize, matrix)
    return pullback(binary_grad)[0]


def place(groups):
    here = lax.axis_index("blk")
    return here // groups, lax.rem(here, groups)


def greet(peers):
    barrier = pltpu.get_barrier_semaphore()
    for peer in peers:
        pl.semaphore_signal(barrier, inc=1, device_id={"blk": peer}, device_id_type=MESH)
    pl.semaphore_wait(barrier, len(peers))


def stream_peers(streams, groups):
    s, r = place(groups)
    return [lax.rem(s + d, streams) * groups + r for d in range(1, streams)]


def core_peers(groups):
    s, r = place(groups)
    return [s * groups + lax.rem(r + j, groups) for j in range(1, groups)]


def swap_copies(streams, groups, source, target, base, send, recv):
    s, r = place(groups)
    return [
        pltpu.make_async_remote_copy(
            src_ref=source.at[lax.rem(s + d, streams)],
            dst_ref=target.at[base + s],
            send_sem=send.at[d],
            recv_sem=recv.at[d],
            device_id={"blk": lax.rem(s + d, streams) * groups + r},
            device_id_type=MESH,
        )
        for d in range(1, streams)
    ]


def share_copy(streams, groups, source, slot, target, d, j, send, recv):
    s, r = place(groups)
    return pltpu.make_async_remote_copy(
        src_ref=source,
        dst_ref=target.at[slot],
        send_sem=send.at[j * streams + d],
        recv_sem=recv.at[j * streams + d],
        device_id={"blk": s * groups + lax.rem(r + j, groups)},
        device_id_type=MESH,
    )


class Gather:
    def __init__(self, streams, groups):
        self.streams, self.groups = streams, groups

    def scratch(self):
        b, g = self.streams, self.groups
        return [
            pltpu.SemaphoreType.DMA((b,)),
            pltpu.SemaphoreType.DMA((b,)),
            pltpu.SemaphoreType.DMA((b * g,)),
            pltpu.SemaphoreType.DMA((b * g,)),
        ]

    def peers(self):
        return stream_peers(self.streams, self.groups) + core_peers(self.groups)

    def first(self, source, target, send, recv, share_send, share_recv):
        b, g = self.streams, self.groups
        s, r = place(g)
        for copy in swap_copies(b, g, source, target, r * b, send, recv):
            copy.start()
        pltpu.make_async_copy(source.at[s], target.at[r * b + s], send.at[0]).start()
        for j in range(1, g):
            share_copy(
                b, g, source.at[s], r * b + s, target, 0, j, share_send, share_recv
            ).start()

    def last(self, source, target, send, recv, share_send, share_recv):
        b, g = self.streams, self.groups
        s, r = place(g)
        swaps = swap_copies(b, g, source, target, r * b, send, recv)
        shares = []
        for d in (1, 3, 2) if b == 4 else range(1, b):
            swaps[d - 1].wait_recv()
            slot = r * b + lax.rem(s + b - d, b)
            for j in range(1, g):
                copy = share_copy(b, g, target.at[slot], slot, target, d, j, share_send, share_recv)
                copy.start()
                shares.append(copy)
        pltpu.make_async_copy(source.at[s], target.at[r * b + s], send.at[0]).wait()
        for j in range(1, g):
            shares.append(
                share_copy(b, g, source.at[s], r * b + s, target, 0, j, share_send, share_recv)
            )
        for copy in shares:
            copy.wait()
        for copy in swaps:
            copy.wait_send()


class Swap:
    def __init__(self, streams, groups):
        self.streams, self.groups = streams, groups

    def scratch(self):
        return [
            pltpu.SemaphoreType.DMA((self.streams,)),
            pltpu.SemaphoreType.DMA((self.streams,)),
        ]

    def peers(self):
        return stream_peers(self.streams, self.groups)

    def first(self, source, target, send, recv):
        s, r = place(self.groups)
        for copy in swap_copies(self.streams, self.groups, source, target, 0, send, recv):
            copy.start()
        pltpu.make_async_copy(source.at[s], target.at[s], send.at[0]).start()

    def last(self, source, target, send, recv):
        s, r = place(self.groups)
        for copy in swap_copies(self.streams, self.groups, source, target, 0, send, recv):
            copy.wait()
        pltpu.make_async_copy(source.at[s], target.at[s], send.at[0]).wait()


class Rows:
    def __init__(self, groups):
        self.groups = groups

    def scratch(self):
        return [
            pltpu.SemaphoreType.DMA((self.groups,)),
            pltpu.SemaphoreType.DMA((self.groups,)),
        ]

    def peers(self):
        return core_peers(self.groups)

    def copies(self, source, target, send, recv):
        s, r = place(self.groups)
        g = self.groups
        return [
            pltpu.make_async_remote_copy(
                src_ref=source.at[lax.rem(r + j, g)],
                dst_ref=target.at[r],
                send_sem=send.at[j],
                recv_sem=recv.at[j],
                device_id={"blk": s * g + lax.rem(r + j, g)},
                device_id_type=MESH,
            )
            for j in range(1, g)
        ]

    def first(self, source, target, send, recv):
        s, r = place(self.groups)
        for copy in self.copies(source, target, send, recv):
            copy.start()
        pltpu.make_async_copy(source.at[r], target.at[r], send.at[0]).start()

    def last(self, source, target, send, recv):
        s, r = place(self.groups)
        for copy in self.copies(source, target, send, recv):
            copy.wait()
        pltpu.make_async_copy(source.at[r], target.at[r], send.at[0]).wait()


def move(job, arrays, out_shapes, collective_id, name):
    count = len(arrays)
    n_sems = len(job.scratch())

    def kernel(*refs):
        sources, targets = refs[:count], refs[count : 2 * count]
        sems = refs[2 * count :]
        greet(job.peers())
        for i in range(count):
            job.first(sources[i], targets[i], *sems[i * n_sems : (i + 1) * n_sems])
        for i in range(count):
            job.last(sources[i], targets[i], *sems[i * n_sems : (i + 1) * n_sems])

    return pl.pallas_call(
        kernel,
        out_shape=out_shapes,
        in_specs=[pl.BlockSpec(memory_space=pl.ANY)] * count,
        out_specs=[pl.BlockSpec(memory_space=pl.ANY)] * count,
        scratch_shapes=job.scratch() * count,
        compiler_params=pltpu.CompilerParams(collective_id=collective_id, has_side_effects=True),
        name=name,
    )(*arrays)


def lanes_of(shape):
    return lax.broadcasted_iota(jnp.int32, shape, 1)


def forward_kernel(job, keep, tile, edge, q_ref, k_ref, v_ref, col_ref, row_ref, src_ref, *rest):
    if keep:
        e_ref, ctx_ref, inv_ref, dst_ref, k_aug, v_aug, *sems = rest
    else:
        ctx_ref, dst_ref, k_aug, v_aug, *sems = rest
    pair, step = pl.program_id(0), pl.program_id(1)
    steps = pl.num_programs(1)
    seq = k_ref.shape[0]

    @pl.when((pair == 0) & (step == 0))
    def _():
        greet(job.peers())
        job.first(src_ref, dst_ref, *sems)

    @pl.when(step == 0)
    def _():
        low = lanes_of((seq, 128)) < 64
        lane = lanes_of((seq, 128))
        keys = k_ref[...].astype(F32)
        turned = pltpu.roll(keys, 64, 1)
        k_aug[0] = jnp.where(low, keys, turned).astype(BF)
        k_aug[1] = jnp.where(low, turned, keys).astype(BF)
        values = v_ref[...].astype(F32)
        v_aug[0] = jnp.where(low, values, jnp.where(lane < 66, 1.0, 0.0)).astype(BF)
        v_aug[1] = jnp.where(low, jnp.where(lane < 2, 1.0, 0.0), values).astype(BF)

    def body(whole):
        low = lanes_of((tile, 128)) < 64
        scaled = q_ref[...].astype(F32) * LOG2E
        upper = scaled.astype(BF).astype(F32)
        rest_part = scaled - upper
        results = []
        for h in range(2):
            if h == 0:
                q_aug = jnp.where(low, upper, pltpu.roll(rest_part, 64, 1)).astype(BF)
            else:
                q_aug = jnp.where(low, pltpu.roll(upper, 64, 1), rest_part).astype(BF)
            scores = dot(q_aug, k_aug[h], NT)
            if whole:
                scores = jnp.where(col_ref[...] == row_ref[...], scores, masked_score)
            else:
                left = jnp.where(
                    col_ref[...] == row_ref[:, :edge], scores[:, :edge], masked_score
                )
                right = jnp.where(
                    col_ref[...] == row_ref[:, seq - edge :], scores[:, seq - edge :], masked_score
                )
                scores = jnp.concatenate([left, scores[:, edge : seq - edge], right], axis=1)
            peak = jnp.max(scores, axis=1, keepdims=True)
            numerators = jnp.exp2(scores - peak).astype(BF)
            if keep:
                e_ref[h] = numerators
            total = dot(numerators, v_aug[h])
            where_sum = 64 if h == 0 else 0
            inverse = 1.0 / total[:, where_sum : where_sum + 1]
            results.append((total * inverse, inverse))
        ctx_ref[...] = jnp.where(low, results[0][0], results[1][0]).astype(BF)
        if keep:
            inv_ref[...] = jnp.where(low, results[0][1], results[1][1])

    at_edge = (step == 0) | (step == steps - 1)

    @pl.when(at_edge)
    def _():
        body(True)

    @pl.when(jnp.logical_not(at_edge))
    def _():
        body(False)

    @pl.when((pair == pl.num_programs(0) - 1) & (step == steps - 1))
    def _():
        job.last(src_ref, dst_ref, *sems)


def attention(qkv, docs, job, moved, moved_shape, keep, collective_id, name):
    seq, width3 = qkv.shape
    width = width3 // 3
    pairs = width // 128
    tile = 256
    edge = 256
    col = docs.reshape(seq, 1)
    row = docs.reshape(1, seq)
    blocks = [
        pl.BlockSpec((tile, 128), lambda p, i: (i, p)),
        pl.BlockSpec((seq, 128), lambda p, i: (0, pairs + p)),
        pl.BlockSpec((seq, 128), lambda p, i: (0, 2 * pairs + p)),
        pl.BlockSpec((tile, 1), lambda p, i: (i, 0)),
        pl.BlockSpec((1, seq), lambda p, i: (0, 0)),
        pl.BlockSpec(memory_space=pl.ANY),
    ]
    outs = [pl.BlockSpec((tile, 128), lambda p, i: (i, p))]
    shapes = [jax.ShapeDtypeStruct((seq, width), BF)]
    if keep:
        outs = [pl.BlockSpec((2, tile, seq), lambda p, i: (p, i, 0))] + outs
        shapes = [jax.ShapeDtypeStruct((2 * pairs, seq, seq), BF)] + shapes
        outs = outs + [pl.BlockSpec((tile, 128), lambda p, i: (i, p))]
        shapes = shapes + [jax.ShapeDtypeStruct((seq, width), F32)]
    outs.append(pl.BlockSpec(memory_space=pl.ANY))
    shapes.append(jax.ShapeDtypeStruct(moved_shape, moved.dtype))
    return pl.pallas_call(
        functools.partial(forward_kernel, job, keep, tile, edge),
        grid=(pairs, seq // tile),
        in_specs=blocks,
        out_specs=outs,
        out_shape=shapes,
        scratch_shapes=[pltpu.VMEM((2, seq, 128), BF), pltpu.VMEM((2, seq, 128), BF)]
        + job.scratch(),
        compiler_params=pltpu.CompilerParams(
            collective_id=collective_id, has_side_effects=True, vmem_limit_bytes=VMEM_BYTES
        ),
        name=name,
    )(qkv, qkv, qkv, col, row, moved)


def split(matrix):
    upper = matrix.astype(BF)
    return upper, (matrix - upper.astype(F32)).astype(BF)


def backward_kernel(
    job,
    tile,
    e_ref,
    q_ref,
    k_ref,
    v_ref,
    tq_ref,
    tk_ref,
    dc_ref,
    ctx_ref,
    inv_ref,
    col_ref,
    row_ref,
    bigc_ref,
    src_ref,
    dq_ref,
    dk_ref,
    dv_ref,
    dst_ref,
    v_aug,
    dk_acc,
    dv_acc,
    grams,
    *sems,
):
    pair, step = pl.program_id(0), pl.program_id(1)
    steps = pl.num_programs(1)
    seq = k_ref.shape[0]
    share = 1.0 / seq

    @pl.when((pair == 0) & (step == 0))
    def _():
        greet(job.peers())
        job.first(src_ref, dst_ref, *sems)

    @pl.when(step == 0)
    def _():
        lane = lanes_of((seq, 128))
        low = lane < 64
        values = v_ref[...].astype(F32)
        v_aug[0] = jnp.where(low, values, jnp.where(lane < 66, 1.0, 0.0)).astype(BF)
        v_aug[1] = jnp.where(low, jnp.where(lane < 2, 1.0, 0.0), values).astype(BF)
        dk_acc[...] = jnp.zeros_like(dk_acc)
        dv_acc[...] = jnp.zeros_like(dv_acc)
        in_big = bigc_ref[...] > 0.0
        kb = jnp.where(in_big, k_ref[...].astype(F32), 0.0).astype(BF)
        tkb = jnp.where(in_big, tk_ref[...].astype(F32), 0.0).astype(BF)
        qb = jnp.where(in_big, q_ref[...].astype(F32), 0.0).astype(BF)
        tqb = jnp.where(in_big, tq_ref[...].astype(F32), 0.0).astype(BF)
        same_head = (lax.broadcasted_iota(jnp.int32, (128, 128), 0) < 64) == (
            lanes_of((128, 128)) < 64
        )
        for i, (a, b) in enumerate(((kb, kb), (tkb, kb), (qb, qb), (tqb, qb))):
            gram = jnp.where(same_head, dot(a, b, TN) * share, 0.0)
            grams[2 * i], grams[2 * i + 1] = split(gram)

    start = pl.multiple_of(step * tile, tile)
    rows = pl.ds(start, tile)
    lane = lanes_of((tile, 128))
    low = lane < 64

    def body(whole, columns):
        in_big = bigc_ref[rows, :] > 0.0
        q8 = q_ref[rows, :]
        tq8 = tq_ref[rows, :]
        dc = dc_ref[...].astype(F32)
        inv = inv_ref[...]
        scaled = dc * inv
        product = scaled * ctx_ref[...].astype(F32)
        scaled_low = scaled.astype(BF)
        q_turned = q8.astype(F32).T.astype(BF)
        dc_turned = scaled_low.astype(F32).T.astype(BF)
        d_queries = []
        for h in range(2):
            mine = low if h == 0 else jnp.logical_not(low)
            delta = -jnp.sum(jnp.where(mine, product, 0.0), axis=1, keepdims=True)
            upper = delta.astype(BF).astype(F32)
            first = 64 if h == 0 else 0
            extra = jnp.where(
                lane == first, upper, jnp.where(lane == first + 1, delta - upper, 0.0)
            )
            dc_aug = jnp.where(mine, scaled, extra).astype(BF)
            numerators = e_ref[h]
            d_probs = dot(dc_aug, v_aug[h], NT)
            d_scores = numerators.astype(F32) * d_probs
            if whole:
                q_mine = jnp.where(mine, q8, 0.0).astype(BF)
                tq_mine = jnp.where(mine, tq8, 0.0).astype(BF)
                gap = dot(q_mine, k_ref[columns, :], NT) - dot(tq_mine, tk_ref[columns, :], NT)
                small = (col_ref[...] == row_ref[:, columns]) & jnp.logical_not(in_big)
                gap = jnp.where(small, gap * share, 0.0)
                if columns.start == 0:
                    d_scores = jnp.concatenate(
                        [d_scores[:, :tile] + gap, d_scores[:, tile:]], axis=1
                    )
                else:
                    d_scores = jnp.concatenate(
                        [d_scores[:, : seq - tile], d_scores[:, seq - tile :] + gap], axis=1
                    )
            d_scores = d_scores.astype(BF)
            d_queries.append(dot(d_scores, k_ref[...]))
            half = slice(64 * h, 64 * h + 64)
            dk_acc[half, :] += dot(q_turned[half, :], d_scores)
            dv_acc[half, :] += dot(dc_turned[half, :], numerators)
        d_query = jnp.where(low, d_queries[0], d_queries[1])
        qb = jnp.where(in_big, q8.astype(F32), 0.0).astype(BF)
        tqb = jnp.where(in_big, tq8.astype(F32), 0.0).astype(BF)
        d_query += dot(qb, grams[0]) + dot(qb, grams[1]) - dot(tqb, grams[2]) - dot(tqb, grams[3])
        dq_ref[...] = (d_query * 0.125).astype(BF)

    @pl.when(step == 0)
    def _():
        body(True, slice(0, tile))

    @pl.when(step == steps - 1)
    def _():
        body(True, slice(seq - tile, seq))

    @pl.when((step > 0) & (step < steps - 1))
    def _():
        body(False, None)

    @pl.when(step == steps - 1)
    def _():
        in_big = bigc_ref[...] > 0.0
        kb = jnp.where(in_big, k_ref[...].astype(F32), 0.0).astype(BF)
        tkb = jnp.where(in_big, tk_ref[...].astype(F32), 0.0).astype(BF)
        d_key = dk_acc[...].T
        d_key += dot(kb, grams[4]) + dot(kb, grams[5]) - dot(tkb, grams[6]) - dot(tkb, grams[7])
        dk_ref[...] = d_key.astype(BF)
        dv_ref[...] = dv_acc[...].T.astype(BF)

    @pl.when((pair == pl.num_programs(0) - 1) & (step == steps - 1))
    def _():
        job.last(src_ref, dst_ref, *sems)


def attention_back(numerators, qkv, teacher_qkv, d_context, context, inverse, docs, in_big, job, moved, collective_id):
    seq, width3 = qkv.shape
    width = width3 // 3
    pairs = width // 128
    tile = 256
    part = pl.BlockSpec((tile, 128), lambda p, i: (i, p))

    def whole(which):
        return pl.BlockSpec((seq, 128), lambda p, i: (0, which * pairs + p))

    any_space = pl.BlockSpec(memory_space=pl.ANY)
    return pl.pallas_call(
        functools.partial(backward_kernel, job, tile),
        grid=(pairs, seq // tile),
        in_specs=[
            pl.BlockSpec((2, tile, seq), lambda p, i: (p, i, 0)),
            whole(0),
            whole(1),
            whole(2),
            whole(0),
            whole(1),
            part,
            part,
            part,
            pl.BlockSpec((tile, 1), lambda p, i: (i, 0)),
            pl.BlockSpec((1, seq), lambda p, i: (0, 0)),
            pl.BlockSpec((seq, 1), lambda p, i: (0, 0)),
            any_space,
        ],
        out_specs=[part, whole(0), whole(0), any_space],
        out_shape=[
            jax.ShapeDtypeStruct((seq, width), BF),
            jax.ShapeDtypeStruct((seq, width), BF),
            jax.ShapeDtypeStruct((seq, width), BF),
            jax.ShapeDtypeStruct(moved.shape, moved.dtype),
        ],
        scratch_shapes=[
            pltpu.VMEM((2, seq, 128), BF),
            pltpu.VMEM((128, seq), F32),
            pltpu.VMEM((128, seq), F32),
            pltpu.VMEM((8, 128, 128), BF),
        ]
        + job.scratch(),
        compiler_params=pltpu.CompilerParams(
            collective_id=collective_id, has_side_effects=True, vmem_limit_bytes=VMEM_BYTES
        ),
        name="attention_back",
    )(
        numerators,
        qkv,
        qkv,
        qkv,
        teacher_qkv,
        teacher_qkv,
        d_context,
        context,
        inverse,
        docs.reshape(seq, 1),
        docs.reshape(1, seq),
        in_big.astype(F32).reshape(seq, 1),
        moved,
    )


def middle_kernel(
    x_ref,
    tx_ref,
    cot_ref,
    ctx_ref,
    tctx_ref,
    bo_ref,
    bup_ref,
    bdown_ref,
    to_ref,
    tup_ref,
    tdown_ref,
    sg_ref,
    sb_ref,
    sub_ref,
    tg_ref,
    tb_ref,
    tub_ref,
    out_ref,
    d1_ref,
    dctx_ref,
    gout_ref,
    gup_ref,
    gdown_ref,
    ggain_ref,
    gbias_ref,
    gub_ref,
):
    step = pl.program_id(0)
    groups = ctx_ref.shape[0]
    width = ctx_ref.shape[2]

    @pl.when(step == 0)
    def _():
        for ref in (gout_ref, gup_ref, gdown_ref, ggain_ref, gbias_ref, gub_ref):
            ref[...] = jnp.zeros_like(ref)

    def row(ref, i):
        return ref[i : i + 1, :]

    tctx = jnp.concatenate([tctx_ref[j] for j in range(groups)], axis=1)
    t_att = dot(tctx, to_ref[...]) + row(tb_ref, 2)
    t_hidden = layer_norm(tx_ref[...].astype(F32) + t_att, row(tg_ref, 0), row(tb_ref, 3))[0]
    t_inner = gelu_parts(dot(t_hidden.astype(BF), tup_ref[...]) + tub_ref[...])[0]
    t_out = layer_norm(
        t_hidden + dot(t_inner.astype(BF), tdown_ref[...]) + row(tb_ref, 4),
        row(tg_ref, 1),
        row(tb_ref, 5),
    )[0]

    context = jnp.concatenate([ctx_ref[j] for j in range(groups)], axis=1).astype(F32)
    bent = jnp.tanh(context * (1.0 / clip_level))
    ctx_active = (clip_level * bent).astype(BF)
    ctx_slope = 1.0 - bent * bent
    attended = dot(ctx_active, bo_ref[...]) + row(sb_ref, 2)
    hidden, normed_one, inverse_one = layer_norm(
        x_ref[...].astype(F32) + attended, row(sg_ref, 0), row(sb_ref, 3)
    )
    bent = jnp.tanh(hidden * (1.0 / clip_level))
    hidden_active = (clip_level * bent).astype(BF)
    hidden_slope = 1.0 - bent * bent
    inner_pre = dot(hidden_active, bup_ref[...]) + sub_ref[...]
    inner_act, phi = gelu_parts(inner_pre)
    bent = jnp.tanh(inner_act * (1.0 / clip_level))
    inner_active = (clip_level * bent).astype(BF)
    slope = (1.0 - bent * bent) * (
        phi + inner_pre * jnp.exp(-0.5 * inner_pre * inner_pre) * 0.3989422804014327
    )
    branch = dot(inner_active, bdown_ref[...]) + row(sb_ref, 4)
    output, normed_two, inverse_two = layer_norm(hidden + branch, row(sg_ref, 1), row(sb_ref, 5))
    out_ref[...] = output.astype(BF)
    upstream = cot_ref[...].astype(F32) + 0.5 * (output - t_out)
    d_two = norm_back(upstream, row(sg_ref, 1), normed_two, inverse_two)
    d_branch = d_two.astype(BF)
    gdown_ref[...] += dot(inner_active, d_branch, TN)
    d_inner = (dot(d_branch, bdown_ref[...], NT) * slope).astype(BF)
    gup_ref[...] += dot(hidden_active, d_inner, TN)
    d_hidden = d_two + dot(d_inner, bup_ref[...], NT) * hidden_slope
    d_one = norm_back(d_hidden, row(sg_ref, 0), normed_one, inverse_one)
    d1_ref[...] = d_one
    d_attended = d_one.astype(BF)
    gout_ref[...] += dot(ctx_active, d_attended, TN)
    d_context = (dot(d_attended, bo_ref[...], NT) * ctx_slope).astype(BF)
    for j in range(groups):
        dctx_ref[j] = d_context[:, j * width : (j + 1) * width]

    def total(value):
        return jnp.sum(value, axis=0, keepdims=True)

    ggain_ref[0:1, :] += total(d_hidden * normed_one)
    ggain_ref[1:2, :] += total(upstream * normed_two)
    gbias_ref[2:3, :] += total(d_attended.astype(F32))
    gbias_ref[3:4, :] += total(d_hidden)
    gbias_ref[4:5, :] += total(d_branch.astype(F32))
    gbias_ref[5:6, :] += total(upstream)
    gub_ref[...] += total(d_inner.astype(F32))


def middle(x, tx, cot, ctx, tctx, weights, teacher_weights, vectors):
    rows, depth = x.shape
    ff = weights[1].shape[1]
    tile = min(256, rows)
    groups, unused, width = ctx.shape
    tall = pl.BlockSpec((tile, depth), lambda i: (i, 0))
    split_rows = pl.BlockSpec((groups, tile, width), lambda i: (0, i, 0))

    def full(shape):
        return pl.BlockSpec(shape, lambda i: (0,) * len(shape))

    def full_of(array):
        return full(array.shape)

    out_full = [(depth, depth), (depth, ff), (ff, depth), (2, depth), (6, depth), (1, ff)]
    return pl.pallas_call(
        middle_kernel,
        grid=(rows // tile,),
        in_specs=[tall, tall, tall, split_rows, split_rows]
        + [full_of(a) for a in weights + teacher_weights + vectors],
        out_specs=[tall, tall, split_rows] + [full(s) for s in out_full],
        out_shape=[
            jax.ShapeDtypeStruct((rows, depth), BF),
            jax.ShapeDtypeStruct((rows, depth), F32),
            jax.ShapeDtypeStruct((groups, rows, width), BF),
        ]
        + [jax.ShapeDtypeStruct(s, F32) for s in out_full],
        compiler_params=pltpu.CompilerParams(vmem_limit_bytes=VMEM_BYTES),
        name="middle",
    )(x, tx, cot, ctx, tctx, *weights, *teacher_weights, *vectors)


def shards(
    tokens,
    teacher_tokens,
    segment_ids,
    cotangent,
    latent_qkv,
    latent_out,
    latent_up,
    latent_down,
    student_gain,
    student_bias,
    student_up_bias,
    teacher_qkv,
    teacher_out,
    teacher_up,
    teacher_down,
    teacher_gain,
    teacher_bias,
    teacher_up_bias,
):
    streams, shard_len, depth = tokens.shape
    blocks = lax.axis_size("blk")
    groups = blocks // streams
    seq = shard_len * blocks
    rows = seq // groups
    width = depth // groups
    s, r = place(groups)

    gather, swap, by_rows = Gather(streams, groups), Swap(streams, groups), Rows(groups)
    whole_shape = (blocks, shard_len, depth)

    docs_all = lax.all_gather(segment_ids, "blk", axis=0, tiled=False)
    docs = lax.dynamic_index_in_dim(docs_all, s, axis=1, keepdims=False)
    big = docs[1, 0]
    docs = docs.reshape(streams, groups, shard_len).transpose(1, 0, 2).reshape(seq)
    in_big = docs == big

    (token_blocks,) = move(
        gather, [tokens], [jax.ShapeDtypeStruct(whole_shape, BF)], 1, "gather_tokens"
    )
    stream_tokens = token_blocks.reshape(seq, depth)

    def own_columns(matrices):
        mine = lax.dynamic_slice_in_dim(matrices, r * width, width, axis=2)
        return mine.transpose(1, 0, 2).reshape(depth, 3 * width)

    def own_bias(bias):
        q_part = lax.dynamic_slice_in_dim(bias[0], r * width, width, axis=0)
        v_part = lax.dynamic_slice_in_dim(bias[1], r * width, width, axis=0)
        return jnp.concatenate([q_part, jnp.zeros_like(q_part), v_part])

    scale = jnp.concatenate([jnp.full((width,), 0.125, F32), jnp.ones((2 * width,), F32)])

    bin_own = binarize(own_columns(latent_qkv).astype(F32)).astype(BF)
    bin_out = binarize(latent_out.astype(F32)).astype(BF)
    bin_up = binarize(latent_up.astype(F32)).astype(BF)
    bin_down = binarize(latent_down.astype(F32)).astype(BF)

    full_qkv = lax.all_gather(teacher_qkv, "dp", axis=1, tiled=True)
    full_out = lax.all_gather(teacher_out, "dp", axis=0, tiled=True)
    full_up = lax.all_gather(teacher_up, "dp", axis=0, tiled=True)
    full_down = lax.all_gather(teacher_down, "dp", axis=0, tiled=True)

    active = squash(stream_tokens.astype(F32)).astype(BF)
    qkv = ((dot(active, bin_own) + own_bias(student_bias)).astype(BF).astype(F32) * scale).astype(
        BF
    )
    numerators, context, inverse, teacher_blocks = attention(
        qkv, docs, gather, teacher_tokens, whole_shape, True, 2, "attention_student"
    )
    teacher_stream = teacher_blocks.reshape(seq, depth)
    teacher_own = (
        (dot(teacher_stream, own_columns(full_qkv)) + own_bias(teacher_bias))
        .astype(BF)
        .astype(F32)
        * scale
    ).astype(BF)
    teacher_context, cot_blocks = attention(
        teacher_own, docs, swap, cotangent, cotangent.shape, False, 3, "attention_teacher"
    )
    row_shape = (groups, rows, width)
    ctx_rows, tctx_rows = move(
        by_rows,
        [context.reshape(row_shape), teacher_context.reshape(row_shape)],
        [jax.ShapeDtypeStruct(row_shape, BF)] * 2,
        4,
        "context_rows",
    )
    own_rows = lax.dynamic_slice_in_dim(stream_tokens, r * rows, rows, axis=0)
    own_teacher = lax.dynamic_slice_in_dim(teacher_stream, r * rows, rows, axis=0)
    output, d_one, d_context, g_out, g_up, g_down, g_gain, g_bias, g_ub = middle(
        own_rows,
        own_teacher,
        cot_blocks.reshape(rows, depth),
        ctx_rows,
        tctx_rows,
        [bin_out, bin_up, bin_down],
        [full_out, full_up, full_down],
        [
            student_gain,
            student_bias,
            student_up_bias.reshape(1, -1),
            teacher_gain,
            teacher_bias,
            teacher_up_bias.reshape(1, -1),
        ],
    )
    early = lax.psum(
        (g_out.astype(BF), g_up.astype(BF), g_down.astype(BF)), ("dp", "blk")
    )
    (d_ctx_rows,) = move(
        by_rows, [d_context], [jax.ShapeDtypeStruct(row_shape, BF)], 5, "d_context_rows"
    )
    d_queries, d_keys, d_values, output_blocks = attention_back(
        numerators,
        qkv,
        teacher_own,
        d_ctx_rows.reshape(seq, width),
        context,
        inverse,
        docs,
        in_big,
        swap,
        output.reshape(streams, shard_len, depth),
        6,
    )
    d_qkv = jnp.concatenate([d_queries, d_keys, d_values], axis=1)
    g_own = dot(active, d_qkv, TN)
    d_active = dot(d_qkv, bin_own, NT).astype(BF)
    (d_active_parts,) = move(
        by_rows,
        [d_active.reshape(groups, rows, depth)],
        [jax.ShapeDtypeStruct((groups, rows, depth), BF)],
        7,
        "d_active_rows",
    )
    bent = jnp.tanh(own_rows.astype(F32) * (1.0 / clip_level))
    grad_rows = d_one + jnp.sum(d_active_parts.astype(F32), axis=0) * (1.0 - bent * bent)
    (grad_tokens,) = move(
        swap,
        [grad_rows.astype(BF).reshape(streams, shard_len, depth)],
        [jax.ShapeDtypeStruct((streams, shard_len, depth), BF)],
        8,
        "grad_tokens_back",
    )
    zero_at = jnp.zeros((3, depth, depth), BF)
    g_qkv = lax.dynamic_update_slice_in_dim(
        zero_at, g_own.reshape(depth, 3, width).transpose(1, 0, 2).astype(BF), r * width, axis=2
    )

    def columns_back(vector):
        return lax.dynamic_update_slice_in_dim(jnp.zeros((depth,), F32), vector, r * width, axis=0)

    g_bias = g_bias.at[0].set(columns_back(jnp.sum(d_queries.astype(F32), axis=0)))
    g_bias = g_bias.at[1].set(columns_back(jnp.sum(d_values.astype(F32), axis=0)))
    late, small = lax.psum(g_qkv, ("dp", "blk")), lax.psum((g_gain, g_bias, g_ub), ("dp", "blk"))
    return (
        output_blocks,
        grad_tokens,
        latent_grad(latent_qkv, late.astype(F32)),
        latent_grad(latent_out, early[0].astype(F32)),
        latent_grad(latent_up, early[1].astype(F32)),
        latent_grad(latent_down, early[2].astype(F32)),
        small[0],
        small[1],
        small[2].reshape(-1),
    )


def solution(mesh):
    return jax.shard_map(
        shards,
        mesh=mesh,
        in_specs=(
            P("dp", "blk", None),
            P("dp", "blk", None),
            P("dp", "blk"),
            P("dp", "blk", None),
            P(),
            P(),
            P(),
            P(),
            P(),
            P(),
            P(),
            P(None, "dp", None),
            P("dp", None),
            P("dp", None),
            P("dp", None),
            P(),
            P(),
            P(),
        ),
        out_specs=(P("dp", "blk", None), P("dp", "blk", None), P(), P(), P(), P(), P(), P(), P()),
        check_vma=False,
    )
```

time: 1510 us -> 544 us (0.36)
  waiting for transfers between devices: 738 us -> 44.8 us
  matrix products: 414 us -> 16.5 us
  Pallas kernels: 0 us -> 303 us
  other arithmetic: 172 us -> 48.5 us
  local copies, waits for them, and re-layouts: 88.7 us -> 27.2 us
    dot_general x67 -> x4, matrix products: 414 us -> 16.5 us  [dot(): return lax.dot_general(a, b, dims, preferred_element_type=F32)]
    ppermute x48 -> x0, waiting for transfers between devices: 358 us -> none  [shifted(): return lax.ppermute(block, axis, route)]
    pallas_call x0 -> x9, Pallas kernels: none -> 303 us  [the longest x5 133 us: move(): pl.pallas_call(kernel, out_shape=out_shapes, in_specs=[pl.BlockSpec(memor...]
    all_gather x7 -> x3, waiting for transfers between devices: 194 us -> 0.04 us  [the longest x1 0.02 us: shards(): full_down = lax.all_gather(teacher_down, 'dp', axis=0, tiled=True)]
    psum x1, waiting for transfers between devices: 184 us -> 43.4 us  [shards(): lax.psum(g_qkv, ('dp', 'blk'))]
    convert_element_type x36 -> x10, other arithmetic: 83.6 us -> 19.1 us  [the longest x1 4.01 us: shards(): g_up.astype(BF)]
    reduce_sum x11 -> x3, other arithmetic: 58.8 us -> 5.55 us  [the longest x1 2.5 us: shards(): jnp.sum(d_active_parts.astype(F32), axis=0) * (1.0 - bent * bent)]
    while x114 -> x0, local copies, waits for them, and re-layouts: 49.4 us -> none
  transfers between devices with their start and end apart: 56 -> 4, of which waited for: 30 -> 1; matrix products, arithmetic and copies ran while one was open for 23% -> 9% of each run, Pallas kernels for 0% -> 36%
where the time goes in v1:
time: 544 us; the launch traced here: 540 us
  Pallas kernels  303 us (56%)
  blocking collectives  85.3 us (16%)
  other arithmetic  48.5 us (9%)
  waiting for transfers between devices  44.8 us (8%)
  local copies, waits for them, and re-layouts  27.2 us (5%)
  matrix products  16.5 us (3%)
  between operations  14.4 us (3%)
    pallas_call x5, Pallas kernels, move(): pl.pallas_call(kernel, out_shape=out_shapes, in_specs=[pl.BlockSpec(memor...  133 us
    pallas_call x2, Pallas kernels, attention(): pl.pallas_call(functools.partial(forward_kernel, job, keep, tile, edge),...  81.9 us
    pallas_call x1, Pallas kernels, attention_back(): pl.pallas_call(functools.partial(backward_kernel, job, tile), grid=(pairs...  50 us
    psum x1, blocking collectives, shards(): lax.psum((g_gain, g_bias, g_ub), ('dp', 'blk'))  46.5 us
    psum x1, waiting for transfers between devices, shards(): lax.psum(g_qkv, ('dp', 'blk'))  43.4 us
    pallas_call x1, Pallas kernels, middle(): pl.pallas_call(middle_kernel, grid=(rows // tile,), in_specs=[tall, tall,...  38.4 us
    all_gather x1, blocking collectives, shards(): full_out = lax.all_gather(teacher_out, 'dp', axis=0, tiled=True)  22.9 us
    dot_general x4, matrix products, dot(): return lax.dot_general(a, b, dims, preferred_element_type=F32)  16.5 us
  transfers between devices with their start and end apart: 4, of which 1 were waited for; matrix products, arithmetic and copies ran while one was open for 9% of the time, Pallas kernels for 36%

profile of v1, /device:TPU:0, one launch (start us, length us, event | category | flops | bytes accessed | tf_op | source)
XLA Modules:
  0.0 539.6 jit_solution(13351240714066597003)
XLA Ops:
  7.2 2.0 copy.53
  9.3 0.7 all-gather.10.cloned.1.call-update
  10.1 0.7 all-gather.8.cloned.1.call-update
  10.8 15.8 %all-gather.1 = s32[8,4,256]{2,1,0:T(4,128)S(1)} all-gather(s32[1,4,256]{2,1,0:T(4,128)} %bitcast.80), channel_id=2, replica_groups=mesh['dp'=4,'blk'=8] {'blk'}, dimensions={0}, use_global_device_ids=true | all-gather | bytes 36864 | tf_op jit(solution)/shard_map/all_gather | solution.py:739
  26.7 1.9 reshape_reshape.12.col_ref
  28.6 0.6 reshape_reshape.5.row_ref
  29.2 0.8 fusion.42
  30.0 0.8 fusion.41
  30.8 0.3 copy.64
  31.1 0.2 fusion.21
  31.4 1.5 convert_multiply_fusion.15
  32.9 23.8 %gather_tokens.1 = bf16[8,256,512]{2,1,0:T(8,128)(2,1)} custom-call(bf16[4,256,512]{2,1,0:T(8,128)(2,1)} %refs_0_.1), custom_call_target="tpu_custom_call" | custom-call | tf_op jit(solution)/shard_map/gather_tokens/pallas_call | solution.py:241
  56.7 2.3 multiply_convert_fusion.4
  59.0 3.5 multiply_convert_fusion.1.q_ref.k_ref.v_ref
  62.5 47.2 %attention_student.1 = (bf16[4,2048,2048]{2,1,0:T(8,128)(2,1)}, bf16[2048,256]{1,0:T(8,128)(2,1)}, f32[2048,256]{1,0:T(8,128)}, bf16[8,256,512]{2,1,0:T(8,128)(2,1)}) custom-call(bf16[2048,768]{1,0:T(8,128)(2,1)} %multiply_convert_fusion.1.q_ref.k_ref.v_ref, bf16[2048,768]{1,0:T(8,128)(2,1)} %multiply_convert_fusion.1.q_ref.k_ref.v_ref, ...), custom_call_target="tpu_custom_call" | custom-call | tf_op jit(solution)/shard_map/attention_student/pallas_call | solution.py:356
  109.7 2.4 constant_dynamic-slice_fusion.tx_ref
  112.2 1.0 constant_dynamic-slice_fusion.1.x_ref
  113.2 0.5 fusion.13
  113.9 22.9 %all_gather.21.to_ref = bf16[512,512]{1,0:T(8,128)(2,1)} all-gather(bf16[128,512]{1,0:T(8,128)(2,1)S(1)} %copy-done.22), channel_id=1, replica_groups=mesh['dp'=4,'blk'=8] {'dp'}, dimensions={0}, use_global_device_ids=true | all-gather | bytes 655360 | tf_op jit(solution)/shard_map/all_gather | solution.py:767
  136.9 0.5 slice.50
  137.4 0.5 fusion.12
  137.9 1.0 multiply_convert_fusion.6.bo_ref
  138.9 1.7 compare_convert_fusion.bigc_ref
  140.6 2.1 multiply_convert_fusion.2.bdown_ref
  142.6 2.1 multiply_convert_fusion.3.bup_ref
  144.7 1.2 constant_dynamic-slice_fusion.4
  145.9 5.1 multiply_convert_fusion.q_ref.k_ref.v_ref.tq_ref.tk_ref
  151.0 34.7 %attention_teacher.1 = (bf16[2048,256]{1,0:T(8,128)(2,1)}, bf16[4,256,512]{2,1,0:T(8,128)(2,1)}) custom-call(bf16[2048,768]{1,0:T(8,128)(2,1)} %multiply_convert_fusion.q_ref.k_ref.v_ref.tq_ref.tk_ref, bf16[2048,768]{1,0:T(8,128)(2,1)} %multiply_convert_fusion.q_ref.k_ref.v_ref.tq_ref.tk_ref, ...), custom_call_target="tpu_custom_call" | custom-call | tf_op jit(solution)/shard_map/attention_teacher/pallas_call | solution.py:356
  185.7 33.0 %context_rows.1 = (bf16[2,1024,256]{2,1,0:T(8,128)(2,1)}, bf16[2,1024,256]{2,1,0:T(8,128)(2,1)}) custom-call(bf16[2,1024,256]{2,1,0:T(8,128)(2,1)} %bitcast.60, bf16[2,1024,256]{2,1,0:T(8,128)(2,1)} %bitcast.66), custom_call_target="tpu_custom_call" | custom-call | tf_op jit(solution)/shard_map/context_rows/pallas_call | solution.py:241
  218.8 38.4 %middle.1 = (bf16[1024,512]{1,0:T(8,128)(2,1)}, f32[1024,512]{1,0:T(8,128)}, bf16[2,1024,256]{2,1,0:T(8,128)(2,1)}, f32[512,512]{1,0:T(8,128)}, f32[512,2048]{1,...) custom-call(bf16[1024,512]{1,0:T(8,128)(2,1)} %constant_dynamic-slice_fusion.1.x_ref,, ...), custom_call_target="tpu_custom_call" | custom-call | tf_op jit(solution)/shard_map/middle/pallas_call | solution.py:691
  257.1 17.6 %d_context_rows.1 = bf16[2,1024,256]{2,1,0:T(8,128)(2,1)} custom-call(bf16[2,1024,256]{2,1,0:T(8,128)(2,1)} %get-tuple-element.61.refs_0_), custom_call_target="tpu_custom_call" | custom-call | tf_op jit(solution)/shard_map/d_context_rows/pallas_call | solution.py:241
  274.7 50.0 %attention_back.1 = (bf16[2048,256]{1,0:T(8,128)(2,1)}, bf16[2048,256]{1,0:T(8,128)(2,1)}, bf16[2048,256]{1,0:T(8,128)(2,1)}, bf16[4,256,512]{2,1,0:T(8,128)(2,1)}) custom-call(bf16[4,2048,2048]{2,1,0:T(8,128)(2,1)} %get-tuple-element.54.e_ref, bf16[2048,768]{1,0:T(8,128)(2,1)} %multiply_convert_fusion.1.q_ref.k_ref.v_ref, ...), custom_call_target="tpu_custom_call" | custom-call | tf_op jit(solution)/shard_map/attention_back/pallas_call | solution.py:525
  324.7 2.4 constant_dynamic-update-slice_fusion.2
  327.1 2.3 constant_dynamic-update-slice_fusion.1
  329.3 1.0 constant_dynamic-update-slice_fusion
  330.4 5.2 copy.58
  335.6 4.0 convert_element_type.155
  339.6 1.6 convert_element_type.157
  341.2 0.9 convert_element_type.153
  342.0 1.3 broadcast_in_dim.14
  343.3 0.7 copy-done.15
  344.0 2.8 fusion.26
  346.9 1.7 fusion.20
  348.6 1.8 fusion.24
  350.5 5.1 convolution_convert_fusion
  355.6 32.9 %d_active_rows.1 = bf16[2,1024,512]{2,1,0:T(8,128)(2,1)} custom-call(bf16[2,1024,512]{2,1,0:T(8,128)(2,1)} %bitcast.65), custom_call_target="tpu_custom_call" | custom-call | tf_op jit(solution)/shard_map/d_active_rows/pallas_call | solution.py:241
  388.5 2.5 convert_reduce_fusion
  391.0 0.5 copy-done.16
  391.5 1.6 add_convert_fusion.2
  393.1 25.3 %grad_tokens_back.1 = bf16[4,256,512]{2,1,0:T(8,128)(2,1)} custom-call(bf16[4,256,512]{2,1,0:T(8,128)(2,1)} %bitcast.59), custom_call_target="tpu_custom_call" | custom-call | tf_op jit(solution)/shard_map/grad_tokens_back/pallas_call | solution.py:241
  418.4 1.5 convert_reduce_fusion.2
  420.1 1.5 convert_reduce_fusion.1
  421.7 46.5 %all-reduce = (f32[2,512]{1,0:T(2,128)}, f32[6,512]{1,0:T(8,128)}, f32[2048]{0:T(1024)}) all-reduce(f32[2,512]{1,0:T(2,128)S(1)} %copy-done.25, f32[6,512]{1,0:T(8,128)S(1)} %scatter.9, f32[2048]{0:T(1024)S(1)} %bitcast.76), channel_id=1, replica_groups=mesh['dp'=4,'blk'=8] {'dp','blk'}, use_global_device_ids=true, to_apply=%region_18.19 | all-reduce | flops 6144 | bytes 49152 | tf_op jit(solution)/shard_map/psum | solution.py:863
  468.2 43.4 %all-reduce.4.cloned.1.call-done = (bf16[3,512,512]{2,1,0:T(8,128)(2,1)}, bf16[512,512]{1,0:T(8,128)(2,1)}, bf16[512,2048]{1,0:T(8,128)(2,1)}, bf16[2048,512]{1,0:T(8,128)(2,1)}) async-done(((bf16[3,512,512]{2,1,0:T(8,128)(2,1)}, bf16[512,512]{1,0:T(8,128)(2,1)}, bf16[512,2048]{1,0:T(8,128)(2,1)}, bf16[2048,512]{1,0:T(8,128)(2,1)}), (bf16[3,512,512]{2,1,0:T(8,128)(2,1)}, bf16[512,512]{1,0:T(8,128)(2,1)}, ...) | async-done | bytes 6291472 | tf_op jit(solution)/shard_map/psum | solution.py:863
  511.6 3.4 fusion.5
  515.1 3.4 add_add_fusion
  518.5 2.1 fusion.7
  520.6 3.4 add_add_fusion.1
  524.0 0.5 fusion.30
  524.6 1.5 add_add_fusion.3
  526.1 1.6 fusion.17
  527.7 3.2 add_add_fusion.2
  530.9 1.0 copy.80
  531.9 1.0 copy.81
  (87 shorter events, 0.9 us)
Async XLA Ops:
  7.2 23.6 %copy-start.4 = (bf16[3,512,512]{2,1,0:T(8,128)(2,1)S(1)}, bf16[3,512,512]{2,1,0:T(8,128)(2,1)}, u32[]{:S(2)}) copy-start(bf16[3,512,512]{2,1,0:T(8,128)(2,1)} %param.26) | copy-start | bytes 4718596
  7.2 137.5 %all-gather.6.cloned.1.call-start = ((), (), s32[]{:S(2)}) async-start(), calls=%async_computation | async-start | bytes 1966080 | tf_op jit(solution)/shard_map/all_gather | solution.py:766
  9.3 209.4 %all-gather.10.cloned.1.call-start = ((), (), s32[]{:S(2)}) async-start(), calls=%async_computation.2 | async-start | bytes 2621440 | tf_op jit(solution)/shard_map/all_gather | solution.py:769
  10.0 208.7 %all-gather.8.cloned.1.call-start = ((), (), s32[]{:S(2)}) async-start(), calls=%async_computation.1 | async-start | bytes 2621440 | tf_op jit(solution)/shard_map/all_gather | solution.py:768
  10.8 500.8 %all-reduce.4.cloned.1.call-start = ((), (), s32[]{:S(2)}) async-start(), calls=%async_computation.3 | async-start | bytes 12582912 | tf_op jit(solution)/shard_map/psum | solution.py:863
  32.9 26.1 %copy-start.26 = (f32[768]{0:T(1024)S(1)}, f32[768]{0:T(1024)}, u32[]{:S(2)}) copy-start(f32[768]{0:T(1024)} %constant.141.clone.1) | copy-start | bytes 9220
  58.9 3.6 copy-start.17
  62.5 49.6 %copy-start.6 = (bf16[8,256,512]{2,1,0:T(8,128)(2,1)S(1)}, bf16[8,256,512]{2,1,0:T(8,128)(2,1)}, u32[]{:S(2)}) copy-start(bf16[8,256,512]{2,1,0:T(8,128)(2,1)} %gather_tokens.1) | copy-start | bytes 6291460
  109.7 3.5 copy-start
  109.7 4.0 copy-start.8
  109.7 4.2 copy-start.22
  112.2 25.2 %copy-start.1 = (bf16[512,2048]{1,0:T(8,128)(2,1)S(1)}, bf16[512,2048]{1,0:T(8,128)(2,1)}, u32[]{:S(2)}) copy-start(bf16[512,2048]{1,0:T(8,128)(2,1)} %param.28) | copy-start | bytes 6291460
  113.2 25.7 %copy-start.3 = (s32[2048,1]{1,0:T(8,128)S(1)}, s32[2048,1]{1,0:T(8,128)}, u32[]{:S(2)}) copy-start(s32[2048,1]{1,0:T(8,128)} %reshape_reshape.12.col_ref) | copy-start | bytes 24580
  324.7 4.6 copy-start.14
  335.5 4.0 copy-start.12
  339.6 1.6 copy-start.20
  339.6 3.7 copy-start.18
  341.2 2.9 copy-start.15
  388.5 2.5 copy-start.7
  388.5 3.0 copy-start.16
  393.1 26.9 %copy-start.23 = (f32[6,512]{1,0:T(8,128)S(1)}, f32[6,512]{1,0:T(8,128)}, u32[]{:S(2)}) copy-start(f32[6,512]{1,0:T(8,128)} %get-tuple-element.73) | copy-start | bytes 36868
  393.1 28.6 %copy-start.24 = (f32[1,2048]{1,0:T(1,128)S(1)}, f32[1,2048]{1,0:T(1,128)}, u32[]{:S(2)}) copy-start(f32[1,2048]{1,0:T(1,128)} %get-tuple-element.74) | copy-start | bytes 24580
  393.1 28.6 %copy-start.25 = (f32[2,512]{1,0:T(2,128)S(1)}, f32[2,512]{1,0:T(2,128)}, u32[]{:S(2)}) copy-start(f32[2,512]{1,0:T(2,128)} %get-tuple-element.72) | copy-start | bytes 12292
  511.6 3.5 copy-start.10
  515.1 3.4 copy-start.2
  515.1 3.4 copy-start.9
  520.6 3.4 copy-start.19
  524.0 2.0 copy-start.5
  524.0 2.0 copy-start.11
  527.7 3.2 copy-start.21
  527.7 4.2 copy-start.13
Sparse Core Ops, SparseCore 0:
  10.4 33.5 all-gather.5
  45.8 35.3 all-gather.9
  83.0 35.3 all-gather.7
  347.0 164.5 all-reduce.3

commit v2 on v1

v2 whole, which is shorter than its diff:
```python
import functools

import jax
import jax.numpy as jnp
from jax import lax
from jax.experimental import pallas as pl
from jax.experimental.pallas import tpu as pltpu
from jax.sharding import PartitionSpec as P

HEADS = 8
BF = jnp.bfloat16
F32 = jnp.float32
LOG2E = 1.4426950408889634
clip_level = 2.5
masked_score = -1e30
VMEM_BYTES = 56 << 20
MESH = pl.DeviceIdType.MESH
NT = (((1,), (1,)), ((), ()))
TN = (((0,), (0,)), ((), ()))


def squash(tensor):
    return clip_level * jnp.tanh(tensor * (1.0 / clip_level))


def gelu_parts(tensor):
    phi = 0.5 * (1.0 + lax.erf(tensor * 0.7071067811865476))
    return tensor * phi, phi


def binarize(matrix):
    column_scale = jnp.sqrt(jnp.mean(matrix * matrix, axis=-2, keepdims=True) + 1e-06)
    return column_scale * jnp.tanh(2.0 * matrix / column_scale)


def layer_norm(tensor, gain_row, shift_row):
    centre = tensor - jnp.mean(tensor, axis=-1, keepdims=True)
    inverse_std = lax.rsqrt(jnp.mean(centre * centre, axis=-1, keepdims=True) + 1e-05)
    normed = centre * inverse_std
    return (normed * gain_row + shift_row, normed, inverse_std)


def norm_back(upstream, gain_row, normed, inverse_std):
    scaled = upstream * gain_row
    return inverse_std * (
        scaled
        - jnp.mean(scaled, axis=-1, keepdims=True)
        - normed * jnp.mean(scaled * normed, axis=-1, keepdims=True)
    )


def dot(a, b, dims=(((1,), (0,)), ((), ()))):
    return lax.dot_general(a, b, dims, preferred_element_type=F32)


def latent_grad(latent, binary_grad):
    matrix = latent.astype(F32)
    unused, pullback = jax.vjp(binarize, matrix)
    return pullback(binary_grad)[0]


def place(groups):
    here = lax.axis_index("blk")
    return here // groups, lax.rem(here, groups)


def greet(peers):
    barrier = pltpu.get_barrier_semaphore()
    for peer in peers:
        pl.semaphore_signal(barrier, inc=1, device_id=peer, device_id_type=MESH)
    pl.semaphore_wait(barrier, len(peers))


def stream_peers(streams, groups):
    s, r = place(groups)
    return [{"blk": lax.rem(s + d, streams) * groups + r} for d in range(1, streams)]


def core_peers(groups):
    s, r = place(groups)
    return [{"blk": s * groups + lax.rem(r + j, groups)} for j in range(1, groups)]


def dp_peers():
    size = lax.axis_size("dp")
    here = lax.axis_index("dp")
    return [{"dp": lax.rem(here + d, size)} for d in range(1, size)]


def unique(jobs):
    peers, kinds = [], []
    for job in jobs:
        for kind, found in job.peers():
            if kind not in kinds:
                kinds.append(kind)
                peers += found
    return peers


def remote(source, target, send, recv, peer):
    return pltpu.make_async_remote_copy(
        src_ref=source,
        dst_ref=target,
        send_sem=send,
        recv_sem=recv,
        device_id=peer,
        device_id_type=MESH,
    )


def dma(count):
    return pltpu.SemaphoreType.DMA((count,))


class Staged:
    def __init__(self, source, target, stage, sems):
        self.load = pltpu.make_async_copy(source, stage, sems.at[0])
        self.store = pltpu.make_async_copy(stage, target, sems.at[1])

    def first(self):
        self.load.start()

    def last(self):
        self.load.wait()
        self.store.start()
        self.store.wait()


class Gather:
    def __init__(self, streams, groups, block, dtype):
        self.streams, self.groups, self.block, self.dtype = streams, groups, block, dtype

    def scratch(self):
        b, g = self.streams, self.groups
        return [dma(b), dma(b), dma(b * g), dma(b * g), pltpu.VMEM(self.block, self.dtype), dma(2)]

    def out_shape(self):
        return jax.ShapeDtypeStruct((self.streams * self.groups,) + self.block, self.dtype)

    def peers(self):
        return [
            ("stream", stream_peers(self.streams, self.groups)),
            ("core", core_peers(self.groups)),
        ]

    def parts(self, source, target, send, recv, share_send, share_recv, stage, sems):
        b, g = self.streams, self.groups
        s, r = place(g)
        peers, cores = stream_peers(b, g), core_peers(g)
        swaps = [
            remote(
                source.at[lax.rem(s + d, b)],
                target.at[r * b + s],
                send.at[d],
                recv.at[d],
                peers[d - 1],
            )
            for d in range(1, b)
        ]
        shares = [
            [
                remote(
                    source.at[s] if d == 0 else target.at[r * b + lax.rem(s + b - d, b)],
                    target.at[r * b + lax.rem(s + b - d, b)],
                    share_send.at[j * b + d],
                    share_recv.at[j * b + d],
                    cores[j - 1],
                )
                for j in range(1, g)
            ]
            for d in range(b)
        ]
        own = Staged(source.at[s], target.at[r * b + s], stage, sems)
        return swaps, shares, own

    def first(self, *refs):
        swaps, shares, own = self.parts(*refs)
        for copy in swaps:
            copy.start()
        own.first()
        for copy in shares[0]:
            copy.start()

    def last(self, *refs):
        swaps, shares, own = self.parts(*refs)
        own.last()
        for d in [1, 3, 2] if self.streams == 4 else range(1, self.streams):
            swaps[d - 1].wait_recv()
            for copy in shares[d]:
                copy.start()
        for row in shares:
            for copy in row:
                copy.wait()
        for copy in swaps:
            copy.wait_send()


class Swap:
    def __init__(self, streams, groups, block, dtype):
        self.streams, self.groups, self.block, self.dtype = streams, groups, block, dtype

    def scratch(self):
        return [dma(self.streams), dma(self.streams), pltpu.VMEM(self.block, self.dtype), dma(2)]

    def out_shape(self):
        return jax.ShapeDtypeStruct((self.streams,) + self.block, self.dtype)

    def peers(self):
        return [("stream", stream_peers(self.streams, self.groups))]

    def parts(self, source, target, send, recv, stage, sems):
        b, g = self.streams, self.groups
        s, r = place(g)
        peers = stream_peers(b, g)
        swaps = [
            remote(source.at[lax.rem(s + d, b)], target.at[s], send.at[d], recv.at[d], peers[d - 1])
            for d in range(1, b)
        ]
        return swaps, Staged(source.at[s], target.at[s], stage, sems)

    def first(self, *refs):
        swaps, own = self.parts(*refs)
        for copy in swaps:
            copy.start()
        own.first()

    def last(self, *refs):
        swaps, own = self.parts(*refs)
        own.last()
        for copy in swaps:
            copy.wait()


class Rows:
    def __init__(self, streams, groups, block, dtype):
        self.groups, self.block, self.dtype = groups, block, dtype

    def scratch(self):
        return [dma(self.groups), dma(self.groups), pltpu.VMEM(self.block, self.dtype), dma(2)]

    def out_shape(self):
        return jax.ShapeDtypeStruct((self.groups,) + self.block, self.dtype)

    def peers(self):
        return [("core", core_peers(self.groups))]

    def parts(self, source, target, send, recv, stage, sems):
        g = self.groups
        s, r = place(g)
        cores = core_peers(g)
        copies = [
            remote(source.at[lax.rem(r + j, g)], target.at[r], send.at[j], recv.at[j], cores[j - 1])
            for j in range(1, g)
        ]
        return copies, Staged(source.at[r], target.at[r], stage, sems)

    first = Swap.first
    last = Swap.last


class Spread:
    def __init__(self, block, dtype):
        self.block, self.dtype = block, dtype

    def scratch(self):
        size = lax.axis_size("dp")
        return [dma(size), dma(size), pltpu.VMEM(self.block, self.dtype), dma(2)]

    def out_shape(self):
        return jax.ShapeDtypeStruct((lax.axis_size("dp"),) + self.block, self.dtype)

    def peers(self):
        return [("dp", dp_peers())]

    def parts(self, source, target, send, recv, stage, sems):
        here = lax.axis_index("dp")
        copies = [
            remote(source, target.at[here], send.at[d], recv.at[d], peer)
            for d, peer in enumerate(dp_peers(), 1)
        ]
        return copies, Staged(source, target.at[here], stage, sems)

    first = Swap.first
    last = Swap.last


class Moves:
    def __init__(self, *jobs):
        self.jobs = jobs
        self.counts = [len(job.scratch()) for job in jobs]

    def scratch(self):
        return [item for job in self.jobs for item in job.scratch()]

    def out_shapes(self):
        return [job.out_shape() for job in self.jobs]

    def spaces(self):
        return [pl.BlockSpec(memory_space=pl.ANY)] * len(self.jobs)

    def each(self, sources, targets, scratch):
        at = 0
        for job, count, source, target in zip(self.jobs, self.counts, sources, targets):
            yield job, (source, target, *scratch[at : at + count])
            at += count

    def first(self, sources, targets, scratch):
        greet(unique(self.jobs))
        for job, refs in self.each(sources, targets, scratch):
            job.first(*refs)

    def last(self, sources, targets, scratch):
        for job, refs in self.each(sources, targets, scratch):
            job.last(*refs)


def remote_params(collective_id):
    return pltpu.CompilerParams(
        collective_id=collective_id, has_side_effects=True, vmem_limit_bytes=VMEM_BYTES
    )


def move(moves, arrays, collective_id, name):
    count = len(arrays)

    def kernel(*refs):
        sources, targets, scratch = refs[:count], refs[count : 2 * count], refs[2 * count :]
        moves.first(sources, targets, scratch)
        moves.last(sources, targets, scratch)

    return pl.pallas_call(
        kernel,
        out_shape=moves.out_shapes(),
        in_specs=moves.spaces(),
        out_specs=moves.spaces(),
        scratch_shapes=moves.scratch(),
        compiler_params=remote_params(collective_id),
        name=name,
    )(*arrays)


def binary_columns(latent):
    matrix = latent.astype(F32)
    scale = jnp.sqrt(jnp.mean(matrix * matrix, axis=0, keepdims=True) + 1e-06)
    return (scale * jnp.tanh(matrix * (2.0 / scale))).astype(BF)


def intake_kernel(moves, qkv_ref, out_ref, up_ref, down_ref, *refs):
    count = len(moves.jobs)
    sources = refs[:count]
    own_bin, out_bin, up_bin, down_bin = refs[count : count + 4]
    targets = refs[count + 4 : 2 * count + 4]
    scratch = refs[2 * count + 4 :]
    moves.first(sources, targets, scratch)
    for i in range(3):
        own_bin[i] = binary_columns(qkv_ref[i])
    out_bin[...] = binary_columns(out_ref[...])
    for i in range(0, up_ref.shape[1], 512):
        up_bin[:, i : i + 512] = binary_columns(up_ref[:, i : i + 512])
    for i in range(0, down_ref.shape[1], 128):
        down_bin[:, i : i + 128] = binary_columns(down_ref[:, i : i + 128])
    moves.last(sources, targets, scratch)


def intake(moves, latents, arrays, collective_id):
    vmem = pl.BlockSpec(memory_space=pltpu.VMEM)
    return pl.pallas_call(
        functools.partial(intake_kernel, moves),
        out_shape=[jax.ShapeDtypeStruct(a.shape, BF) for a in latents] + moves.out_shapes(),
        in_specs=[vmem] * 4 + moves.spaces(),
        out_specs=[vmem] * 4 + moves.spaces(),
        scratch_shapes=moves.scratch(),
        compiler_params=remote_params(collective_id),
        name="intake",
    )(*latents, *arrays)


def lanes_of(shape):
    return lax.broadcasted_iota(jnp.int32, shape, 1)


def forward_kernel(moves, keep, tile, edge, q_ref, k_ref, v_ref, col_ref, row_ref, *rest):
    count = len(moves.jobs)
    sources, rest = rest[:count], rest[count:]
    if keep:
        e_ref, ctx_ref, inv_ref, *rest = rest
    else:
        ctx_ref, *rest = rest
    targets, (k_aug, v_aug, *scratch) = rest[:count], rest[count:]
    pair, step = pl.program_id(0), pl.program_id(1)
    steps = pl.num_programs(1)
    seq = k_ref.shape[0]

    @pl.when((pair == 0) & (step == 0))
    def _():
        moves.first(sources, targets, scratch)

    @pl.when(step == 0)
    def _():
        low = lanes_of((seq, 128)) < 64
        lane = lanes_of((seq, 128))
        keys = k_ref[...].astype(F32)
        turned = pltpu.roll(keys, 64, 1)
        k_aug[0] = jnp.where(low, keys, turned).astype(BF)
        k_aug[1] = jnp.where(low, turned, keys).astype(BF)
        values = v_ref[...].astype(F32)
        v_aug[0] = jnp.where(low, values, jnp.where(lane < 66, 1.0, 0.0)).astype(BF)
        v_aug[1] = jnp.where(low, jnp.where(lane < 2, 1.0, 0.0), values).astype(BF)

    def body(whole):
        low = lanes_of((tile, 128)) < 64
        scaled = q_ref[...].astype(F32) * LOG2E
        upper = scaled.astype(BF).astype(F32)
        rest_part = scaled - upper
        results = []
        for h in range(2):
            if h == 0:
                q_aug = jnp.where(low, upper, pltpu.roll(rest_part, 64, 1)).astype(BF)
            else:
                q_aug = jnp.where(low, pltpu.roll(upper, 64, 1), rest_part).astype(BF)
            scores = dot(q_aug, k_aug[h], NT)
            if whole:
                scores = jnp.where(col_ref[...] == row_ref[...], scores, masked_score)
            else:
                left = jnp.where(
                    col_ref[...] == row_ref[:, :edge], scores[:, :edge], masked_score
                )
                right = jnp.where(
                    col_ref[...] == row_ref[:, seq - edge :], scores[:, seq - edge :], masked_score
                )
                scores = jnp.concatenate([left, scores[:, edge : seq - edge], right], axis=1)
            peak = jnp.max(scores, axis=1, keepdims=True)
            numerators = jnp.exp2(scores - peak).astype(BF)
            if keep:
                e_ref[h] = numerators
            total = dot(numerators, v_aug[h])
            where_sum = 64 if h == 0 else 0
            inverse = 1.0 / total[:, where_sum : where_sum + 1]
            results.append((total * inverse, inverse))
        ctx_ref[...] = jnp.where(low, results[0][0], results[1][0]).astype(BF)
        if keep:
            inv_ref[...] = jnp.where(low, results[0][1], results[1][1])

    at_edge = (step == 0) | (step == steps - 1)

    @pl.when(at_edge)
    def _():
        body(True)

    @pl.when(jnp.logical_not(at_edge))
    def _():
        body(False)

    @pl.when((pair == pl.num_programs(0) - 1) & (step == steps - 1))
    def _():
        moves.last(sources, targets, scratch)


def attention(qkv, docs, moves, moved, keep, collective_id, name):
    seq, width3 = qkv.shape
    width = width3 // 3
    pairs = width // 128
    tile = 256
    edge = 256
    col = docs.reshape(seq, 1)
    row = docs.reshape(1, seq)
    blocks = [
        pl.BlockSpec((tile, 128), lambda p, i: (i, p)),
        pl.BlockSpec((seq, 128), lambda p, i: (0, pairs + p)),
        pl.BlockSpec((seq, 128), lambda p, i: (0, 2 * pairs + p)),
        pl.BlockSpec((tile, 1), lambda p, i: (i, 0)),
        pl.BlockSpec((1, seq), lambda p, i: (0, 0)),
    ] + moves.spaces()
    outs = [pl.BlockSpec((tile, 128), lambda p, i: (i, p))]
    shapes = [jax.ShapeDtypeStruct((seq, width), BF)]
    if keep:
        outs = [pl.BlockSpec((2, tile, seq), lambda p, i: (p, i, 0))] + outs
        shapes = [jax.ShapeDtypeStruct((2 * pairs, seq, seq), BF)] + shapes
        outs = outs + [pl.BlockSpec((tile, 128), lambda p, i: (i, p))]
        shapes = shapes + [jax.ShapeDtypeStruct((seq, width), F32)]
    return pl.pallas_call(
        functools.partial(forward_kernel, moves, keep, tile, edge),
        grid=(pairs, seq // tile),
        in_specs=blocks,
        out_specs=outs + moves.spaces(),
        out_shape=shapes + moves.out_shapes(),
        scratch_shapes=[pltpu.VMEM((2, seq, 128), BF), pltpu.VMEM((2, seq, 128), BF)]
        + moves.scratch(),
        compiler_params=remote_params(collective_id),
        name=name,
    )(qkv, qkv, qkv, col, row, *moved)


def split(matrix):
    upper = matrix.astype(BF)
    return upper, (matrix - upper.astype(F32)).astype(BF)


def backward_kernel(
    moves,
    tile,
    e_ref,
    q_ref,
    k_ref,
    v_ref,
    tq_ref,
    tk_ref,
    dc_ref,
    ctx_ref,
    inv_ref,
    col_ref,
    row_ref,
    bigc_ref,
    *rest,
):
    count = len(moves.jobs)
    sources, (dq_ref, dk_ref, dv_ref, *rest) = rest[:count], rest[count:]
    targets, (v_aug, dk_acc, dv_acc, grams, *scratch) = rest[:count], rest[count:]
    pair, step = pl.program_id(0), pl.program_id(1)
    steps = pl.num_programs(1)
    seq = k_ref.shape[0]
    share = 1.0 / seq

    @pl.when((pair == 0) & (step == 0))
    def _():
        moves.first(sources, targets, scratch)

    @pl.when(step == 0)
    def _():
        lane = lanes_of((seq, 128))
        low = lane < 64
        values = v_ref[...].astype(F32)
        v_aug[0] = jnp.where(low, values, jnp.where(lane < 66, 1.0, 0.0)).astype(BF)
        v_aug[1] = jnp.where(low, jnp.where(lane < 2, 1.0, 0.0), values).astype(BF)
        dk_acc[...] = jnp.zeros_like(dk_acc)
        dv_acc[...] = jnp.zeros_like(dv_acc)
        in_big = bigc_ref[...] > 0.0
        kb = jnp.where(in_big, k_ref[...].astype(F32), 0.0).astype(BF)
        tkb = jnp.where(in_big, tk_ref[...].astype(F32), 0.0).astype(BF)
        qb = jnp.where(in_big, q_ref[...].astype(F32), 0.0).astype(BF)
        tqb = jnp.where(in_big, tq_ref[...].astype(F32), 0.0).astype(BF)
        same_head = (lax.broadcasted_iota(jnp.int32, (128, 128), 0) < 64) == (
            lanes_of((128, 128)) < 64
        )
        for i, (a, b) in enumerate(((kb, kb), (tkb, kb), (qb, qb), (tqb, qb))):
            gram = jnp.where(same_head, dot(a, b, TN) * share, 0.0)
            grams[2 * i], grams[2 * i + 1] = split(gram)

    start = pl.multiple_of(step * tile, tile)
    rows = pl.ds(start, tile)
    lane = lanes_of((tile, 128))
    low = lane < 64

    def body(whole, columns):
        in_big = bigc_ref[rows, :] > 0.0
        q8 = q_ref[rows, :]
        tq8 = tq_ref[rows, :]
        dc = dc_ref[...].astype(F32)
        inv = inv_ref[...]
        scaled = dc * inv
        product = scaled * ctx_ref[...].astype(F32)
        scaled_low = scaled.astype(BF)
        q_turned = q8.astype(F32).T.astype(BF)
        dc_turned = scaled_low.astype(F32).T.astype(BF)
        d_queries = []
        for h in range(2):
            mine = low if h == 0 else jnp.logical_not(low)
            delta = -jnp.sum(jnp.where(mine, product, 0.0), axis=1, keepdims=True)
            upper = delta.astype(BF).astype(F32)
            first = 64 if h == 0 else 0
            extra = jnp.where(
                lane == first, upper, jnp.where(lane == first + 1, delta - upper, 0.0)
            )
            dc_aug = jnp.where(mine, scaled, extra).astype(BF)
            numerators = e_ref[h]
            d_probs = dot(dc_aug, v_aug[h], NT)
            d_scores = numerators.astype(F32) * d_probs
            if whole:
                q_mine = jnp.where(mine, q8, 0.0).astype(BF)
                tq_mine = jnp.where(mine, tq8, 0.0).astype(BF)
                gap = dot(q_mine, k_ref[columns, :], NT) - dot(tq_mine, tk_ref[columns, :], NT)
                small = (col_ref[...] == row_ref[:, columns]) & jnp.logical_not(in_big)
                gap = jnp.where(small, gap * share, 0.0)
                if columns.start == 0:
                    d_scores = jnp.concatenate(
                        [d_scores[:, :tile] + gap, d_scores[:, tile:]], axis=1
                    )
                else:
                    d_scores = jnp.concatenate(
                        [d_scores[:, : seq - tile], d_scores[:, seq - tile :] + gap], axis=1
                    )
            d_scores = d_scores.astype(BF)
            d_queries.append(dot(d_scores, k_ref[...]))
            half = slice(64 * h, 64 * h + 64)
            dk_acc[half, :] += dot(q_turned[half, :], d_scores)
            dv_acc[half, :] += dot(dc_turned[half, :], numerators)
        d_query = jnp.where(low, d_queries[0], d_queries[1])
        qb = jnp.where(in_big, q8.astype(F32), 0.0).astype(BF)
        tqb = jnp.where(in_big, tq8.astype(F32), 0.0).astype(BF)
        d_query += dot(qb, grams[0]) + dot(qb, grams[1]) - dot(tqb, grams[2]) - dot(tqb, grams[3])
        dq_ref[...] = (d_query * 0.125).astype(BF)

    @pl.when(step == 0)
    def _():
        body(True, slice(0, tile))

    @pl.when(step == steps - 1)
    def _():
        body(True, slice(seq - tile, seq))

    @pl.when((step > 0) & (step < steps - 1))
    def _():
        body(False, None)

    @pl.when(step == steps - 1)
    def _():
        in_big = bigc_ref[...] > 0.0
        kb = jnp.where(in_big, k_ref[...].astype(F32), 0.0).astype(BF)
        tkb = jnp.where(in_big, tk_ref[...].astype(F32), 0.0).astype(BF)
        d_key = dk_acc[...].T
        d_key += dot(kb, grams[4]) + dot(kb, grams[5]) - dot(tkb, grams[6]) - dot(tkb, grams[7])
        dk_ref[...] = d_key.astype(BF)
        dv_ref[...] = dv_acc[...].T.astype(BF)

    @pl.when((pair == pl.num_programs(0) - 1) & (step == steps - 1))
    def _():
        moves.last(sources, targets, scratch)


def attention_back(
    numerators, qkv, teacher_qkv, d_context, context, inverse, docs, in_big, moves, moved, collective_id
):
    seq, width3 = qkv.shape
    width = width3 // 3
    pairs = width // 128
    tile = 256
    part = pl.BlockSpec((tile, 128), lambda p, i: (i, p))

    def whole(which):
        return pl.BlockSpec((seq, 128), lambda p, i: (0, which * pairs + p))

    return pl.pallas_call(
        functools.partial(backward_kernel, moves, tile),
        grid=(pairs, seq // tile),
        in_specs=[
            pl.BlockSpec((2, tile, seq), lambda p, i: (p, i, 0)),
            whole(0),
            whole(1),
            whole(2),
            whole(0),
            whole(1),
            part,
            part,
            part,
            pl.BlockSpec((tile, 1), lambda p, i: (i, 0)),
            pl.BlockSpec((1, seq), lambda p, i: (0, 0)),
            pl.BlockSpec((seq, 1), lambda p, i: (0, 0)),
        ]
        + moves.spaces(),
        out_specs=[part, whole(0), whole(0)] + moves.spaces(),
        out_shape=[
            jax.ShapeDtypeStruct((seq, width), BF),
            jax.ShapeDtypeStruct((seq, width), BF),
            jax.ShapeDtypeStruct((seq, width), BF),
        ]
        + moves.out_shapes(),
        scratch_shapes=[
            pltpu.VMEM((2, seq, 128), BF),
            pltpu.VMEM((128, seq), F32),
            pltpu.VMEM((128, seq), F32),
            pltpu.VMEM((8, 128, 128), BF),
        ]
        + moves.scratch(),
        compiler_params=remote_params(collective_id),
        name="attention_back",
    )(
        numerators,
        qkv,
        qkv,
        qkv,
        teacher_qkv,
        teacher_qkv,
        d_context,
        context,
        inverse,
        docs.reshape(seq, 1),
        docs.reshape(1, seq),
        in_big.astype(F32).reshape(seq, 1),
        *moved,
    )


def middle_kernel(
    unused_place,
    x_ref,
    tx_ref,
    cot_ref,
    ctx_ref,
    tctx_ref,
    bo_ref,
    bup_ref,
    bdown_ref,
    to_ref,
    tup_ref,
    tdown_ref,
    sg_ref,
    sb_ref,
    sub_ref,
    tg_ref,
    tb_ref,
    tub_ref,
    out_ref,
    d1_ref,
    dctx_ref,
    gout_ref,
    gup_ref,
    gdown_ref,
    ggain_ref,
    gbias_ref,
    gub_ref,
):
    step = pl.program_id(0)
    groups = ctx_ref.shape[0]
    width = ctx_ref.shape[2]

    @pl.when(step == 0)
    def _():
        for ref in (gout_ref, gup_ref, gdown_ref, ggain_ref, gbias_ref, gub_ref):
            ref[...] = jnp.zeros_like(ref)

    def row(ref, i):
        return ref[i : i + 1, :]

    tctx = jnp.concatenate([tctx_ref[j] for j in range(groups)], axis=1)
    t_att = dot(tctx, to_ref[...]) + row(tb_ref, 2)
    t_hidden = layer_norm(tx_ref[...].astype(F32) + t_att, row(tg_ref, 0), row(tb_ref, 3))[0]
    t_inner = gelu_parts(dot(t_hidden.astype(BF), tup_ref[...]) + tub_ref[...])[0]
    t_out = layer_norm(
        t_hidden + dot(t_inner.astype(BF), tdown_ref[...]) + row(tb_ref, 4),
        row(tg_ref, 1),
        row(tb_ref, 5),
    )[0]

    context = jnp.concatenate([ctx_ref[j] for j in range(groups)], axis=1).astype(F32)
    bent = jnp.tanh(context * (1.0 / clip_level))
    ctx_active = (clip_level * bent).astype(BF)
    ctx_slope = 1.0 - bent * bent
    attended = dot(ctx_active, bo_ref[...]) + row(sb_ref, 2)
    hidden, normed_one, inverse_one = layer_norm(
        x_ref[...].astype(F32) + attended, row(sg_ref, 0), row(sb_ref, 3)
    )
    bent = jnp.tanh(hidden * (1.0 / clip_level))
    hidden_active = (clip_level * bent).astype(BF)
    hidden_slope = 1.0 - bent * bent
    inner_pre = dot(hidden_active, bup_ref[...]) + sub_ref[...]
    inner_act, phi = gelu_parts(inner_pre)
    bent = jnp.tanh(inner_act * (1.0 / clip_level))
    inner_active = (clip_level * bent).astype(BF)
    slope = (1.0 - bent * bent) * (
        phi + inner_pre * jnp.exp(-0.5 * inner_pre * inner_pre) * 0.3989422804014327
    )
    branch = dot(inner_active, bdown_ref[...]) + row(sb_ref, 4)
    output, normed_two, inverse_two = layer_norm(hidden + branch, row(sg_ref, 1), row(sb_ref, 5))
    out_ref[...] = output.astype(BF)
    upstream = cot_ref[...].astype(F32) + 0.5 * (output - t_out)
    d_two = norm_back(upstream, row(sg_ref, 1), normed_two, inverse_two)
    d_branch = d_two.astype(BF)
    gdown_ref[...] += dot(inner_active, d_branch, TN)
    d_inner = (dot(d_branch, bdown_ref[...], NT) * slope).astype(BF)
    gup_ref[...] += dot(hidden_active, d_inner, TN)
    d_hidden = d_two + dot(d_inner, bup_ref[...], NT) * hidden_slope
    d_one = norm_back(d_hidden, row(sg_ref, 0), normed_one, inverse_one)
    d1_ref[...] = d_one
    d_attended = d_one.astype(BF)
    gout_ref[...] += dot(ctx_active, d_attended, TN)
    d_context = (dot(d_attended, bo_ref[...], NT) * ctx_slope).astype(BF)
    for j in range(groups):
        dctx_ref[j] = d_context[:, j * width : (j + 1) * width]

    def total(value):
        return jnp.sum(value, axis=0, keepdims=True)

    ggain_ref[0:1, :] += total(d_hidden * normed_one)
    ggain_ref[1:2, :] += total(upstream * normed_two)
    gbias_ref[2:3, :] += total(d_attended.astype(F32))
    gbias_ref[3:4, :] += total(d_hidden)
    gbias_ref[4:5, :] += total(d_branch.astype(F32))
    gbias_ref[5:6, :] += total(upstream)
    gub_ref[...] += total(d_inner.astype(F32))


def middle(r, x, tx, cot, ctx, tctx, weights, teacher_weights, vectors):
    rows, depth = cot.shape
    ff = weights[1].shape[1]
    tile = min(256, rows)
    groups, unused, width = ctx.shape
    steps = rows // tile
    tall = pl.BlockSpec((tile, depth), lambda i, r: (i, 0))
    of_stream = pl.BlockSpec((tile, depth), lambda i, r: (r[0] * steps + i, 0))
    split_rows = pl.BlockSpec((groups, tile, width), lambda i, r: (0, i, 0))

    def full(shape):
        return pl.BlockSpec(shape, lambda i, r: (0,) * len(shape))

    def full_of(array):
        return full(array.shape)

    out_full = [(depth, depth), (depth, ff), (ff, depth), (2, depth), (6, depth), (1, ff)]
    return pl.pallas_call(
        middle_kernel,
        grid_spec=pltpu.PrefetchScalarGridSpec(
            num_scalar_prefetch=1,
            grid=(steps,),
            in_specs=[of_stream, of_stream, tall, split_rows, split_rows]
            + [full_of(a) for a in weights + teacher_weights + vectors],
            out_specs=[tall, tall, split_rows] + [full(s) for s in out_full],
        ),
        out_shape=[
            jax.ShapeDtypeStruct((rows, depth), BF),
            jax.ShapeDtypeStruct((rows, depth), F32),
            jax.ShapeDtypeStruct((groups, rows, width), BF),
        ]
        + [jax.ShapeDtypeStruct(s, F32) for s in out_full],
        compiler_params=pltpu.CompilerParams(vmem_limit_bytes=VMEM_BYTES),
        name="middle",
    )(r.reshape(1), x, tx, cot, ctx, tctx, *weights, *teacher_weights, *vectors)


def finish_kernel(
    streams,
    groups,
    wire,
    dq_ref,
    dk_ref,
    dv_ref,
    active_ref,
    bin_ref,
    d1_ref,
    tokens_ref,
    small_ref,
    grad_ref,
    late_ref,
    sum_ref,
    mine,
    outbox,
    inbox,
    x_rows,
    blocks,
    partial,
    partial_wire,
    dp_box,
    chunk_wire,
    z_box,
    piece,
    small_send,
    small_dp,
    small_z,
    small_core,
    x_sem,
    core_send,
    core_recv,
    back_send,
    back_recv,
    dp_send,
    dp_recv,
    z_send,
    z_recv,
    zg_send,
    zg_recv,
    dpg_send,
    dpg_recv,
    cg_send,
    cg_recv,
    ss,
    sr,
    local_sems,
):
    size = lax.axis_size("dp")
    here = lax.axis_index("dp")
    s, r = place(groups)
    rows, depth = mine.shape
    width = dq_ref.shape[1]
    parts = (dq_ref, dk_ref, dv_ref)
    along_z, cores, along_dp = stream_peers(streams, groups), core_peers(groups), dp_peers()
    greet(along_z + cores + along_dp)
    load = pltpu.make_async_copy(tokens_ref.at[pl.ds(r * streams, streams)], x_rows, x_sem)
    load.start()

    def d_active(start):
        total = None
        for i, ref in enumerate(parts):
            term = dot(ref[pl.ds(start, rows), :], bin_ref[i], NT)
            total = term if total is None else total + term
        return total

    core_copies = []
    for j in range(1, groups):
        other = lax.rem(r + j, groups)
        outbox[j - 1] = d_active(pl.multiple_of(other * rows, rows)).astype(BF)
        copy = remote(
            outbox.at[j - 1], inbox.at[j - 1], core_send.at[j], core_recv.at[j], cores[j - 1]
        )
        copy.start()
        core_copies.append(copy)

    chunk = depth // size
    for i, ref in enumerate(parts):
        partial[:, i * width : (i + 1) * width] = dot(active_ref[...], ref[...], TN)
    for p in range(size):
        partial_wire[p] = partial[p * chunk : (p + 1) * chunk, :].astype(wire)
    dp_copies = []
    for d, peer in enumerate(along_dp, 1):
        copy = remote(
            partial_wire.at[lax.rem(here + d, size)],
            dp_box.at[d - 1],
            dp_send.at[d],
            dp_recv.at[d],
            peer,
        )
        copy.start()
        dp_copies.append(copy)

    def own_columns(vector):
        return jnp.concatenate(
            [jnp.where(r == j, vector, 0.0) for j in range(groups)], axis=1
        )

    small_send[0] = small_ref[...]
    small_send[0, 2:3, :] = own_columns(jnp.sum(dq_ref[...].astype(F32), axis=0, keepdims=True))
    small_send[0, 3:4, :] = own_columns(jnp.sum(dv_ref[...].astype(F32), axis=0, keepdims=True))
    small_copies = []
    for d, peer in enumerate(along_dp, 1):
        copy = remote(small_send.at[0], small_dp.at[d - 1], ss.at[d], sr.at[d], peer)
        copy.start()
        small_copies.append(copy)

    mine[...] = d_active(pl.multiple_of(r * rows, rows))
    load.wait()
    for copy in core_copies:
        copy.wait_recv()
    shard = rows // streams
    back_copies = []
    order = [2, 1, 3] if streams == 4 else list(range(1, streams))
    for d in order + [0]:
        target = lax.rem(s + d, streams)
        at = pl.ds(pl.multiple_of(target * shard, shard), shard)
        bent = jnp.tanh(x_rows[target].astype(F32) * (1.0 / clip_level))
        total = mine[at, :]
        for j in range(groups - 1):
            total = total + inbox[j, at, :].astype(F32)
        blocks[target] = (d1_ref[at, :] + total * (1.0 - bent * bent)).astype(BF)
        if d:
            copy = remote(
                blocks.at[target], grad_ref.at[s], back_send.at[d], back_recv.at[d], along_z[d - 1]
            )
        else:
            copy = pltpu.make_async_copy(blocks.at[s], grad_ref.at[s], local_sems.at[0])
        copy.start()
        back_copies.append(copy)

    for copy in dp_copies:
        copy.wait_recv()
    total = partial[pl.ds(pl.multiple_of(here * chunk, chunk), chunk), :]
    for d in range(size - 1):
        total = total + dp_box[d].astype(F32)
    slim = chunk // streams
    for z in range(streams):
        chunk_wire[z] = total[z * slim : (z + 1) * slim, :].astype(wire)
    z_copies = []
    for d, peer in enumerate(along_z, 1):
        copy = remote(
            chunk_wire.at[lax.rem(s + d, streams)], z_box.at[d - 1], z_send.at[d], z_recv.at[d], peer
        )
        copy.start()
        z_copies.append(copy)
    for copy in small_copies:
        copy.wait_recv()
    small_total = small_send[0]
    for d in range(size - 1):
        small_total = small_total + small_dp[d]
    small_send[1] = small_total
    small_z_copies = []
    for d, peer in enumerate(along_z, 1):
        at = size + d
        copy = remote(small_send.at[1], small_z.at[d - 1], ss.at[at], sr.at[at], peer)
        copy.start()
        small_z_copies.append(copy)

    for copy in z_copies:
        copy.wait_recv()
    total = chunk_wire[s].astype(F32)
    for d in range(streams - 1):
        total = total + z_box[d].astype(F32)
    piece[...] = total.astype(wire)
    zg_copies = []
    keep = pltpu.make_async_copy(piece, late_ref.at[r, here, s], local_sems.at[1])
    keep.start()
    for d, peer in enumerate(along_z, 1):
        copy = remote(piece, late_ref.at[r, here, s], zg_send.at[d], zg_recv.at[d], peer)
        copy.start()
        zg_copies.append(copy)
    for copy in small_z_copies:
        copy.wait_recv()
    small_total = small_send[1]
    for d in range(streams - 1):
        small_total = small_total + small_z[d]
    small_send[2] = small_total
    small_c_copies = []
    for j, peer in enumerate(cores, 1):
        at = size + streams + j
        copy = remote(small_send.at[2], small_core.at[j - 1], ss.at[at], sr.at[at], peer)
        copy.start()
        small_c_copies.append(copy)

    keep.wait()
    for copy in zg_copies:
        copy.wait_recv()
    dpg_copies = []
    for d, peer in enumerate(along_dp, 1):
        copy = remote(
            late_ref.at[r, here], late_ref.at[r, here], dpg_send.at[d], dpg_recv.at[d], peer
        )
        copy.start()
        dpg_copies.append(copy)
    for copy in small_c_copies:
        copy.wait_recv()
    small_total = small_send[2]
    for j in range(groups - 1):
        small_total = small_total + small_core[j]
    sum_ref[...] = small_total
    for copy in dpg_copies:
        copy.wait_recv()
    cg_copies = []
    for j, peer in enumerate(cores, 1):
        copy = remote(late_ref.at[r], late_ref.at[r], cg_send.at[j], cg_recv.at[j], peer)
        copy.start()
        cg_copies.append(copy)
    for copy in cg_copies:
        copy.wait()
    for copy in back_copies:
        copy.wait()
    for copy in (
        core_copies
        + dp_copies
        + z_copies
        + zg_copies
        + dpg_copies
        + small_copies
        + small_z_copies
        + small_c_copies
    ):
        copy.wait_send()


def finish(streams, groups, d_queries, d_keys, d_values, active, bin_own, d_one, tokens, small, cid):
    seq, width = d_queries.shape
    rows, depth = d_one.shape
    size = lax.axis_size("dp")
    chunk = depth // size
    slim = chunk // streams
    wire = BF if slim % 16 == 0 else F32
    wide = 3 * width
    vmem = pl.BlockSpec(memory_space=pltpu.VMEM)
    any_space = pl.BlockSpec(memory_space=pl.ANY)
    small_shape = small.shape
    return pl.pallas_call(
        functools.partial(finish_kernel, streams, groups, wire),
        in_specs=[vmem] * 6 + [any_space, vmem],
        out_specs=[any_space, any_space, vmem],
        out_shape=[
            jax.ShapeDtypeStruct((streams, rows // streams, depth), BF),
            jax.ShapeDtypeStruct((groups, size, streams, slim, wide), wire),
            jax.ShapeDtypeStruct(small_shape, F32),
        ],
        scratch_shapes=[
            pltpu.VMEM((rows, depth), F32),
            pltpu.VMEM((groups - 1, rows, depth), BF),
            pltpu.VMEM((groups - 1, rows, depth), BF),
            pltpu.VMEM((streams, rows // streams, depth), BF),
            pltpu.VMEM((streams, rows // streams, depth), BF),
            pltpu.VMEM((depth, wide), F32),
            pltpu.VMEM((size, chunk, wide), wire),
            pltpu.VMEM((size - 1, chunk, wide), wire),
            pltpu.VMEM((streams, slim, wide), wire),
            pltpu.VMEM((streams - 1, slim, wide), wire),
            pltpu.VMEM((slim, wide), wire),
            pltpu.VMEM((3,) + small_shape, F32),
            pltpu.VMEM((size - 1,) + small_shape, F32),
            pltpu.VMEM((streams - 1,) + small_shape, F32),
            pltpu.VMEM((groups - 1,) + small_shape, F32),
            pltpu.SemaphoreType.DMA,
            dma(groups),
            dma(groups),
            dma(streams),
            dma(streams),
            dma(size),
            dma(size),
            dma(streams),
            dma(streams),
            dma(streams),
            dma(streams),
            dma(size),
            dma(size),
            dma(groups),
            dma(groups),
            dma(size + streams + groups),
            dma(size + streams + groups),
            dma(2),
        ],
        compiler_params=remote_params(cid),
        name="finish",
    )(d_queries, d_keys, d_values, active, bin_own, d_one, tokens, small)


def latent_columns(latent, binary_grad):
    matrix = latent.astype(F32)
    grad = binary_grad.astype(F32)
    scale = jnp.sqrt(jnp.mean(matrix * matrix, axis=0, keepdims=True) + 1e-06)
    inner = matrix * (2.0 / scale)
    bent = jnp.tanh(inner)
    slope = 1.0 - bent * bent
    through_scale = jnp.sum(grad * (bent - inner * slope), axis=0, keepdims=True)
    factor = through_scale / (matrix.shape[0] * scale)
    return 2.0 * grad * slope + matrix * factor


def early_latents_kernel(lo, lu, ld, go, gu, gd, oo, ou, od):
    oo[...] = latent_columns(lo[...], go[...])
    ou[...] = latent_columns(lu[...], gu[...])
    od[...] = latent_columns(ld[...], gd[...])


def early_latents(latents, grads):
    steps = 4
    specs = [
        pl.BlockSpec((a.shape[0], a.shape[1] // steps), lambda i: (0, i)) for a in latents
    ]
    return pl.pallas_call(
        early_latents_kernel,
        grid=(steps,),
        in_specs=specs * 2,
        out_specs=specs,
        out_shape=[jax.ShapeDtypeStruct(a.shape, F32) for a in latents],
        compiler_params=pltpu.CompilerParams(vmem_limit_bytes=VMEM_BYTES),
        name="early_latents",
    )(*latents, *grads)


def late_latents_kernel(latent, grad, out):
    out[0] = latent_columns(latent[0], grad[0])


def late_latents(latent, grads):
    groups, depth, wide = grads.shape
    width = wide // 3
    spec = pl.BlockSpec((1, depth, width), lambda m, j: (m, 0, j))
    return pl.pallas_call(
        late_latents_kernel,
        grid=(3, groups),
        in_specs=[spec, pl.BlockSpec((1, depth, width), lambda m, j: (j, 0, m))],
        out_specs=spec,
        out_shape=jax.ShapeDtypeStruct(latent.shape, F32),
        compiler_params=pltpu.CompilerParams(vmem_limit_bytes=VMEM_BYTES),
        name="late_latents",
    )(latent, grads)


def shards(
    tokens,
    teacher_tokens,
    segment_ids,
    cotangent,
    latent_qkv,
    latent_out,
    latent_up,
    latent_down,
    student_gain,
    student_bias,
    student_up_bias,
    teacher_qkv,
    teacher_out,
    teacher_up,
    teacher_down,
    teacher_gain,
    teacher_bias,
    teacher_up_bias,
):
    streams, shard_len, depth = tokens.shape
    blocks = lax.axis_size("blk")
    groups = blocks // streams
    seq = shard_len * blocks
    rows = seq // groups
    width = depth // groups
    s, r = place(groups)
    block = (shard_len, depth)
    gather, swap = Gather(streams, groups, block, BF), Swap(streams, groups, block, BF)
    row_block = (rows, width)
    by_rows = Rows(streams, groups, row_block, BF)
    doc_block = (shard_len // 128, 128)

    def own_columns(matrices):
        return lax.dynamic_slice_in_dim(matrices, r * width, width, axis=2)

    def own_bias(bias):
        return lax.dynamic_slice_in_dim(bias, r * width, width, axis=1)

    latents = [own_columns(latent_qkv), latent_out, latent_up, latent_down]
    taken = [
        tokens,
        segment_ids.reshape((streams,) + doc_block),
        teacher_qkv,
        teacher_out,
    ]
    bin_own, bin_out, bin_up, bin_down, token_blocks, docs, qkv_parts, out_parts = intake(
        Moves(
            gather,
            Gather(streams, groups, doc_block, jnp.int32),
            Spread(teacher_qkv.shape, BF),
            Spread(teacher_out.shape, BF),
        ),
        latents,
        taken,
        1,
    )
    docs = docs.reshape(seq)
    big = docs[streams * shard_len] if groups > 1 else docs[shard_len]
    in_big = docs == big
    stream_tokens = token_blocks.reshape(seq, depth)

    def project(rows_in, matrices, bias):
        q = dot(rows_in, matrices[0]) + own_bias(bias)[0]
        k = dot(rows_in, matrices[1])
        v = dot(rows_in, matrices[2]) + own_bias(bias)[1]
        return jnp.concatenate(
            [(q.astype(BF).astype(F32) * 0.125).astype(BF), k.astype(BF), v.astype(BF)], axis=1
        )

    active = squash(stream_tokens.astype(F32)).astype(BF)
    qkv = project(active, bin_own, student_bias)
    numerators, context, inverse, teacher_blocks, up_parts = attention(
        qkv,
        docs,
        Moves(gather, Spread(teacher_up.shape, BF)),
        [teacher_tokens, teacher_up],
        True,
        2,
        "attention_student",
    )
    teacher_stream = teacher_blocks.reshape(seq, depth)
    full_qkv = own_columns(qkv_parts.transpose(1, 0, 2, 3).reshape(3, depth, depth))
    teacher_own = project(teacher_stream, full_qkv, teacher_bias)
    row_shape = (groups,) + row_block
    teacher_context, cot_blocks, down_parts, ctx_rows = attention(
        teacher_own,
        docs,
        Moves(swap, Spread(teacher_down.shape, BF), by_rows),
        [cotangent, teacher_down, context.reshape(row_shape)],
        False,
        3,
        "attention_teacher",
    )
    (tctx_rows,) = move(
        Moves(by_rows), [teacher_context.reshape(row_shape)], 4, "teacher_context_rows"
    )
    output, d_one, d_context, g_out, g_up, g_down, g_gain, g_bias, g_ub = middle(
        r,
        stream_tokens,
        teacher_stream,
        cot_blocks.reshape(rows, depth),
        ctx_rows,
        tctx_rows,
        [bin_out, bin_up, bin_down],
        [
            out_parts.reshape(-1, depth),
            up_parts.reshape(depth, -1),
            down_parts.reshape(-1, depth),
        ],
        [
            student_gain,
            student_bias,
            student_up_bias.reshape(1, -1),
            teacher_gain,
            teacher_bias,
            teacher_up_bias.reshape(1, -1),
        ],
    )
    early = lax.psum((g_out.astype(BF), g_up.astype(BF), g_down.astype(BF)), ("dp", "blk"))
    small = jnp.concatenate(
        [g_gain, g_bias, g_ub.reshape(-1, depth), jnp.zeros((4, depth), F32)], axis=0
    )
    (d_ctx_rows,) = move(Moves(by_rows), [d_context], 5, "d_context_rows")
    d_queries, d_keys, d_values, output_blocks = attention_back(
        numerators,
        qkv,
        teacher_own,
        d_ctx_rows.reshape(seq, width),
        context,
        inverse,
        docs,
        in_big,
        Moves(swap),
        [output.reshape(streams, shard_len, depth)],
        6,
    )
    grad_tokens, late, small = finish(
        streams, groups, d_queries, d_keys, d_values, active, bin_own, d_one, token_blocks, small, 7
    )
    up_rows = latent_up.shape[1] // depth
    grad_out, grad_up, grad_down = early_latents([latent_out, latent_up, latent_down], early)
    return (
        output_blocks,
        grad_tokens,
        late_latents(latent_qkv, late.reshape(groups, depth, 3 * width)),
        grad_out,
        grad_up,
        grad_down,
        small[0:2],
        small[2:8],
        small[8 : 8 + up_rows].reshape(-1),
    )


def solution(mesh):
    return jax.shard_map(
        shards,
        mesh=mesh,
        in_specs=(
            P("dp", "blk", None),
            P("dp", "blk", None),
            P("dp", "blk"),
            P("dp", "blk", None),
            P(),
            P(),
            P(),
            P(),
            P(),
            P(),
            P(),
            P(None, "dp", None),
            P("dp", None),
            P("dp", None),
            P("dp", None),
            P(),
            P(),
            P(),
        ),
        out_specs=(P("dp", "blk", None), P("dp", "blk", None), P(), P(), P(), P(), P(), P(), P()),
        check_vma=False,
    )
```

time: 544 us -> 406 us (0.75)
  blocking collectives: 85.3 us -> 0 us
  other arithmetic: 48.5 us -> 17.8 us
  local copies, waits for them, and re-layouts: 27.2 us -> 15.6 us
  Pallas kernels: 303 us -> 297 us
  matrix products: 16.5 us -> 11 us
    psum x1 -> x0, blocking collectives: 46.5 us -> none  [shards(): lax.psum((g_gain, g_bias, g_ub), ('dp', 'blk'))]
    all_gather x2 -> x0, blocking collectives: 38.8 us -> none  [the longest x1 22.9 us: shards(): full_out = lax.all_gather(teacher_out, 'dp', axis=0, tiled=True)]
    reduce_sum x12 -> x0, other arithmetic: 16.3 us -> none  [the longest x4 7.66 us: binarize(): return column_scale * jnp.tanh(2.0 * matrix / column_scale)]
    add_any x4 -> x0, other arithmetic: 11.5 us -> none  [binarize(): matrix * matrix]
    convert_element_type x5 -> x0, other arithmetic: 8.64 us -> none  [the longest x1 2.1 us: shards(): bin_up = binarize(latent_up.astype(F32)).astype(BF)]
    unnamed x61 -> x36, local copies, waits for them, and re-layouts: 10.2 us -> 4.07 us
    pallas_call x9 -> x10, Pallas kernels: 303 us -> 297 us  [the longest x2 83.9 us: attention(): pl.pallas_call(functools.partial(forward_kernel, moves, keep, tile, edge)...]
    dot_general x4 -> x6, matrix products: 16.5 us -> 11 us  [dot(): return lax.dot_general(a, b, dims, preferred_element_type=F32)]
  transfers between devices with their start and end apart: 4 -> 1, of which waited for: 1 -> 1; matrix products, arithmetic and copies ran while one was open for 9% -> 3% of each run, Pallas kernels for 36% -> 31%
where the time goes in v2:
time: 406 us; the launch traced here: 400 us
  Pallas kernels  297 us (73%)
  waiting for transfers between devices  43.8 us (11%)
  other arithmetic  17.8 us (4%)
  local copies, waits for them, and re-layouts  15.6 us (4%)
  between operations  14.5 us (4%)
  matrix products  11 us (3%)
    pallas_call x2, Pallas kernels, attention(): pl.pallas_call(functools.partial(forward_kernel, moves, keep, tile, edge)...  83.9 us
    pallas_call x1, Pallas kernels, finish(): pl.pallas_call(functools.partial(finish_kernel, streams, groups, wire), i...  63.2 us
    pallas_call x1, Pallas kernels, attention_back(): pl.pallas_call(functools.partial(backward_kernel, moves, tile), grid=(pai...  50.1 us
    psum x1, waiting for transfers between devices, shards(): lax.psum((g_out.astype(BF), g_up.astype(BF), g_down.astype(BF)), ('dp', '...  43.8 us
    pallas_call x1, Pallas kernels, middle(): pl.pallas_call(middle_kernel, grid_spec=pltpu.PrefetchScalarGridSpec(num_...  38.7 us
    pallas_call x1, Pallas kernels, intake(): pl.pallas_call(functools.partial(intake_kernel, moves), out_shape=[jax.Sh...  38.1 us
    pallas_call x1, Pallas kernels, early_latents(): pl.pallas_call(early_latents_kernel, grid=(steps,), in_specs=specs * 2, o...  12.1 us
    dot_general x6, matrix products, dot(): return lax.dot_general(a, b, dims, preferred_element_type=F32)  11 us
  transfers between devices with their start and end apart: 1, of which 1 were waited for; matrix products, arithmetic and copies ran while one was open for 3% of the time, Pallas kernels for 31%

profile of v2, /device:TPU:0, one launch (start us, length us, event | category | flops | bytes accessed | tf_op | source)
XLA Modules:
  0.0 399.7 jit_solution(13762228165618877746)
XLA Ops:
  7.2 0.0 all-reduce.3.cloned.1.call-start
  7.2 1.3 reshape.92.refs_1_
  8.5 2.1 constant_dynamic-slice_fusion.2.qkv_ref
  10.6 38.1 %intake.1 = (bf16[3,512,256]{2,1,0:T(8,128)(2,1)}, bf16[512,512]{1,0:T(8,128)(2,1)}, bf16[512,2048]{1,0:T(8,128)(2,1)}, bf16[2048,512]{1,0:T(8,128)(2,1)}, bf16[...) custom-call(bf16[3,512,256]{2,1,0:T(8,128)(2,1)} %constant_dynamic-s, ...), custom_call_target="tpu_custom_call" | custom-call | tf_op jit(solution)/shard_map/intake/pallas_call | solution.py:367
  48.7 2.3 multiply_convert_fusion.1
  51.0 0.0 copy-start.11
  51.0 1.7 convolution_convert_fusion.1
  52.7 0.9 constant_dynamic-slice_fusion
  53.6 0.0 copy-done.11
  53.6 1.7 fusion.9
  55.3 1.7 fusion.1
  56.9 0.0 copy-done.12
  56.9 1.3 copy.47.col_ref
  58.3 1.5 copy.48
  59.8 0.0 copy-done.9
  59.8 0.0 copy-done.10
  59.8 0.0 copy-start.4
  59.8 2.2 pad_maximum_fusion.q_ref.k_ref.v_ref
  62.0 44.2 %attention_student.1 = (bf16[4,2048,2048]{2,1,0:T(8,128)(2,1)}, bf16[2048,256]{1,0:T(8,128)(2,1)}, f32[2048,256]{1,0:T(8,128)}, bf16[8,256,512]{2,1,0:T(8,128)(2,1)}, bf16[4,128,2048]{2,1,0:T(8,128)(2,1)}) custom-call(bf16[2048,768]{1,0:T(8,128)(2,1)} %pad_maximum_fusion.q_ref.k_ref.v_ref, bf16[2048,768]{1,0:T(8,128)(2,1)} %pad_maximum_fusion.q_ref.k_ref.v_ref, ...), custom_call_target="tpu_custom_call" | custom-call | tf_op jit(solution)/shard_map/attention_student/pallas_call | solution.py:481
  106.2 0.0 copy-start.2
  106.2 2.5 convolution_convert_fusion
  108.7 0.0 copy-done.4
  108.7 0.0 copy-done.2
  108.7 1.7 fusion.6
  110.4 1.7 fusion.3
  112.1 0.0 copy-done.8
  112.1 1.8 pad_maximum_fusion.1.q_ref.k_ref.v_ref.tq_ref.tk_ref
  113.9 39.7 %attention_teacher.1 = (bf16[2048,256]{1,0:T(8,128)(2,1)}, bf16[4,256,512]{2,1,0:T(8,128)(2,1)}, bf16[4,512,512]{2,1,0:T(8,128)(2,1)}, bf16[2,1024,256]{2,1,0:T(8,128)(2,1)}) custom-call(bf16[2048,768]{1,0:T(8,128)(2,1)} %pad_maximum_fusion.1.q_ref.k_ref.v_ref.tq_ref.tk_ref, bf16[2048,768]{1,0:T(8,128)(2,1)} %pad_maximum_fusion.1.q_ref.k_ref.v_ref.tq_ref.tk_ref, ...), custom_call_target="tpu_custom_call" | custom-call | tf_op jit(solution)/shard_map/attention_teacher/pallas_call | solution.py:481
  153.6 2.3 teacher_context_rows.1.tctx_ref
  156.0 38.7 %middle.1 = (bf16[1024,512]{1,0:T(8,128)(2,1)}, f32[1024,512]{1,0:T(8,128)}, bf16[2,1024,256]{2,1,0:T(8,128)(2,1)}, f32[512,512]{1,0:T(8,128)}, f32[512,2048]{1,...) custom-call(s32[1]{0:T(128)} %bitcast.16.unused_place, ...), custom_call_target="tpu_custom_call" | custom-call | tf_op jit(solution)/shard_map/middle/pallas_call | solution.py:809
  194.7 0.0 copy-start.3
  194.7 4.0 convert_element_type.81
  198.7 0.0 copy-done.3
  198.7 1.6 convert_element_type.82
  200.3 0.0 copy-done.5
  200.3 0.9 convert_element_type.80
  201.2 0.0 all-reduce.3.cloned.1.call-update
  201.2 0.0 copy-start.1
  201.2 0.5 broadcast.25
  201.7 0.1 copy-done.14
  201.9 0.7 reduce.3
  202.5 2.3 d_context_rows.1
  204.9 1.2 slice.56
  206.1 0.1 pad.3.clone
  206.1 0.0 copy-done.1
  206.2 1.7 compare_convert_fusion.bigc_ref
  207.8 50.1 %attention_back.1 = (bf16[2048,256]{1,0:T(8,128)(2,1)}, bf16[2048,256]{1,0:T(8,128)(2,1)}, bf16[2048,256]{1,0:T(8,128)(2,1)}, bf16[4,256,512]{2,1,0:T(8,128)(2,1)}) custom-call(bf16[4,2048,2048]{2,1,0:T(8,128)(2,1)} %get-tuple-element.48.e_ref, bf16[2048,768]{1,0:T(8,128)(2,1)} %pad_maximum_fusion.q_ref.k_ref.v_ref, ...), custom_call_target="tpu_custom_call" | custom-call | tf_op jit(solution)/shard_map/attention_back/pallas_call | solution.py:642
  257.9 0.0 copy-done.13
  258.0 0.0 copy-done.15
  258.0 0.7 maximum_maximum_fusion.small_ref
  258.7 0.0 copy-done
  258.7 2.1 multiply_convert_fusion.active_ref
  260.8 63.2 %finish.1 = (bf16[4,256,512]{2,1,0:T(8,128)(2,1)}, bf16[2,4,4,32,768]{4,3,2,1,0:T(8,128)(2,1)}, f32[16,512]{1,0:T(8,128)}) custom-call(bf16[2048,256]{1,0:T(8,128)(2,1)} %get-tuple-element.65.dq_ref, bf16[2048,256]{1,0:T(8,128)(2,1)} %get-tuple-element.66.dk_ref, bf16[2048,256]{1,0:T(8,128)(2,1)} %get-tuple-element.67.dv_ref, ...), custom_call_target="tpu_custom_call" | custom-call | tf_op jit(solution)/shard_map/finish/pallas_call | solution.py:1066
  324.0 1.3 slice.54
  325.3 1.3 slice.53
  326.6 6.3 %late_latents.1 = f32[3,512,512]{2,1,0:T(8,128)} custom-call(bf16[3,512,512]{2,1,0:T(8,128)(2,1)} %latent.1, bf16[2,512,768]{2,1,0:T(8,128)(2,1)} %bitcast.69), custom_call_target="tpu_custom_call" | custom-call | tf_op jit(solution)/shard_map/late_latents/pallas_call | solution.py:1157
  332.9 0.7 slice_bitcast_fusion
  333.6 0.6 copy.62
  334.3 43.8 %all-reduce.3.cloned.1.call-done = (bf16[512,512]{1,0:T(8,128)(2,1)}, bf16[512,2048]{1,0:T(8,128)(2,1)}, bf16[2048,512]{1,0:T(8,128)(2,1)}) async-done(((bf16[512,512]{1,0:T(8,128)(2,1)}, bf16[512,2048]{1,0:T(8,128)(2,1)}, bf16[2048,512]{1,0:T(8,128)(2,1)}), (bf16[512,512]{1,0:T(8,128)(2,1)}, bf16[512,2048]{1,0:T(8,128)(2,1)}, bf16[2048,512]{1,0:T(8,128)(2,1)})) %all-reduce.3.cloned.1.call-update) | async-done | bytes 4718608 | tf_op jit(solution)/shard_map/psum | solution.py:1287
  378.1 12.1 %early_latents.1 = (f32[512,512]{1,0:T(8,128)}, f32[512,2048]{1,0:T(8,128)}, f32[2048,512]{1,0:T(8,128)}) custom-call(bf16[512,512]{1,0:T(8,128)(2,1)} %lo.1, bf16[512,2048]{1,0:T(8,128)(2,1)} %lu.1, bf16[2048,512]{1,0:T(8,128)(2,1)} %ld.1, bf16[512,512]{1,0:T(8,128)(2,1)} %get-tuple-element.81.go, bf16[512,2048]{1,0:T(8,128)(2,1)} %get-tuple-element.82.gu, ...), custom_call_target="tpu_custom_call" | custom-call | tf_op jit(solution)/shard_map/early_latents/pallas_call | solution.py:1138
  390.1 0.0 copy-done.6
  390.1 1.0 copy.68
  391.1 0.6 copy-done.7
  391.7 1.0 copy.69
  (13 shorter events, 0.0 us)
Async XLA Ops:
  7.2 370.9 %all-reduce.3.cloned.1.call-start = ((), (), s32[]{:S(2)}) async-start(), calls=%async_computation | async-start | bytes 9437184 | tf_op jit(solution)/shard_map/psum | solution.py:1287
  51.0 2.6 copy-start.11
  55.3 1.7 copy-start.12
  56.9 2.9 copy-start.9
  56.9 2.9 copy-start.10
  59.8 48.8 %copy-start.4 = (bf16[3,4,128,512]{3,2,1,0:T(8,128)(2,1)}, bf16[3,4,128,512]{3,2,1,0:T(8,128)(2,1)S(1)}, u32[]{:S(2)}) copy-start(bf16[3,4,128,512]{3,2,1,0:T(8,128)(2,1)S(1)} %copy.48) | copy-start | bytes 4718596
  106.2 2.5 copy-start.2
  110.4 1.8 copy-start.8
  194.7 4.0 copy-start.3
  198.7 1.6 copy-start.5
  201.2 0.7 copy-start.14
  201.2 5.0 %copy-start.1 = (s32[2048,1]{1,0:T(8,128)S(1)}, s32[2048,1]{1,0:T(8,128)}, u32[]{:S(2)}) copy-start(s32[2048,1]{1,0:T(8,128)} %copy.47.col_ref) | copy-start | bytes 24580
  207.8 50.1 %copy-start.13 = (f32[6,512]{1,0:T(8,128)S(1)}, f32[6,512]{1,0:T(8,128)}, u32[]{:S(2)}) copy-start(f32[6,512]{1,0:T(8,128)} %get-tuple-element.70) | copy-start | bytes 36868
  207.8 50.1 %copy-start.15 = (f32[2,512]{1,0:T(2,128)S(1)}, f32[2,512]{1,0:T(2,128)}, u32[]{:S(2)}) copy-start(f32[2,512]{1,0:T(2,128)} %get-tuple-element.69) | copy-start | bytes 12292
  207.8 50.8 %copy-start = (bf16[8,256,512]{2,1,0:T(8,128)(2,1)S(1)}, bf16[8,256,512]{2,1,0:T(8,128)(2,1)}, u32[]{:S(2)}) copy-start(bf16[8,256,512]{2,1,0:T(8,128)(2,1)} %get-tuple-element.45.tokens_ref) | copy-start | bytes 6291460
  378.1 12.1 %copy-start.6 = (bf16[4,256,512]{2,1,0:T(8,128)(2,1)S(1)}, bf16[4,256,512]{2,1,0:T(8,128)(2,1)}, u32[]{:S(2)}) copy-start(bf16[4,256,512]{2,1,0:T(8,128)(2,1)} %get-tuple-element.99) | copy-start | bytes 3145732
  390.1 1.6 copy-start.7
Sparse Core Ops, SparseCore 0:
  201.3 176.7 all-reduce.2

commit v3 on v2

--- a/solution.py
+++ b/solution.py
@@ -282,6 +282,177 @@
 
     first = Swap.first
     last = Swap.last
+
+
+class Bag:
+    def __init__(self):
+        self.items = {}
+
+    def add(self, name, item):
+        self.items[name] = item
+
+    def bind(self, refs):
+        return dict(zip(self.items, refs))
+
+
+class Reduce:
+    def __init__(self, bag, name, streams, groups, shapes, over_cores):
+        self.name, self.streams, self.groups = name, streams, groups
+        self.size = lax.axis_size("dp")
+        self.over_cores = over_cores
+        self.count = len(shapes)
+        share = self.size * (groups if over_cores else 1)
+        self.shapes = [(rows // share, cols) for rows, cols in shapes]
+        self.wires = [BF if (c // streams) % 16 == 0 else F32 for c, cols in self.shapes]
+        for i, (chunk, cols) in enumerate(self.shapes):
+            wire, slim = self.wires[i], chunk // streams
+            bag.add(f"{name}half{i}", pltpu.VMEM((self.size, chunk, cols), wire))
+            if over_cores:
+                bag.add(f"{name}core{i}", pltpu.VMEM((groups - 1, self.size, chunk, cols), wire))
+            bag.add(f"{name}dp{i}", pltpu.VMEM((self.size - 1, chunk, cols), wire))
+            bag.add(f"{name}cut{i}", pltpu.VMEM((streams, slim, cols), wire))
+            bag.add(f"{name}z{i}", pltpu.VMEM((streams - 1, slim, cols), wire))
+            bag.add(f"{name}fin{i}", pltpu.VMEM((slim, cols), wire))
+            for kind, n in self.sem_counts().items():
+                bag.add(f"{name}{kind}s{i}", dma(n))
+                bag.add(f"{name}{kind}r{i}", dma(n))
+            bag.add(f"{name}local{i}", dma(2))
+
+    def sem_counts(self):
+        b, g, d = self.streams, self.groups, self.size
+        return {"a": g, "b": d, "c": b, "d": b, "e": d, "f": g}
+
+    def out_shapes(self):
+        return [
+            jax.ShapeDtypeStruct(
+                (self.groups, self.size, self.streams, chunk // self.streams, cols), wire
+            )
+            for (chunk, cols), wire in zip(self.shapes, self.wires)
+        ]
+
+    def bind(self, sources, targets, scratch):
+        self.sources, self.targets, self.scratch = sources, targets, scratch
+
+    def get(self, what, i):
+        return self.scratch[f"{self.name}{what}{i}"]
+
+    def copies(self, kind, i):
+        s, r = place(self.groups)
+        here = lax.axis_index("dp")
+        b, g, size = self.streams, self.groups, self.size
+        send, recv = self.get(kind + "s", i), self.get(kind + "r", i)
+        if kind in "af":
+            peers = core_peers(g)
+        elif kind in "be":
+            peers = dp_peers()
+        else:
+            peers = stream_peers(b, g)
+        order = list(enumerate(peers, 1))
+        if kind in "cd" and b == 4:
+            order = [order[1], order[0], order[2]]
+        for d, peer in order:
+            if kind == "a":
+                pair = self.sources[i].at[lax.rem(r + d, g)], self.get("core", i).at[d - 1]
+            elif kind == "b":
+                pair = self.get("half", i).at[lax.rem(here + d, size)], self.get("dp", i).at[d - 1]
+            elif kind == "c":
+                pair = self.get("cut", i).at[lax.rem(s + d, b)], self.get("z", i).at[d - 1]
+            elif kind == "d":
+                pair = self.get("fin", i), self.targets[i].at[r, here, s]
+            elif kind == "e":
+                pair = self.targets[i].at[r, here], self.targets[i].at[r, here]
+            else:
+                pair = self.targets[i].at[r], self.targets[i].at[r]
+            yield remote(*pair, send.at[d], recv.at[d], peer)
+
+    def start(self, kind, i):
+        for copy in self.copies(kind, i):
+            copy.start()
+
+    def arrive(self, kind, i):
+        for copy in self.copies(kind, i):
+            copy.wait_recv()
+
+    def load(self, i):
+        s, r = place(self.groups)
+        return pltpu.make_async_copy(
+            self.sources[i].at[r], self.get("half", i), self.get("local", i).at[0]
+        )
+
+    def keep(self, i):
+        s, r = place(self.groups)
+        return pltpu.make_async_copy(
+            self.get("fin", i),
+            self.targets[i].at[r, lax.axis_index("dp"), s],
+            self.get("local", i).at[1],
+        )
+
+    def core_start(self):
+        for i in range(self.count):
+            self.start("a", i)
+            self.load(i).start()
+
+    def dp_start(self):
+        for i in range(self.count):
+            if self.over_cores:
+                self.load(i).wait()
+                self.arrive("a", i)
+                half, box, wire = self.get("half", i), self.get("core", i), self.wires[i]
+                for p in range(self.size):
+                    total = half[p].astype(F32)
+                    for j in range(self.groups - 1):
+                        total = total + box[j, p].astype(F32)
+                    half[p] = total.astype(wire)
+            self.start("b", i)
+
+    def z_start(self):
+        here = lax.axis_index("dp")
+        for i in range(self.count):
+            self.arrive("b", i)
+            half, box, cut, wire = (
+                self.get("half", i),
+                self.get("dp", i),
+                self.get("cut", i),
+                self.wires[i],
+            )
+            slim = self.shapes[i][0] // self.streams
+            for z in range(self.streams):
+                at = slice(z * slim, (z + 1) * slim)
+                total = half[here, at, :].astype(F32)
+                for d in range(self.size - 1):
+                    total = total + box[d, at, :].astype(F32)
+                cut[z] = total.astype(wire)
+            self.start("c", i)
+
+    def z_back(self):
+        s, r = place(self.groups)
+        for i in range(self.count):
+            self.arrive("c", i)
+            box = self.get("z", i)
+            total = self.get("cut", i)[s].astype(F32)
+            for d in range(self.streams - 1):
+                total = total + box[d].astype(F32)
+            self.get("fin", i)[...] = total.astype(self.wires[i])
+            self.keep(i).start()
+            self.start("d", i)
+
+    def dp_back(self):
+        for i in range(self.count):
+            self.keep(i).wait()
+            self.arrive("d", i)
+            self.start("e", i)
+
+    def core_back(self):
+        for i in range(self.count):
+            self.arrive("e", i)
+            self.start("f", i)
+
+    def end(self):
+        for i in range(self.count):
+            self.arrive("f", i)
+            for kind in "abcdef" if self.over_cores else "bcdef":
+                for copy in self.copies(kind, i):
+                    copy.wait_send()
 
 
 class Moves:
@@ -497,8 +668,13 @@
 
 
 def backward_kernel(
-    moves,
+    streams,
+    groups,
     tile,
+    bag,
+    back,
+    early,
+    late,
     e_ref,
     q_ref,
     k_ref,
@@ -511,19 +687,76 @@
     col_ref,
     row_ref,
     bigc_ref,
+    small_ref,
+    active_hbm,
+    bin_hbm,
+    d1_hbm,
+    tokens_hbm,
+    output_ref,
     *rest,
 ):
-    count = len(moves.jobs)
-    sources, (dq_ref, dk_ref, dv_ref, *rest) = rest[:count], rest[count:]
-    targets, (v_aug, dk_acc, dv_acc, grams, *scratch) = rest[:count], rest[count:]
+    n_early = sum(job.count for job in early)
+    sources, rest = rest[:n_early], rest[n_early:]
+    output_back, grad_ref, *rest = rest
+    early_out, rest = rest[:n_early], rest[n_early:]
+    late_out, (sum_ref, *rest) = rest[: len(late)], rest[len(late) :]
+    have = bag.bind(rest)
+    at = 0
+    for job in early:
+        job.bind(sources[at : at + job.count], early_out[at : at + job.count], have)
+        at += job.count
+    for job, target in zip(late, late_out):
+        job.bind(None, [target], have)
+    back_refs = (output_ref, output_back) + tuple(have[f"back{i}"] for i in range(4))
+
     pair, step = pl.program_id(0), pl.program_id(1)
-    steps = pl.num_programs(1)
+    pairs, steps = len(late), q_ref.shape[0] // tile
     seq = k_ref.shape[0]
     share = 1.0 / seq
-
-    @pl.when((pair == 0) & (step == 0))
-    def _():
-        moves.first(sources, targets, scratch)
+    time = pair * steps + step
+    total_time = pairs * steps
+    size = lax.axis_size("dp")
+    here = lax.axis_index("dp")
+    s, r = place(groups)
+    rows, depth = d1_hbm.shape
+    width = pairs * 128
+    v_aug, dk_acc, dv_acc, grams = have["v_aug"], have["dk_acc"], have["dv_acc"], have["grams"]
+    dq_all, d_act, active, weights = have["dq_all"], have["d_act"], have["active"], have["weights"]
+    d_one, x_rows = have["d_one"], have["x_rows"]
+    along_z, cores, along_dp = stream_peers(streams, groups), core_peers(groups), dp_peers()
+
+    def loads():
+        sems = have["load"]
+        return [
+            pltpu.make_async_copy(active_hbm, active, sems.at[0]),
+            pltpu.make_async_copy(bin_hbm, weights, sems.at[1]),
+            pltpu.make_async_copy(d1_hbm, d_one, sems.at[2]),
+            pltpu.make_async_copy(tokens_hbm.at[pl.ds(r * streams, streams)], x_rows, sems.at[3]),
+        ]
+
+    def at_time(when, *work):
+        @pl.when(time == when)
+        def _():
+            for item in work:
+                item()
+
+    def begin():
+        greet(along_z + cores + along_dp)
+        back.first(*back_refs)
+        for job in early:
+            job.core_start()
+        for copy in loads():
+            copy.start()
+
+    at_time(0, begin)
+    unit = total_time / 16
+    for n, job in enumerate(early):
+        for when, work in zip(EARLY_TIMES[n], (job.dp_start, job.z_start, job.z_back, job.dp_back)):
+            at_time(int(when * unit), work)
+    for p, job in enumerate(late[:-1]):
+        first = (p + 1) * steps
+        for when, work in zip(LATE_TIMES, (job.dp_start, job.z_start, job.z_back, job.dp_back)):
+            at_time(first + when, work)
 
     @pl.when(step == 0)
     def _():
@@ -547,14 +780,14 @@
             grams[2 * i], grams[2 * i + 1] = split(gram)
 
     start = pl.multiple_of(step * tile, tile)
-    rows = pl.ds(start, tile)
+    rows_here = pl.ds(start, tile)
     lane = lanes_of((tile, 128))
     low = lane < 64
 
     def body(whole, columns):
-        in_big = bigc_ref[rows, :] > 0.0
-        q8 = q_ref[rows, :]
-        tq8 = tq_ref[rows, :]
+        in_big = bigc_ref[rows_here, :] > 0.0
+        q8 = q_ref[rows_here, :]
+        tq8 = tq_ref[rows_here, :]
         dc = dc_ref[...].astype(F32)
         inv = inv_ref[...]
         scaled = dc * inv
@@ -598,7 +831,7 @@
         qb = jnp.where(in_big, q8.astype(F32), 0.0).astype(BF)
         tqb = jnp.where(in_big, tq8.astype(F32), 0.0).astype(BF)
         d_query += dot(qb, grams[0]) + dot(qb, grams[1]) - dot(tqb, grams[2]) - dot(tqb, grams[3])
-        dq_ref[...] = (d_query * 0.125).astype(BF)
+        dq_all[rows_here, :] = (d_query * 0.125).astype(BF)
 
     @pl.when(step == 0)
     def _():
@@ -612,35 +845,232 @@
     def _():
         body(False, None)
 
-    @pl.when(step == steps - 1)
-    def _():
+    def pair_end(p):
+        job = late[p]
         in_big = bigc_ref[...] > 0.0
         kb = jnp.where(in_big, k_ref[...].astype(F32), 0.0).astype(BF)
         tkb = jnp.where(in_big, tk_ref[...].astype(F32), 0.0).astype(BF)
         d_key = dk_acc[...].T
         d_key += dot(kb, grams[4]) + dot(kb, grams[5]) - dot(tkb, grams[6]) - dot(tkb, grams[7])
-        dk_ref[...] = d_key.astype(BF)
-        dv_ref[...] = dv_acc[...].T.astype(BF)
-
-    @pl.when((pair == pl.num_programs(0) - 1) & (step == steps - 1))
+        d_value = dv_acc[...].T.astype(BF)
+        d_query = dq_all[...]
+        d_pair = jnp.concatenate([d_query, d_key.astype(BF), d_value], axis=1)
+        if p == 0:
+            for copy in loads():
+                copy.wait()
+        columns = slice(p * 128, (p + 1) * 128)
+        bins = jnp.concatenate([weights[i, :, columns] for i in range(3)], axis=1)
+        if p == 0:
+            d_act[...] = dot(d_pair, bins, NT)
+        else:
+            d_act[...] += dot(d_pair, bins, NT)
+        if p == pairs - 1:
+            for j in range(1, groups):
+                other = pl.multiple_of(lax.rem(r + j, groups) * rows, rows)
+                have["outbox"][j - 1] = d_act[pl.ds(other, rows), :].astype(BF)
+            for copy in core_copies():
+                copy.start()
+        partial = dot(active[...], d_pair, TN)
+        chunk = depth // size
+        half = job.get("half", 0)
+        for d in range(size):
+            half[d] = partial[d * chunk : (d + 1) * chunk, :].astype(job.wires[0])
+        sums = have["sums"]
+        sums[0:1, columns] = jnp.sum(d_query.astype(F32), axis=0, keepdims=True)
+        sums[1:2, columns] = jnp.sum(d_value.astype(F32), axis=0, keepdims=True)
+
+    def core_copies():
+        return [
+            remote(
+                have["outbox"].at[j - 1],
+                have["inbox"].at[j - 1],
+                have["core_s"].at[j],
+                have["core_r"].at[j],
+                cores[j - 1],
+            )
+            for j in range(1, groups)
+        ]
+
+    def small_copies(stage, peers, base):
+        return [
+            remote(
+                have["small"].at[stage],
+                have["small_box"].at[base + d],
+                have["small_s"].at[base + d],
+                have["small_r"].at[base + d],
+                peer,
+            )
+            for d, peer in enumerate(peers)
+        ]
+
+    def small_start(stage, peers, base):
+        for copy in small_copies(stage, peers, base):
+            copy.start()
+
+    def small_sum(stage, peers, base):
+        for copy in small_copies(stage, peers, base):
+            copy.wait_recv()
+        total = have["small"][stage]
+        for d in range(len(peers)):
+            total = total + have["small_box"][base + d]
+        return total
+
+    for p in range(pairs - 1):
+
+        @pl.when((pair == p) & (step == steps - 1))
+        def _():
+            pair_end(p)
+
+    @pl.when(time == total_time - 1)
     def _():
-        moves.last(sources, targets, scratch)
+        pair_end(pairs - 1)
+        last = late[-1]
+        last.dp_start()
+        small = have["small"]
+        small[0] = small_ref[...]
+        for i in range(2):
+            vector = have["sums"][i : i + 1, :]
+            small[0, 2 + i : 3 + i, :] = jnp.concatenate(
+                [jnp.where(r == j, vector, 0.0) for j in range(groups)], axis=1
+            )
+        small_start(0, along_dp, 0)
+        for copy in core_copies():
+            copy.wait_recv()
+        shard = rows // streams
+        back_copies = []
+        blocks = have["blocks"]
+        order = [2, 1, 3] if streams == 4 else list(range(1, streams))
+        for d in order + [0]:
+            target = lax.rem(s + d, streams)
+            here_rows = pl.ds(pl.multiple_of(target * shard, shard), shard)
+            bent = jnp.tanh(x_rows[target].astype(F32) * (1.0 / clip_level))
+            total = d_act[pl.ds(pl.multiple_of(r * rows + target * shard, shard), shard), :]
+            for j in range(groups - 1):
+                total = total + have["inbox"][j, here_rows, :].astype(F32)
+            blocks[target] = (d_one[here_rows, :] + total * (1.0 - bent * bent)).astype(BF)
+            if d:
+                copy = remote(
+                    blocks.at[target],
+                    grad_ref.at[s],
+                    have["grad_s"].at[d],
+                    have["grad_r"].at[d],
+                    along_z[d - 1],
+                )
+            else:
+                copy = pltpu.make_async_copy(blocks.at[s], grad_ref.at[s], have["grad_s"].at[0])
+            copy.start()
+            back_copies.append(copy)
+        for job in early[:1]:
+            job.core_back()
+        last.z_start()
+        small[1] = small_sum(0, along_dp, 0)
+        small_start(1, along_z, size)
+        for job in late[:-1]:
+            job.core_back()
+        last.z_back()
+        for job in early[1:]:
+            job.core_back()
+        small[2] = small_sum(1, along_z, size)
+        small_start(2, cores, size + streams)
+        last.dp_back()
+        sum_ref[...] = small_sum(2, cores, size + streams)
+        last.core_back()
+        back.last(*back_refs)
+        for copy in back_copies:
+            copy.wait()
+        for job in early + late:
+            job.end()
+        for copy in (
+            core_copies()
+            + small_copies(0, along_dp, 0)
+            + small_copies(1, along_z, size)
+            + small_copies(2, cores, size + streams)
+        ):
+            copy.wait_send()
+
+
+EARLY_TIMES = ((1, 7, 10, 12), (2, 11, 13, 15))
+LATE_TIMES = (0, 3, 5, 7)
 
 
 def attention_back(
-    numerators, qkv, teacher_qkv, d_context, context, inverse, docs, in_big, moves, moved, collective_id
+    streams,
+    groups,
+    numerators,
+    qkv,
+    teacher_qkv,
+    d_context,
+    context,
+    inverse,
+    docs,
+    in_big,
+    small,
+    active,
+    bin_own,
+    d_one,
+    tokens,
+    output,
+    early_arrays,
+    collective_id,
 ):
     seq, width3 = qkv.shape
     width = width3 // 3
     pairs = width // 128
     tile = 256
+    rows, depth = d_one.shape
+    size = lax.axis_size("dp")
+    shard = rows // streams
+    bag = Bag()
+    bag.add("v_aug", pltpu.VMEM((2, seq, 128), BF))
+    bag.add("dk_acc", pltpu.VMEM((128, seq), F32))
+    bag.add("dv_acc", pltpu.VMEM((128, seq), F32))
+    bag.add("grams", pltpu.VMEM((8, 128, 128), BF))
+    bag.add("dq_all", pltpu.VMEM((seq, 128), BF))
+    bag.add("d_act", pltpu.VMEM((seq, depth), F32))
+    bag.add("active", pltpu.VMEM((seq, depth), BF))
+    bag.add("weights", pltpu.VMEM((3, depth, width), BF))
+    bag.add("d_one", pltpu.VMEM((rows, depth), F32))
+    bag.add("x_rows", pltpu.VMEM((streams, shard, depth), BF))
+    bag.add("load", dma(4))
+    bag.add("sums", pltpu.VMEM((8, width), F32))
+    bag.add("outbox", pltpu.VMEM((groups - 1, rows, depth), BF))
+    bag.add("inbox", pltpu.VMEM((groups - 1, rows, depth), BF))
+    bag.add("core_s", dma(groups))
+    bag.add("core_r", dma(groups))
+    bag.add("blocks", pltpu.VMEM((streams, shard, depth), BF))
+    bag.add("grad_s", dma(streams))
+    bag.add("grad_r", dma(streams))
+    count = size + streams + groups
+    bag.add("small", pltpu.VMEM((3,) + small.shape, F32))
+    bag.add("small_box", pltpu.VMEM((count,) + small.shape, F32))
+    bag.add("small_s", dma(count))
+    bag.add("small_r", dma(count))
+    back = Swap(streams, groups, (shard, depth), BF)
+    for i, item in enumerate(back.scratch()):
+        bag.add(f"back{i}", item)
+    early, flat = [], []
+    for n, arrays in enumerate(early_arrays):
+        job = Reduce(bag, f"early{n}", streams, groups, [a.shape for a in arrays], True)
+        early.append(job)
+        flat += [
+            a.reshape(groups, size, chunk, cols) for a, (chunk, cols) in zip(arrays, job.shapes)
+        ]
+    late = [
+        Reduce(bag, f"late{p}", streams, groups, [(depth, 3 * 128)], False) for p in range(pairs)
+    ]
     part = pl.BlockSpec((tile, 128), lambda p, i: (i, p))
+    any_space = pl.BlockSpec(memory_space=pl.ANY)
 
     def whole(which):
         return pl.BlockSpec((seq, 128), lambda p, i: (0, which * pairs + p))
 
-    return pl.pallas_call(
-        functools.partial(backward_kernel, moves, tile),
+    def constant(shape):
+        return pl.BlockSpec(shape, lambda p, i: (0,) * len(shape))
+
+    early_shapes = [shape for job in early for shape in job.out_shapes()]
+    late_shapes = [shape for job in late for shape in job.out_shapes()]
+    results = pl.pallas_call(
+        functools.partial(backward_kernel, streams, groups, tile, bag, back, early, late),
         grid=(pairs, seq // tile),
         in_specs=[
             pl.BlockSpec((2, tile, seq), lambda p, i: (p, i, 0)),
@@ -653,24 +1083,18 @@
             part,
             part,
             pl.BlockSpec((tile, 1), lambda p, i: (i, 0)),
-            pl.BlockSpec((1, seq), lambda p, i: (0, 0)),
-            pl.BlockSpec((seq, 1), lambda p, i: (0, 0)),
+            constant((1, seq)),
+            constant((seq, 1)),
+            constant(small.shape),
         ]
-        + moves.spaces(),
-        out_specs=[part, whole(0), whole(0)] + moves.spaces(),
-        out_shape=[
-            jax.ShapeDtypeStruct((seq, width), BF),
-            jax.ShapeDtypeStruct((seq, width), BF),
-            jax.ShapeDtypeStruct((seq, width), BF),
-        ]
-        + moves.out_shapes(),
-        scratch_shapes=[
-            pltpu.VMEM((2, seq, 128), BF),
-            pltpu.VMEM((128, seq), F32),
-            pltpu.VMEM((128, seq), F32),
-            pltpu.VMEM((8, 128, 128), BF),
-        ]
-        + moves.scratch(),
+        + [any_space] * (5 + len(flat)),
+        out_specs=[any_space] * (2 + len(early_shapes) + len(late_shapes))
+        + [constant(small.shape)],
+        out_shape=[back.out_shape(), jax.ShapeDtypeStruct((streams, shard, depth), BF)]
+        + early_shapes
+        + late_shapes
+        + [jax.ShapeDtypeStruct(small.shape, F32)],
+        scratch_shapes=list(bag.items.values()),
         compiler_params=remote_params(collective_id),
         name="attention_back",
     )(
@@ -686,7 +1110,24 @@
         docs.reshape(seq, 1),
         docs.reshape(1, seq),
         in_big.astype(F32).reshape(seq, 1),
-        *moved,
+        small,
+        active,
+        bin_own,
+        d_one,
+        tokens,
+        output,
+        *flat,
+    )
+    output_back, grad_tokens, *rest = results
+    early_sums = rest[: len(flat)]
+    late_sums = rest[len(flat) : -1]
+    shapes = [a.shape for arrays in early_arrays for a in arrays]
+    return (
+        output_back,
+        grad_tokens,
+        [e.reshape(shape) for e, shape in zip(early_sums, shapes)],
+        [l.reshape(groups, depth, 3 * 128) for l in late_sums],
+        rest[-1],
     )
 
 
@@ -718,6 +1159,9 @@
     ggain_ref,
     gbias_ref,
     gub_ref,
+    gout_acc,
+    gup_acc,
+    gdown_acc,
 ):
     step = pl.program_id(0)
     groups = ctx_ref.shape[0]
@@ -725,7 +1169,7 @@
 
     @pl.when(step == 0)
     def _():
-        for ref in (gout_ref, gup_ref, gdown_ref, ggain_ref, gbias_ref, gub_ref):
+        for ref in (gout_acc, gup_acc, gdown_acc, ggain_ref, gbias_ref, gub_ref):
             ref[...] = jnp.zeros_like(ref)
 
     def row(ref, i):
@@ -765,14 +1209,14 @@
     upstream = cot_ref[...].astype(F32) + 0.5 * (output - t_out)
     d_two = norm_back(upstream, row(sg_ref, 1), normed_two, inverse_two)
     d_branch = d_two.astype(BF)
-    gdown_ref[...] += dot(inner_active, d_branch, TN)
+    gdown_acc[...] += dot(inner_active, d_branch, TN)
     d_inner = (dot(d_branch, bdown_ref[...], NT) * slope).astype(BF)
-    gup_ref[...] += dot(hidden_active, d_inner, TN)
+    gup_acc[...] += dot(hidden_active, d_inner, TN)
     d_hidden = d_two + dot(d_inner, bup_ref[...], NT) * hidden_slope
     d_one = norm_back(d_hidden, row(sg_ref, 0), normed_one, inverse_one)
     d1_ref[...] = d_one
     d_attended = d_one.astype(BF)
-    gout_ref[...] += dot(ctx_active, d_attended, TN)
+    gout_acc[...] += dot(ctx_active, d_attended, TN)
     d_context = (dot(d_attended, bo_ref[...], NT) * ctx_slope).astype(BF)
     for j in range(groups):
         dctx_ref[j] = d_context[:, j * width : (j + 1) * width]
@@ -787,6 +1231,12 @@
     gbias_ref[4:5, :] += total(d_branch.astype(F32))
     gbias_ref[5:6, :] += total(upstream)
     gub_ref[...] += total(d_inner.astype(F32))
+
+    @pl.when(step == pl.num_programs(0) - 1)
+    def _():
+        gout_ref[...] = gout_acc[...].astype(BF)
+        gup_ref[...] = gup_acc[...].astype(BF)
+        gdown_ref[...] = gdown_acc[...].astype(BF)
 
 
 def middle(r, x, tx, cot, ctx, tctx, weights, teacher_weights, vectors):
@@ -814,302 +1264,17 @@
             in_specs=[of_stream, of_stream, tall, split_rows, split_rows]
             + [full_of(a) for a in weights + teacher_weights + vectors],
             out_specs=[tall, tall, split_rows] + [full(s) for s in out_full],
+            scratch_shapes=[pltpu.VMEM(s, F32) for s in out_full[:3]],
         ),
         out_shape=[
             jax.ShapeDtypeStruct((rows, depth), BF),
             jax.ShapeDtypeStruct((rows, depth), F32),
             jax.ShapeDtypeStruct((groups, rows, width), BF),
         ]
-        + [jax.ShapeDtypeStruct(s, F32) for s in out_full],
+        + [jax.ShapeDtypeStruct(s, BF if i < 3 else F32) for i, s in enumerate(out_full)],
         compiler_params=pltpu.CompilerParams(vmem_limit_bytes=VMEM_BYTES),
         name="middle",
     )(r.reshape(1), x, tx, cot, ctx, tctx, *weights, *teacher_weights, *vectors)
-
-
-def finish_kernel(
-    streams,
-    groups,
-    wire,
-    dq_ref,
-    dk_ref,
-    dv_ref,
-    active_ref,
-    bin_ref,
-    d1_ref,
-    tokens_ref,
-    small_ref,
-    grad_ref,
-    late_ref,
-    sum_ref,
-    mine,
-    outbox,
-    inbox,
-    x_rows,
-    blocks,
-    partial,
-    partial_wire,
-    dp_box,
-    chunk_wire,
-    z_box,
-    piece,
-    small_send,
-    small_dp,
-    small_z,
-    small_core,
-    x_sem,
-    core_send,
-    core_recv,
-    back_send,
-    back_recv,
-    dp_send,
-    dp_recv,
-    z_send,
-    z_recv,
-    zg_send,
-    zg_recv,
-    dpg_send,
-    dpg_recv,
-    cg_send,
-    cg_recv,
-    ss,
-    sr,
-    local_sems,
-):
-    size = lax.axis_size("dp")
-    here = lax.axis_index("dp")
-    s, r = place(groups)
-    rows, depth = mine.shape
-    width = dq_ref.shape[1]
-    parts = (dq_ref, dk_ref, dv_ref)
-    along_z, cores, along_dp = stream_peers(streams, groups), core_peers(groups), dp_peers()
-    greet(along_z + cores + along_dp)
-    load = pltpu.make_async_copy(tokens_ref.at[pl.ds(r * streams, streams)], x_rows, x_sem)
-    load.start()
-
-    def d_active(start):
-        total = None
-        for i, ref in enumerate(parts):
-            term = dot(ref[pl.ds(start, rows), :], bin_ref[i], NT)
-            total = term if total is None else total + term
-        return total
-
-    core_copies = []
-    for j in range(1, groups):
-        other = lax.rem(r + j, groups)
-        outbox[j - 1] = d_active(pl.multiple_of(other * rows, rows)).astype(BF)
-        copy = remote(
-            outbox.at[j - 1], inbox.at[j - 1], core_send.at[j], core_recv.at[j], cores[j - 1]
-        )
-        copy.start()
-        core_copies.append(copy)
-
-    chunk = depth // size
-    for i, ref in enumerate(parts):
-        partial[:, i * width : (i + 1) * width] = dot(active_ref[...], ref[...], TN)
-    for p in range(size):
-        partial_wire[p] = partial[p * chunk : (p + 1) * chunk, :].astype(wire)
-    dp_copies = []
-    for d, peer in enumerate(along_dp, 1):
-        copy = remote(
-            partial_wire.at[lax.rem(here + d, size)],
-            dp_box.at[d - 1],
-            dp_send.at[d],
-            dp_recv.at[d],
-            peer,
-        )
-        copy.start()
-        dp_copies.append(copy)
-
-    def own_columns(vector):
-        return jnp.concatenate(
-            [jnp.where(r == j, vector, 0.0) for j in range(groups)], axis=1
-        )
-
-    small_send[0] = small_ref[...]
-    small_send[0, 2:3, :] = own_columns(jnp.sum(dq_ref[...].astype(F32), axis=0, keepdims=True))
-    small_send[0, 3:4, :] = own_columns(jnp.sum(dv_ref[...].astype(F32), axis=0, keepdims=True))
-    small_copies = []
-    for d, peer in enumerate(along_dp, 1):
-        copy = remote(small_send.at[0], small_dp.at[d - 1], ss.at[d], sr.at[d], peer)
-        copy.start()
-        small_copies.append(copy)
-
-    mine[...] = d_active(pl.multiple_of(r * rows, rows))
-    load.wait()
-    for copy in core_copies:
-        copy.wait_recv()
-    shard = rows // streams
-    back_copies = []
-    order = [2, 1, 3] if streams == 4 else list(range(1, streams))
-    for d in order + [0]:
-        target = lax.rem(s + d, streams)
-        at = pl.ds(pl.multiple_of(target * shard, shard), shard)
-        bent = jnp.tanh(x_rows[target].astype(F32) * (1.0 / clip_level))
-        total = mine[at, :]
-        for j in range(groups - 1):
-            total = total + inbox[j, at, :].astype(F32)
-        blocks[target] = (d1_ref[at, :] + total * (1.0 - bent * bent)).astype(BF)
-        if d:
-            copy = remote(
-                blocks.at[target], grad_ref.at[s], back_send.at[d], back_recv.at[d], along_z[d - 1]
-            )
-        else:
-            copy = pltpu.make_async_copy(blocks.at[s], grad_ref.at[s], local_sems.at[0])
-        copy.start()
-        back_copies.append(copy)
-
-    for copy in dp_copies:
-        copy.wait_recv()
-    total = partial[pl.ds(pl.multiple_of(here * chunk, chunk), chunk), :]
-    for d in range(size - 1):
-        total = total + dp_box[d].astype(F32)
-    slim = chunk // streams
-    for z in range(streams):
-        chunk_wire[z] = total[z * slim : (z + 1) * slim, :].astype(wire)
-    z_copies = []
-    for d, peer in enumerate(along_z, 1):
-        copy = remote(
-            chunk_wire.at[lax.rem(s + d, streams)], z_box.at[d - 1], z_send.at[d], z_recv.at[d], peer
-        )
-        copy.start()
-        z_copies.append(copy)
-    for copy in small_copies:
-        copy.wait_recv()
-    small_total = small_send[0]
-    for d in range(size - 1):
-        small_total = small_total + small_dp[d]
-    small_send[1] = small_total
-    small_z_copies = []
-    for d, peer in enumerate(along_z, 1):
-        at = size + d
-        copy = remote(small_send.at[1], small_z.at[d - 1], ss.at[at], sr.at[at], peer)
-        copy.start()
-        small_z_copies.append(copy)
-
-    for copy in z_copies:
-        copy.wait_recv()
-    total = chunk_wire[s].astype(F32)
-    for d in range(streams - 1):
-        total = total + z_box[d].astype(F32)
-    piece[...] = total.astype(wire)
-    zg_copies = []
-    keep = pltpu.make_async_copy(piece, late_ref.at[r, here, s], local_sems.at[1])
-    keep.start()
-    for d, peer in enumerate(along_z, 1):
-        copy = remote(piece, late_ref.at[r, here, s], zg_send.at[d], zg_recv.at[d], peer)
-        copy.start()
-        zg_copies.append(copy)
-    for copy in small_z_copies:
-        copy.wait_recv()
-    small_total = small_send[1]
-    for d in range(streams - 1):
-        small_total = small_total + small_z[d]
-    small_send[2] = small_total
-    small_c_copies = []
-    for j, peer in enumerate(cores, 1):
-        at = size + streams + j
-        copy = remote(small_send.at[2], small_core.at[j - 1], ss.at[at], sr.at[at], peer)
-        copy.start()
-        small_c_copies.append(copy)
-
-    keep.wait()
-    for copy in zg_copies:
-        copy.wait_recv()
-    dpg_copies = []
-    for d, peer in enumerate(along_dp, 1):
-        copy = remote(
-            late_ref.at[r, here], late_ref.at[r, here], dpg_send.at[d], dpg_recv.at[d], peer
-        )
-        copy.start()
-        dpg_copies.append(copy)
-    for copy in small_c_copies:
-        copy.wait_recv()
-    small_total = small_send[2]
-    for j in range(groups - 1):
-        small_total = small_total + small_core[j]
-    sum_ref[...] = small_total
-    for copy in dpg_copies:
-        copy.wait_recv()
-    cg_copies = []
-    for j, peer in enumerate(cores, 1):
-        copy = remote(late_ref.at[r], late_ref.at[r], cg_send.at[j], cg_recv.at[j], peer)
-        copy.start()
-        cg_copies.append(copy)
-    for copy in cg_copies:
-        copy.wait()
-    for copy in back_copies:
-        copy.wait()
-    for copy in (
-        core_copies
-        + dp_copies
-        + z_copies
-        + zg_copies
-        + dpg_copies
-        + small_copies
-        + small_z_copies
-        + small_c_copies
-    ):
-        copy.wait_send()
-
-
-def finish(streams, groups, d_queries, d_keys, d_values, active, bin_own, d_one, tokens, small, cid):
-    seq, width = d_queries.shape
-    rows, depth = d_one.shape
-    size = lax.axis_size("dp")
-    chunk = depth // size
-    slim = chunk // streams
-    wire = BF if slim % 16 == 0 else F32
-    wide = 3 * width
-    vmem = pl.BlockSpec(memory_space=pltpu.VMEM)
-    any_space = pl.BlockSpec(memory_space=pl.ANY)
-    small_shape = small.shape
-    return pl.pallas_call(
-        functools.partial(finish_kernel, streams, groups, wire),
-        in_specs=[vmem] * 6 + [any_space, vmem],
-        out_specs=[any_space, any_space, vmem],
-        out_shape=[
-            jax.ShapeDtypeStruct((streams, rows // streams, depth), BF),
-            jax.ShapeDtypeStruct((groups, size, streams, slim, wide), wire),
-            jax.ShapeDtypeStruct(small_shape, F32),
-        ],
-        scratch_shapes=[
-            pltpu.VMEM((rows, depth), F32),
-            pltpu.VMEM((groups - 1, rows, depth), BF),
-            pltpu.VMEM((groups - 1, rows, depth), BF),
-            pltpu.VMEM((streams, rows // streams, depth), BF),
-            pltpu.VMEM((streams, rows // streams, depth), BF),
-            pltpu.VMEM((depth, wide), F32),
-            pltpu.VMEM((size, chunk, wide), wire),
-            pltpu.VMEM((size - 1, chunk, wide), wire),
-            pltpu.VMEM((streams, slim, wide), wire),
-            pltpu.VMEM((streams - 1, slim, wide), wire),
-            pltpu.VMEM((slim, wide), wire),
-            pltpu.VMEM((3,) + small_shape, F32),
-            pltpu.VMEM((size - 1,) + small_shape, F32),
-            pltpu.VMEM((streams - 1,) + small_shape, F32),
-            pltpu.VMEM((groups - 1,) + small_shape, F32),
-            pltpu.SemaphoreType.DMA,
-            dma(groups),
-            dma(groups),
-            dma(streams),
-            dma(streams),
-            dma(size),
-            dma(size),
-            dma(streams),
-            dma(streams),
-            dma(streams),
-            dma(streams),
-            dma(size),
-            dma(size),
-            dma(groups),
-            dma(groups),
-            dma(size + streams + groups),
-            dma(size + streams + groups),
-            dma(2),
-        ],
-        compiler_params=remote_params(cid),
-        name="finish",
-    )(d_queries, d_keys, d_values, active, bin_own, d_one, tokens, small)
 
 
 def latent_columns(latent, binary_grad):
@@ -1146,23 +1311,26 @@
     )(*latents, *grads)
 
 
-def late_latents_kernel(latent, grad, out):
-    out[0] = latent_columns(latent[0], grad[0])
+def late_latents_kernel(pairs, latent, *refs):
+    grads, out = refs[:pairs], refs[pairs]
+    for p in range(pairs):
+        columns = slice(p * 128, (p + 1) * 128)
+        out[0, :, columns] = latent_columns(latent[0, :, columns], grads[p][0])
 
 
 def late_latents(latent, grads):
-    groups, depth, wide = grads.shape
-    width = wide // 3
-    spec = pl.BlockSpec((1, depth, width), lambda m, j: (m, 0, j))
+    pairs = len(grads)
+    groups, depth, wide = grads[0].shape
+    spec = pl.BlockSpec((1, depth, pairs * 128), lambda m, j: (m, 0, j))
     return pl.pallas_call(
-        late_latents_kernel,
+        functools.partial(late_latents_kernel, pairs),
         grid=(3, groups),
-        in_specs=[spec, pl.BlockSpec((1, depth, width), lambda m, j: (j, 0, m))],
+        in_specs=[spec] + [pl.BlockSpec((1, depth, 128), lambda m, j: (j, 0, m))] * pairs,
         out_specs=spec,
         out_shape=jax.ShapeDtypeStruct(latent.shape, F32),
         compiler_params=pltpu.CompilerParams(vmem_limit_bytes=VMEM_BYTES),
         name="late_latents",
-    )(latent, grads)
+    )(latent, *grads)
 
 
 def shards(
@@ -1284,12 +1452,15 @@
             teacher_up_bias.reshape(1, -1),
         ],
     )
-    early = lax.psum((g_out.astype(BF), g_up.astype(BF), g_down.astype(BF)), ("dp", "blk"))
     small = jnp.concatenate(
         [g_gain, g_bias, g_ub.reshape(-1, depth), jnp.zeros((4, depth), F32)], axis=0
     )
     (d_ctx_rows,) = move(Moves(by_rows), [d_context], 5, "d_context_rows")
-    d_queries, d_keys, d_values, output_blocks = attention_back(
+    grads = [[g_up], [g_down, g_out]]
+    in_kernel = depth % (16 * blocks * lax.axis_size("dp")) == 0
+    output_blocks, grad_tokens, early, late, small = attention_back(
+        streams,
+        groups,
         numerators,
         qkv,
         teacher_own,
@@ -1298,19 +1469,25 @@
         inverse,
         docs,
         in_big,
-        Moves(swap),
-        [output.reshape(streams, shard_len, depth)],
+        small,
+        active,
+        bin_own,
+        d_one,
+        token_blocks,
+        output.reshape(streams, shard_len, depth),
+        grads if in_kernel else [],
         6,
     )
-    grad_tokens, late, small = finish(
-        streams, groups, d_queries, d_keys, d_values, active, bin_own, d_one, token_blocks, small, 7
-    )
+    if not in_kernel:
+        early = lax.psum((g_up, g_down, g_out), ("dp", "blk"))
     up_rows = latent_up.shape[1] // depth
-    grad_out, grad_up, grad_down = early_latents([latent_out, latent_up, latent_down], early)
+    grad_out, grad_up, grad_down = early_latents(
+        [latent_out, latent_up, latent_down], [early[2], early[0], early[1]]
+    )
     return (
         output_blocks,
         grad_tokens,
-        late_latents(latent_qkv, late.reshape(groups, depth, 3 * width)),
+        late_latents(latent_qkv, late),
         grad_out,
         grad_up,
         grad_down,

time: 406 us -> 336 us (0.83)
  waiting for transfers between devices: 43.8 us -> 0 us
  between operations: 14.5 us -> 1.08 us
  other arithmetic: 17.8 us -> 12.7 us
  matrix products: 11 us -> 6.28 us
    psum x1 -> x0, waiting for transfers between devices: 43.8 us -> none  [shards(): lax.psum((g_out.astype(BF), g_up.astype(BF), g_down.astype(BF)), ('dp', '...]
    convert_element_type x3 -> x0, other arithmetic: 6.43 us -> none  [the longest x1 3.98 us: shards(): g_up.astype(BF)]
    dot_general x6, matrix products: 11 us -> 6.28 us  [dot(): return lax.dot_general(a, b, dims, preferred_element_type=F32)]
    pallas_call x3 -> x2, Pallas kernels: 120 us -> 121 us  [the longest x1 114 us: attention_back(): pl.pallas_call(functools.partial(backward_kernel, streams, groups, tile,...]
  transfers between devices with their start and end apart: 1 -> 0, of which waited for: 1 -> 0; matrix products, arithmetic and copies ran while one was open for 3% -> 0% of each run, Pallas kernels for 31% -> 0%
where the time goes in v3:
time: 336 us; the launch traced here: 331 us
  Pallas kernels  297 us (88%)
  local copies, waits for them, and re-layouts  13.3 us (4%)
  other arithmetic  12.7 us (4%)
  matrix products  6.28 us (2%)
    pallas_call x1, Pallas kernels, attention_back(): pl.pallas_call(functools.partial(backward_kernel, streams, groups, tile,...  114 us
    pallas_call x2, Pallas kernels, attention(): pl.pallas_call(functools.partial(forward_kernel, moves, keep, tile, edge)...  84 us
    pallas_call x1, Pallas kernels, middle(): pl.pallas_call(middle_kernel, grid_spec=pltpu.PrefetchScalarGridSpec(num_...  38.1 us
    pallas_call x1, Pallas kernels, intake(): pl.pallas_call(functools.partial(intake_kernel, moves), out_shape=[jax.Sh...  38 us
    pallas_call x1, Pallas kernels, early_latents(): pl.pallas_call(early_latents_kernel, grid=(steps,), in_specs=specs * 2, o...  12 us

profile of v3, /device:TPU:0, one launch (start us, length us, event | category | flops | bytes accessed | tf_op | source)
XLA Modules:
  0.0 330.6 jit_solution(3642744346915823790)
XLA Ops:
  0.7 2.1 constant_dynamic-slice_fusion.2.qkv_ref
  2.7 1.3 reshape.113.refs_1_
  4.0 38.0 %intake.1 = (bf16[3,512,256]{2,1,0:T(8,128)(2,1)}, bf16[512,512]{1,0:T(8,128)(2,1)}, bf16[512,2048]{1,0:T(8,128)(2,1)}, bf16[2048,512]{1,0:T(8,128)(2,1)}, bf16[...) custom-call(bf16[3,512,256]{2,1,0:T(8,128)(2,1)} %constant_dynamic-s, ...), custom_call_target="tpu_custom_call" | custom-call | tf_op jit(solution)/shard_map/intake/pallas_call | solution.py:538
  42.0 0.0 copy-start.8
  42.0 2.3 multiply_convert_fusion.1
  44.3 0.9 constant_dynamic-slice_fusion
  45.2 0.0 copy-done.8
  45.2 0.7 fusion.9
  45.9 0.7 convolution_convert_fusion.1
  46.6 0.7 fusion.1
  47.3 0.0 copy-start.9
  47.4 2.0 pad_maximum_fusion.q_ref.k_ref.v_ref
  49.3 0.0 copy-done.9
  49.3 1.3 copy.47.col_ref
  50.7 0.0 copy-start.4
  50.7 44.3 %attention_student.1 = (bf16[4,2048,2048]{2,1,0:T(8,128)(2,1)}, bf16[2048,256]{1,0:T(8,128)(2,1)}, f32[2048,256]{1,0:T(8,128)}, bf16[8,256,512]{2,1,0:T(8,128)(2,1)}, bf16[4,128,2048]{2,1,0:T(8,128)(2,1)}) custom-call(bf16[2048,768]{1,0:T(8,128)(2,1)} %pad_maximum_fusion.q_ref.k_ref.v_ref, bf16[2048,768]{1,0:T(8,128)(2,1)} %pad_maximum_fusion.q_ref.k_ref.v_ref, ...), custom_call_target="tpu_custom_call" | custom-call | tf_op jit(solution)/shard_map/attention_student/pallas_call | solution.py:652
  95.0 0.0 copy-start.2
  95.0 0.0 copy-done.4
  95.0 0.1 copy.48
  95.1 0.0 copy-start.3
  95.1 2.0 copy-done.2
  97.1 1.7 fusion.6
  98.8 0.0 copy-done.3
  98.8 0.7 convolution_convert_fusion
  99.5 0.0 copy-start.7
  99.5 1.8 fusion.3
  101.3 0.0 copy-done.7
  101.3 1.8 pad_maximum_fusion.1.q_ref.k_ref.v_ref.tq_ref.tk_ref
  103.1 39.7 %attention_teacher.1 = (bf16[2048,256]{1,0:T(8,128)(2,1)}, bf16[4,256,512]{2,1,0:T(8,128)(2,1)}, bf16[4,512,512]{2,1,0:T(8,128)(2,1)}, bf16[2,1024,256]{2,1,0:T(8,128)(2,1)}) custom-call(bf16[2048,768]{1,0:T(8,128)(2,1)} %pad_maximum_fusion.1.q_ref.k_ref.v_ref.tq_ref.tk_ref, bf16[2048,768]{1,0:T(8,128)(2,1)} %pad_maximum_fusion.1.q_ref.k_ref.v_ref.tq_ref.tk_ref, ...), custom_call_target="tpu_custom_call" | custom-call | tf_op jit(solution)/shard_map/attention_teacher/pallas_call | solution.py:652
  142.8 2.3 teacher_context_rows.1.tctx_ref
  145.1 38.1 %middle.1 = (bf16[1024,512]{1,0:T(8,128)(2,1)}, f32[1024,512]{1,0:T(8,128)}, bf16[2,1024,256]{2,1,0:T(8,128)(2,1)}, bf16[512,512]{1,0:T(8,128)(2,1)}, bf16[512,2...) custom-call(s32[1]{0:T(128)} %bitcast.16.unused_place, ...), custom_call_target="tpu_custom_call" | custom-call | tf_op jit(solution)/shard_map/middle/pallas_call | solution.py:1259
  183.2 0.0 copy-start.1
  183.2 0.6 broadcast.25
  183.8 1.4 reduce.3
  185.2 0.1 pad.3.clone
  185.3 1.4 maximum_maximum_fusion.small_ref
  186.7 0.0 copy-start
  186.7 2.3 d_context_rows.1
  189.0 1.2 slice.56
  190.2 0.0 copy-done.1
  190.2 1.7 compare_convert_fusion.bigc_ref
  191.9 0.0 copy-done
  191.9 2.2 multiply_convert_fusion.active_hbm
  194.1 114.3 %attention_back.1 = (bf16[4,256,512]{2,1,0:T(8,128)(2,1)}, bf16[4,256,512]{2,1,0:T(8,128)(2,1)}, bf16[2,4,4,16,2048]{4,3,2,1,0:T(8,128)(2,1)}, bf16[2,4,4,64,512...) custom-call(bf16[4,2048,2048]{2,1,0:T(8,128)(2,1)} %get-tuple-elemen, ...), custom_call_target="tpu_custom_call" | custom-call | tf_op jit(solution)/shard_map/attention_back/pallas_call | solution.py:1072
  308.4 12.0 %early_latents.1 = (f32[512,512]{1,0:T(8,128)}, f32[512,2048]{1,0:T(8,128)}, f32[2048,512]{1,0:T(8,128)}) custom-call(bf16[512,512]{1,0:T(8,128)(2,1)} %lo.1, bf16[512,2048]{1,0:T(8,128)(2,1)} %lu.1, bf16[2048,512]{1,0:T(8,128)(2,1)} %ld.1, bf16[512,512]{1,0:T(8,128)(2,1)} %bitcast.86, bf16[512,2048]{1,0:T(8,128)(2,1)} %bitcast.75, bf16[2048,512]{1,0:T(8,128)(2,1)} %bitcast.76), custom_call_target="tpu_custom_call" | custom-call | tf_op jit(solution)/shard_map/early_latents/pallas_call | solution.py:1303
  320.4 0.0 copy-start.10
  320.4 0.0 copy-start.6
  320.4 6.2 %late_latents.1 = f32[3,512,512]{2,1,0:T(8,128)} custom-call(bf16[3,512,512]{2,1,0:T(8,128)(2,1)} %latent.1, bf16[2,512,384]{2,1,0:T(8,128)(2,1)} %bitcast.83, bf16[2,512,384]{2,1,0:T(8,128)(2,1)} %bitcast.84), custom_call_target="tpu_custom_call" | custom-call | tf_op jit(solution)/shard_map/late_latents/pallas_call | solution.py:1325
  326.6 0.0 copy-start.5
  326.6 0.0 copy-done.10
  326.6 0.6 copy.62
  327.2 0.6 slice.54
  327.8 0.6 slice.53
  328.4 0.0 copy-done.6
  328.4 1.0 copy.65
  329.4 0.0 copy-done.5
  329.4 1.0 copy.66
  (3 shorter events, 0.0 us)
Async XLA Ops:
  42.0 3.2 copy-start.8
  47.3 2.0 copy-start.9
  50.7 44.3 %copy-start.4 = (bf16[4,3,128,512]{3,2,1,0:T(8,128)(2,1)S(1)}, bf16[4,3,128,512]{3,2,1,0:T(8,128)(2,1)}, u32[]{:S(2)}) copy-start(bf16[4,3,128,512]{3,2,1,0:T(8,128)(2,1)} %get-tuple-element.51) | copy-start | bytes 4718596
  95.0 2.2 copy-start.2
  95.1 3.7 %copy-start.3 = (bf16[3,4,128,512]{3,2,1,0:T(8,128)(2,1)}, bf16[3,4,128,512]{3,2,1,0:T(8,128)(2,1)S(1)}, u32[]{:S(2)}) copy-start(bf16[3,4,128,512]{3,2,1,0:T(8,128)(2,1)S(1)} %copy.48) | copy-start | bytes 4718596
  99.5 1.8 copy-start.7
  183.2 7.0 %copy-start.1 = (s32[2048,1]{1,0:T(8,128)S(1)}, s32[2048,1]{1,0:T(8,128)}, u32[]{:S(2)}) copy-start(s32[2048,1]{1,0:T(8,128)} %copy.47.col_ref) | copy-start | bytes 24580
  186.7 5.2 %copy-start = (bf16[8,256,512]{2,1,0:T(8,128)(2,1)S(1)}, bf16[8,256,512]{2,1,0:T(8,128)(2,1)}, u32[]{:S(2)}) copy-start(bf16[8,256,512]{2,1,0:T(8,128)(2,1)} %get-tuple-element.46.tokens_hbm) | copy-start | bytes 6291460
  320.4 6.2 %copy-start.10 = (f32[16,512]{1,0:T(8,128)S(1)}, f32[16,512]{1,0:T(8,128)}, u32[]{:S(2)}) copy-start(f32[16,512]{1,0:T(8,128)} %get-tuple-element.82) | copy-start | bytes 98308
  320.4 8.0 %copy-start.6 = (bf16[4,256,512]{2,1,0:T(8,128)(2,1)S(1)}, bf16[4,256,512]{2,1,0:T(8,128)(2,1)}, u32[]{:S(2)}) copy-start(bf16[4,256,512]{2,1,0:T(8,128)(2,1)} %get-tuple-element.98) | copy-start | bytes 3145732
  326.6 2.8 copy-start.5

commit v4 on v3

--- a/solution.py
+++ b/solution.py
@@ -231,33 +231,6 @@
             copy.wait()
 
 
-class Rows:
-    def __init__(self, streams, groups, block, dtype):
-        self.groups, self.block, self.dtype = groups, block, dtype
-
-    def scratch(self):
-        return [dma(self.groups), dma(self.groups), pltpu.VMEM(self.block, self.dtype), dma(2)]
-
-    def out_shape(self):
-        return jax.ShapeDtypeStruct((self.groups,) + self.block, self.dtype)
-
-    def peers(self):
-        return [("core", core_peers(self.groups))]
-
-    def parts(self, source, target, send, recv, stage, sems):
-        g = self.groups
-        s, r = place(g)
-        cores = core_peers(g)
-        copies = [
-            remote(source.at[lax.rem(r + j, g)], target.at[r], send.at[j], recv.at[j], cores[j - 1])
-            for j in range(1, g)
-        ]
-        return copies, Staged(source.at[r], target.at[r], stage, sems)
-
-    first = Swap.first
-    last = Swap.last
-
-
 class Spread:
     def __init__(self, block, dtype):
         self.block, self.dtype = block, dtype
@@ -282,6 +255,48 @@
 
     first = Swap.first
     last = Swap.last
+
+
+class Tiles:
+    def __init__(self, bag, name, groups, pairs, per_owner):
+        self.name, self.groups, self.pairs, self.per_owner = name, groups, pairs, per_owner
+        count = pairs * per_owner
+        bag.add(f"{name}_s", dma(groups * count))
+        bag.add(f"{name}_r", dma(groups * count))
+
+    def slot(self, who, pair, at):
+        return (who * self.pairs + pair) * self.per_owner + at
+
+    def copy(self, have, source, target, owner, pair, at):
+        s, r = place(self.groups)
+        return remote(
+            source,
+            target,
+            have[f"{self.name}_s"].at[self.slot(owner, pair, at)],
+            have[f"{self.name}_r"].at[self.slot(r, pair, at)],
+            {"blk": s * self.groups + owner},
+        )
+
+    def own(self, have, source, target, pair, at):
+        s, r = place(self.groups)
+        return pltpu.make_async_copy(
+            source, target, have[f"{self.name}_s"].at[self.slot(r, pair, at)]
+        )
+
+    def finish(self, have, source, target):
+        s, r = place(self.groups)
+        for pair in range(self.pairs):
+            for at in range(self.per_owner):
+                self.own(have, source, target, pair, at).wait()
+                for j in range(1, self.groups):
+                    other = lax.rem(r + j, self.groups)
+                    remote(
+                        source,
+                        target,
+                        have[f"{self.name}_s"].at[self.slot(other, pair, at)],
+                        have[f"{self.name}_r"].at[self.slot(other, pair, at)],
+                        {"blk": s * self.groups + other},
+                    ).wait()
 
 
 class Bag:
@@ -456,8 +471,8 @@
 
 
 class Moves:
-    def __init__(self, *jobs):
-        self.jobs = jobs
+    def __init__(self, *jobs, others=()):
+        self.jobs, self.others = list(jobs), list(others)
         self.counts = [len(job.scratch()) for job in jobs]
 
     def scratch(self):
@@ -476,7 +491,7 @@
             at += count
 
     def first(self, sources, targets, scratch):
-        greet(unique(self.jobs))
+        greet(unique(self.jobs + self.others))
         for job, refs in self.each(sources, targets, scratch):
             job.first(*refs)
 
@@ -491,40 +506,24 @@
     )
 
 
-def move(moves, arrays, collective_id, name):
-    count = len(arrays)
-
-    def kernel(*refs):
-        sources, targets, scratch = refs[:count], refs[count : 2 * count], refs[2 * count :]
-        moves.first(sources, targets, scratch)
-        moves.last(sources, targets, scratch)
-
-    return pl.pallas_call(
-        kernel,
-        out_shape=moves.out_shapes(),
-        in_specs=moves.spaces(),
-        out_specs=moves.spaces(),
-        scratch_shapes=moves.scratch(),
-        compiler_params=remote_params(collective_id),
-        name=name,
-    )(*arrays)
-
-
 def binary_columns(latent):
     matrix = latent.astype(F32)
     scale = jnp.sqrt(jnp.mean(matrix * matrix, axis=0, keepdims=True) + 1e-06)
     return (scale * jnp.tanh(matrix * (2.0 / scale))).astype(BF)
 
 
-def intake_kernel(moves, qkv_ref, out_ref, up_ref, down_ref, *refs):
+def intake_kernel(moves, groups, qkv_ref, out_ref, up_ref, down_ref, *refs):
     count = len(moves.jobs)
     sources = refs[:count]
     own_bin, out_bin, up_bin, down_bin = refs[count : count + 4]
     targets = refs[count + 4 : 2 * count + 4]
     scratch = refs[2 * count + 4 :]
     moves.first(sources, targets, scratch)
+    s, r = place(groups)
+    width = own_bin.shape[3]
+    own = pl.ds(pl.multiple_of(r * width, 128), width)
     for i in range(3):
-        own_bin[i] = binary_columns(qkv_ref[i])
+        own_bin[0, i] = binary_columns(qkv_ref[i, :, own])
     out_bin[...] = binary_columns(out_ref[...])
     for i in range(0, up_ref.shape[1], 512):
         up_bin[:, i : i + 512] = binary_columns(up_ref[:, i : i + 512])
@@ -533,11 +532,13 @@
     moves.last(sources, targets, scratch)
 
 
-def intake(moves, latents, arrays, collective_id):
+def intake(moves, groups, latents, arrays, collective_id):
+    three, depth, unused = latents[0].shape
+    shapes = [(1, three, depth, depth // groups)] + [a.shape for a in latents[1:]]
     vmem = pl.BlockSpec(memory_space=pltpu.VMEM)
     return pl.pallas_call(
-        functools.partial(intake_kernel, moves),
-        out_shape=[jax.ShapeDtypeStruct(a.shape, BF) for a in latents] + moves.out_shapes(),
+        functools.partial(intake_kernel, moves, groups),
+        out_shape=[jax.ShapeDtypeStruct(shape, BF) for shape in shapes] + moves.out_shapes(),
         in_specs=[vmem] * 4 + moves.spaces(),
         out_specs=[vmem] * 4 + moves.spaces(),
         scratch_shapes=moves.scratch(),
@@ -550,116 +551,219 @@
     return lax.broadcasted_iota(jnp.int32, shape, 1)
 
 
-def forward_kernel(moves, keep, tile, edge, q_ref, k_ref, v_ref, col_ref, row_ref, *rest):
+def forward_kernel(
+    moves, keep, streams, groups, tile, bag, tiles, x_ref, w_ref, bias_ref, row_ref, *rest
+):
     count = len(moves.jobs)
     sources, rest = rest[:count], rest[count:]
+    q_ref, k_ref, rows_ref, *rest = rest
     if keep:
-        e_ref, ctx_ref, inv_ref, *rest = rest
-    else:
-        ctx_ref, *rest = rest
-    targets, (k_aug, v_aug, *scratch) = rest[:count], rest[count:]
+        v_ref, e_ref, ctx_ref, inv_ref, active_ref, *rest = rest
+    targets, rest = rest[:count], rest[count:]
+    have = bag.bind(rest)
+    scratch = tuple(have[f"moves{i}"] for i in range(len(moves.scratch())))
+    k_aug, v_aug, ctx_all, mask, edges = (
+        have["k_aug"],
+        have["v_aug"],
+        have["ctx_all"],
+        have["mask"],
+        have["edges"],
+    )
+    active = active_ref if keep else x_ref
     pair, step = pl.program_id(0), pl.program_id(1)
-    steps = pl.num_programs(1)
+    pairs, steps = pl.num_programs(0), pl.num_programs(1)
     seq = k_ref.shape[0]
+    s, r = place(groups)
+    sub = min(256, tile)
+    width = w_ref.shape[3]
+    n_pairs = ctx_all.shape[0]
+    offset = pair * 128 if width == n_pairs * 128 else (r * n_pairs + pair) * 128
+    offset = pl.multiple_of(offset, 128)
+    home = pl.multiple_of((r * n_pairs + pair) * 128, 128)
 
     @pl.when((pair == 0) & (step == 0))
     def _():
         moves.first(sources, targets, scratch)
+        ids = row_ref[...]
+        big_at = long_at(streams, groups, seq)
+        big = ids[:, big_at : big_at + 1]
+        mask[...] = jnp.where(ids == big, 0.0, masked_score)
+        edges[0] = jnp.broadcast_to(ids[:, :sub], (128, sub)).T
+        edges[1] = jnp.broadcast_to(ids[:, seq - sub :], (128, sub)).T
+        if keep:
+            for i in range(0, seq, 256):
+                active_ref[i : i + 256, :] = squash(x_ref[i : i + 256, :].astype(F32)).astype(BF)
 
     @pl.when(step == 0)
     def _():
+        columns = pl.ds(offset, 128)
+
+        def project(i, bias):
+            matrix = jnp.concatenate(
+                [w_ref[d, i, :, columns] for d in range(w_ref.shape[0])], axis=0
+            )
+            result = dot(active[...], matrix)
+            if bias is not None:
+                result = result + bias_ref[bias : bias + 1, pl.ds(home, 128)]
+            return result.astype(BF)
+
         low = lanes_of((seq, 128)) < 64
         lane = lanes_of((seq, 128))
-        keys = k_ref[...].astype(F32)
+        q_ref[...] = (project(0, 0).astype(F32) * 0.125).astype(BF)
+        keys = project(1, None)
+        k_ref[...] = keys
+        keys = keys.astype(F32)
         turned = pltpu.roll(keys, 64, 1)
         k_aug[0] = jnp.where(low, keys, turned).astype(BF)
         k_aug[1] = jnp.where(low, turned, keys).astype(BF)
-        values = v_ref[...].astype(F32)
+        values = project(2, 1)
+        if keep:
+            v_ref[...] = values
+        values = values.astype(F32)
         v_aug[0] = jnp.where(low, values, jnp.where(lane < 66, 1.0, 0.0)).astype(BF)
         v_aug[1] = jnp.where(low, jnp.where(lane < 2, 1.0, 0.0), values).astype(BF)
 
-    def body(whole):
-        low = lanes_of((tile, 128)) < 64
-        scaled = q_ref[...].astype(F32) * LOG2E
-        upper = scaled.astype(BF).astype(F32)
-        rest_part = scaled - upper
-        results = []
-        for h in range(2):
-            if h == 0:
-                q_aug = jnp.where(low, upper, pltpu.roll(rest_part, 64, 1)).astype(BF)
-            else:
-                q_aug = jnp.where(low, pltpu.roll(upper, 64, 1), rest_part).astype(BF)
-            scores = dot(q_aug, k_aug[h], NT)
-            if whole:
-                scores = jnp.where(col_ref[...] == row_ref[...], scores, masked_score)
-            else:
-                left = jnp.where(
-                    col_ref[...] == row_ref[:, :edge], scores[:, :edge], masked_score
+    start = pl.multiple_of(step * tile, tile)
+
+    def body(edge_at):
+        low = lanes_of((sub, 128)) < 64
+        parts = []
+        for at in range(0, tile, sub):
+            scaled = q_ref[pl.ds(start + at, sub), :].astype(F32) * LOG2E
+            upper = scaled.astype(BF).astype(F32)
+            lower = scaled - upper
+            parts.append(
+                (
+                    jnp.where(low, upper, pltpu.roll(lower, 64, 1)).astype(BF),
+                    jnp.where(low, pltpu.roll(upper, 64, 1), lower).astype(BF),
                 )
-                right = jnp.where(
-                    col_ref[...] == row_ref[:, seq - edge :], scores[:, seq - edge :], masked_score
-                )
-                scores = jnp.concatenate([left, scores[:, edge : seq - edge], right], axis=1)
+            )
+        chains = [(at, h) for at in range(0, tile, sub) for h in range(2)]
+
+        def scores_of(at, h):
+            scores = dot(parts[at // sub][h], k_aug[h], NT)
+            if edge_at is not None and at == (0 if edge_at == 0 else tile - sub):
+                return jnp.where(edges[edge_at][:, :1] == row_ref[...], scores, masked_score)
+            return jnp.concatenate(
+                [
+                    scores[:, :sub] + mask[:, :sub],
+                    scores[:, sub : seq - sub],
+                    scores[:, seq - sub :] + mask[:, seq - sub :],
+                ],
+                axis=1,
+            )
+
+        scores = scores_of(*chains[0])
+        results = {}
+        for n, (at, h) in enumerate(chains):
+            if n + 1 < len(chains):
+                later = scores_of(*chains[n + 1])
             peak = jnp.max(scores, axis=1, keepdims=True)
             numerators = jnp.exp2(scores - peak).astype(BF)
             if keep:
-                e_ref[h] = numerators
+                e_ref[h, at : at + sub, :] = numerators
             total = dot(numerators, v_aug[h])
             where_sum = 64 if h == 0 else 0
             inverse = 1.0 / total[:, where_sum : where_sum + 1]
-            results.append((total * inverse, inverse))
-        ctx_ref[...] = jnp.where(low, results[0][0], results[1][0]).astype(BF)
-        if keep:
-            inv_ref[...] = jnp.where(low, results[0][1], results[1][1])
-
-    at_edge = (step == 0) | (step == steps - 1)
-
-    @pl.when(at_edge)
+            results[h] = (total * inverse, inverse)
+            if n + 1 < len(chains):
+                scores = later
+            if h == 1:
+                done = jnp.where(low, results[0][0], results[1][0]).astype(BF)
+                ctx_all[pair, pl.ds(start + at, sub), :] = done
+                if keep:
+                    ctx_ref[at : at + sub, :] = done
+                    inv_ref[at : at + sub, :] = jnp.where(low, results[0][1], results[1][1])
+
+    @pl.when(step == 0)
     def _():
-        body(True)
-
-    @pl.when(jnp.logical_not(at_edge))
+        body(0)
+
+    @pl.when(step == steps - 1)
     def _():
-        body(False)
-
-    @pl.when((pair == pl.num_programs(0) - 1) & (step == steps - 1))
+        body(1)
+
+    @pl.when((step > 0) & (step < steps - 1))
     def _():
+        body(None)
+
+    owned = seq // groups
+    owner = start // owned
+    at = lax.rem(step, owned // tile)
+    source = ctx_all.at[pair, pl.ds(start, tile)]
+    target = rows_ref.at[r, pair, pl.ds(pl.multiple_of(lax.rem(start, owned), tile), tile)]
+
+    @pl.when(owner == r)
+    def _():
+        tiles.own(have, source, target, pair, at).start()
+
+    @pl.when(owner != r)
+    def _():
+        tiles.copy(have, source, target, owner, pair, at).start()
+
+    @pl.when((pair == pairs - 1) & (step == steps - 1))
+    def _():
+        tiles.finish(have, source, target)
         moves.last(sources, targets, scratch)
 
 
-def attention(qkv, docs, moves, moved, keep, collective_id, name):
-    seq, width3 = qkv.shape
-    width = width3 // 3
+def long_at(streams, groups, seq):
+    shard = seq // (streams * groups)
+    return streams * shard if groups > 1 else shard
+
+
+def attention(x, weights, bias, docs, streams, groups, moves, moved, keep, collective_id, name):
+    seq, depth = x.shape
+    width = depth // groups
     pairs = width // 128
-    tile = 256
-    edge = 256
-    col = docs.reshape(seq, 1)
-    row = docs.reshape(1, seq)
-    blocks = [
-        pl.BlockSpec((tile, 128), lambda p, i: (i, p)),
-        pl.BlockSpec((seq, 128), lambda p, i: (0, pairs + p)),
-        pl.BlockSpec((seq, 128), lambda p, i: (0, 2 * pairs + p)),
-        pl.BlockSpec((tile, 1), lambda p, i: (i, 0)),
-        pl.BlockSpec((1, seq), lambda p, i: (0, 0)),
-    ] + moves.spaces()
-    outs = [pl.BlockSpec((tile, 128), lambda p, i: (i, p))]
-    shapes = [jax.ShapeDtypeStruct((seq, width), BF)]
+    tile = 512
+    owned = seq // groups
+    bag = Bag()
+    bag.add("k_aug", pltpu.VMEM((2, seq, 128), BF))
+    bag.add("v_aug", pltpu.VMEM((2, seq, 128), BF))
+    bag.add("ctx_all", pltpu.VMEM((pairs, seq, 128), BF))
+    bag.add("mask", pltpu.VMEM((1, seq), F32))
+    bag.add("edges", pltpu.VMEM((2, 256, 128), F32))
+    tiles = Tiles(bag, "tiles", groups, pairs, owned // tile)
+    for i, item in enumerate(moves.scratch()):
+        bag.add(f"moves{i}", item)
+
+    def constant(shape):
+        return pl.BlockSpec(shape, lambda p, i: (0,) * len(shape))
+
+    part = pl.BlockSpec((tile, 128), lambda p, i: (i, p))
+    whole = pl.BlockSpec((seq, 128), lambda p, i: (0, p))
+    any_space = pl.BlockSpec(memory_space=pl.ANY)
+    wide = jax.ShapeDtypeStruct((seq, width), BF)
+    outs = [whole, whole, any_space]
+    shapes = [wide, wide, jax.ShapeDtypeStruct((groups, pairs, owned, 128), BF)]
     if keep:
-        outs = [pl.BlockSpec((2, tile, seq), lambda p, i: (p, i, 0))] + outs
-        shapes = [jax.ShapeDtypeStruct((2 * pairs, seq, seq), BF)] + shapes
-        outs = outs + [pl.BlockSpec((tile, 128), lambda p, i: (i, p))]
-        shapes = shapes + [jax.ShapeDtypeStruct((seq, width), F32)]
+        outs += [
+            whole,
+            pl.BlockSpec((2, tile, seq), lambda p, i: (p, i, 0)),
+            part,
+            part,
+            constant((seq, depth)),
+        ]
+        shapes += [
+            wide,
+            jax.ShapeDtypeStruct((2 * pairs, seq, seq), BF),
+            wide,
+            jax.ShapeDtypeStruct((seq, width), F32),
+            jax.ShapeDtypeStruct((seq, depth), BF),
+        ]
     return pl.pallas_call(
-        functools.partial(forward_kernel, moves, keep, tile, edge),
+        functools.partial(forward_kernel, moves, keep, streams, groups, tile, bag, tiles),
         grid=(pairs, seq // tile),
-        in_specs=blocks,
+        in_specs=[constant(x.shape), constant(weights.shape), constant(bias.shape)]
+        + [constant((1, seq))]
+        + moves.spaces(),
         out_specs=outs + moves.spaces(),
         out_shape=shapes + moves.out_shapes(),
-        scratch_shapes=[pltpu.VMEM((2, seq, 128), BF), pltpu.VMEM((2, seq, 128), BF)]
-        + moves.scratch(),
+        scratch_shapes=list(bag.items.values()),
         compiler_params=remote_params(collective_id),
         name=name,
-    )(qkv, qkv, qkv, col, row, *moved)
+    )(x, weights, bias, docs, *moved)
 
 
 def split(matrix):
@@ -672,7 +776,6 @@
     groups,
     tile,
     bag,
-    back,
     early,
     late,
     e_ref,
@@ -684,20 +787,17 @@
     dc_ref,
     ctx_ref,
     inv_ref,
-    col_ref,
     row_ref,
-    bigc_ref,
     small_ref,
     active_hbm,
     bin_hbm,
     d1_hbm,
     tokens_hbm,
-    output_ref,
     *rest,
 ):
     n_early = sum(job.count for job in early)
     sources, rest = rest[:n_early], rest[n_early:]
-    output_back, grad_ref, *rest = rest
+    grad_ref, *rest = rest
     early_out, rest = rest[:n_early], rest[n_early:]
     late_out, (sum_ref, *rest) = rest[: len(late)], rest[len(late) :]
     have = bag.bind(rest)
@@ -707,7 +807,6 @@
         at += job.count
     for job, target in zip(late, late_out):
         job.bind(None, [target], have)
-    back_refs = (output_ref, output_back) + tuple(have[f"back{i}"] for i in range(4))
 
     pair, step = pl.program_id(0), pl.program_id(1)
     pairs, steps = len(late), q_ref.shape[0] // tile
@@ -723,6 +822,7 @@
     v_aug, dk_acc, dv_acc, grams = have["v_aug"], have["dk_acc"], have["dv_acc"], have["grams"]
     dq_all, d_act, active, weights = have["dq_all"], have["d_act"], have["active"], have["weights"]
     d_one, x_rows = have["d_one"], have["x_rows"]
+    edges, in_big = have["edges"], have["in_big"]
     along_z, cores, along_dp = stream_peers(streams, groups), core_peers(groups), dp_peers()
 
     def loads():
@@ -742,11 +842,27 @@
 
     def begin():
         greet(along_z + cores + along_dp)
-        back.first(*back_refs)
         for job in early:
             job.core_start()
         for copy in loads():
             copy.start()
+        ids = row_ref[...]
+        big_at = long_at(streams, groups, seq)
+        big = ids[:, big_at : big_at + 1]
+        for n, first in enumerate((0, seq - tile)):
+            column = jnp.broadcast_to(ids[:, first : first + tile], (128, tile)).T
+            edges[n] = column
+            in_big[n] = jnp.where(column == big, 1.0, 0.0)
+
+    def big_rows(ref):
+        return jnp.concatenate(
+            [
+                (ref[:tile, :].astype(F32) * in_big[0]).astype(BF),
+                ref[tile : seq - tile, :],
+                (ref[seq - tile :, :].astype(F32) * in_big[1]).astype(BF),
+            ],
+            axis=0,
+        )
 
     at_time(0, begin)
     unit = total_time / 16
@@ -767,11 +883,7 @@
         v_aug[1] = jnp.where(low, jnp.where(lane < 2, 1.0, 0.0), values).astype(BF)
         dk_acc[...] = jnp.zeros_like(dk_acc)
         dv_acc[...] = jnp.zeros_like(dv_acc)
-        in_big = bigc_ref[...] > 0.0
-        kb = jnp.where(in_big, k_ref[...].astype(F32), 0.0).astype(BF)
-        tkb = jnp.where(in_big, tk_ref[...].astype(F32), 0.0).astype(BF)
-        qb = jnp.where(in_big, q_ref[...].astype(F32), 0.0).astype(BF)
-        tqb = jnp.where(in_big, tq_ref[...].astype(F32), 0.0).astype(BF)
+        kb, tkb, qb, tqb = (big_rows(ref) for ref in (k_ref, tk_ref, q_ref, tq_ref))
         same_head = (lax.broadcasted_iota(jnp.int32, (128, 128), 0) < 64) == (
             lanes_of((128, 128)) < 64
         )
@@ -785,7 +897,7 @@
     low = lane < 64
 
     def body(whole, columns):
-        in_big = bigc_ref[rows_here, :] > 0.0
+        edge = 0 if whole and columns.start == 0 else 1
         q8 = q_ref[rows_here, :]
         tq8 = tq_ref[rows_here, :]
         dc = dc_ref[...].astype(F32)
@@ -812,8 +924,8 @@
                 q_mine = jnp.where(mine, q8, 0.0).astype(BF)
                 tq_mine = jnp.where(mine, tq8, 0.0).astype(BF)
                 gap = dot(q_mine, k_ref[columns, :], NT) - dot(tq_mine, tk_ref[columns, :], NT)
-                small = (col_ref[...] == row_ref[:, columns]) & jnp.logical_not(in_big)
-                gap = jnp.where(small, gap * share, 0.0)
+                same = jnp.where(edges[edge][:, :1] == row_ref[:, columns], share, 0.0)
+                gap = gap * (same * (1.0 - in_big[edge][:, :1]))
                 if columns.start == 0:
                     d_scores = jnp.concatenate(
                         [d_scores[:, :tile] + gap, d_scores[:, tile:]], axis=1
@@ -828,8 +940,10 @@
             dk_acc[half, :] += dot(q_turned[half, :], d_scores)
             dv_acc[half, :] += dot(dc_turned[half, :], numerators)
         d_query = jnp.where(low, d_queries[0], d_queries[1])
-        qb = jnp.where(in_big, q8.astype(F32), 0.0).astype(BF)
-        tqb = jnp.where(in_big, tq8.astype(F32), 0.0).astype(BF)
+        qb, tqb = q8, tq8
+        if whole:
+            qb = (q8.astype(F32) * in_big[edge]).astype(BF)
+            tqb = (tq8.astype(F32) * in_big[edge]).astype(BF)
         d_query += dot(qb, grams[0]) + dot(qb, grams[1]) - dot(tqb, grams[2]) - dot(tqb, grams[3])
         dq_all[rows_here, :] = (d_query * 0.125).astype(BF)
 
@@ -847,9 +961,7 @@
 
     def pair_end(p):
         job = late[p]
-        in_big = bigc_ref[...] > 0.0
-        kb = jnp.where(in_big, k_ref[...].astype(F32), 0.0).astype(BF)
-        tkb = jnp.where(in_big, tk_ref[...].astype(F32), 0.0).astype(BF)
+        kb, tkb = big_rows(k_ref), big_rows(tk_ref)
         d_key = dk_acc[...].T
         d_key += dot(kb, grams[4]) + dot(kb, grams[5]) - dot(tkb, grams[6]) - dot(tkb, grams[7])
         d_value = dv_acc[...].T.astype(BF)
@@ -859,7 +971,7 @@
             for copy in loads():
                 copy.wait()
         columns = slice(p * 128, (p + 1) * 128)
-        bins = jnp.concatenate([weights[i, :, columns] for i in range(3)], axis=1)
+        bins = jnp.concatenate([weights[0, i, :, columns] for i in range(3)], axis=1)
         if p == 0:
             d_act[...] = dot(d_pair, bins, NT)
         else:
@@ -975,7 +1087,6 @@
         last.dp_back()
         sum_ref[...] = small_sum(2, cores, size + streams)
         last.core_back()
-        back.last(*back_refs)
         for copy in back_copies:
             copy.wait()
         for job in early + late:
@@ -997,24 +1108,24 @@
     streams,
     groups,
     numerators,
-    qkv,
-    teacher_qkv,
+    queries,
+    keys,
+    values,
+    teacher_queries,
+    teacher_keys,
     d_context,
     context,
     inverse,
     docs,
-    in_big,
     small,
     active,
     bin_own,
     d_one,
     tokens,
-    output,
     early_arrays,
     collective_id,
 ):
-    seq, width3 = qkv.shape
-    width = width3 // 3
+    seq, width = queries.shape
     pairs = width // 128
     tile = 256
     rows, depth = d_one.shape
@@ -1028,7 +1139,7 @@
     bag.add("dq_all", pltpu.VMEM((seq, 128), BF))
     bag.add("d_act", pltpu.VMEM((seq, depth), F32))
     bag.add("active", pltpu.VMEM((seq, depth), BF))
-    bag.add("weights", pltpu.VMEM((3, depth, width), BF))
+    bag.add("weights", pltpu.VMEM((1, 3, depth, width), BF))
     bag.add("d_one", pltpu.VMEM((rows, depth), F32))
     bag.add("x_rows", pltpu.VMEM((streams, shard, depth), BF))
     bag.add("load", dma(4))
@@ -1045,9 +1156,8 @@
     bag.add("small_box", pltpu.VMEM((count,) + small.shape, F32))
     bag.add("small_s", dma(count))
     bag.add("small_r", dma(count))
-    back = Swap(streams, groups, (shard, depth), BF)
-    for i, item in enumerate(back.scratch()):
-        bag.add(f"back{i}", item)
+    bag.add("edges", pltpu.VMEM((2, tile, 128), F32))
+    bag.add("in_big", pltpu.VMEM((2, tile, 128), F32))
     early, flat = [], []
     for n, arrays in enumerate(early_arrays):
         job = Reduce(bag, f"early{n}", streams, groups, [a.shape for a in arrays], True)
@@ -1061,8 +1171,7 @@
     part = pl.BlockSpec((tile, 128), lambda p, i: (i, p))
     any_space = pl.BlockSpec(memory_space=pl.ANY)
 
-    def whole(which):
-        return pl.BlockSpec((seq, 128), lambda p, i: (0, which * pairs + p))
+    whole = pl.BlockSpec((seq, 128), lambda p, i: (0, p))
 
     def constant(shape):
         return pl.BlockSpec(shape, lambda p, i: (0,) * len(shape))
@@ -1070,27 +1179,25 @@
     early_shapes = [shape for job in early for shape in job.out_shapes()]
     late_shapes = [shape for job in late for shape in job.out_shapes()]
     results = pl.pallas_call(
-        functools.partial(backward_kernel, streams, groups, tile, bag, back, early, late),
+        functools.partial(backward_kernel, streams, groups, tile, bag, early, late),
         grid=(pairs, seq // tile),
         in_specs=[
             pl.BlockSpec((2, tile, seq), lambda p, i: (p, i, 0)),
-            whole(0),
-            whole(1),
-            whole(2),
-            whole(0),
-            whole(1),
+            whole,
+            whole,
+            whole,
+            whole,
+            whole,
             part,
             part,
             part,
-            pl.BlockSpec((tile, 1), lambda p, i: (i, 0)),
             constant((1, seq)),
-            constant((seq, 1)),
             constant(small.shape),
         ]
-        + [any_space] * (5 + len(flat)),
-        out_specs=[any_space] * (2 + len(early_shapes) + len(late_shapes))
+        + [any_space] * (4 + len(flat)),
+        out_specs=[any_space] * (1 + len(early_shapes) + len(late_shapes))
         + [constant(small.shape)],
-        out_shape=[back.out_shape(), jax.ShapeDtypeStruct((streams, shard, depth), BF)]
+        out_shape=[jax.ShapeDtypeStruct((streams, shard, depth), BF)]
         + early_shapes
         + late_shapes
         + [jax.ShapeDtypeStruct(small.shape, F32)],
@@ -1099,31 +1206,27 @@
         name="attention_back",
     )(
         numerators,
-        qkv,
-        qkv,
-        qkv,
-        teacher_qkv,
-        teacher_qkv,
+        queries,
+        keys,
+        values,
+        teacher_queries,
+        teacher_keys,
         d_context,
         context,
         inverse,
-        docs.reshape(seq, 1),
-        docs.reshape(1, seq),
-        in_big.astype(F32).reshape(seq, 1),
+        docs,
         small,
         active,
         bin_own,
         d_one,
         tokens,
-        output,
         *flat,
     )
-    output_back, grad_tokens, *rest = results
+    grad_tokens, *rest = results
     early_sums = rest[: len(flat)]
     late_sums = rest[len(flat) : -1]
     shapes = [a.shape for arrays in early_arrays for a in arrays]
     return (
-        output_back,
         grad_tokens,
         [e.reshape(shape) for e, shape in zip(early_sums, shapes)],
         [l.reshape(groups, depth, 3 * 128) for l in late_sums],
@@ -1132,7 +1235,10 @@
 
 
 def middle_kernel(
-    unused_place,
+    streams,
+    groups,
+    bag,
+    tiles,
     x_ref,
     tx_ref,
     cot_ref,
@@ -1159,13 +1265,25 @@
     ggain_ref,
     gbias_ref,
     gub_ref,
-    gout_acc,
-    gup_acc,
-    gdown_acc,
+    *rest,
 ):
+    have = bag.bind(rest)
+    gout_acc, gup_acc, gdown_acc = have["gout"], have["gup"], have["gdown"]
+    out_box, d_box = have["out_box"], have["d_box"]
     step = pl.program_id(0)
-    groups = ctx_ref.shape[0]
-    width = ctx_ref.shape[2]
+    steps = pl.num_programs(0)
+    width = ctx_ref.shape[1] * 128
+    tile, depth = cot_ref.shape
+    n_steps = out_box.shape[0]
+    shard = n_steps * tile // streams
+    s, r = place(groups)
+    along_z = stream_peers(streams, groups)
+    turned = row_tile(step, n_steps, streams, groups)
+    start = pl.multiple_of(turned * tile, tile)
+
+    @pl.when(step == 0)
+    def _():
+        greet(along_z + core_peers(groups))
 
     @pl.when(step == 0)
     def _():
@@ -1175,7 +1293,8 @@
     def row(ref, i):
         return ref[i : i + 1, :]
 
-    tctx = jnp.concatenate([tctx_ref[j] for j in range(groups)], axis=1)
+    pieces = [(j, p) for j in range(groups) for p in range(ctx_ref.shape[1])]
+    tctx = jnp.concatenate([tctx_ref[j, p] for j, p in pieces], axis=1)
     t_att = dot(tctx, to_ref[...]) + row(tb_ref, 2)
     t_hidden = layer_norm(tx_ref[...].astype(F32) + t_att, row(tg_ref, 0), row(tb_ref, 3))[0]
     t_inner = gelu_parts(dot(t_hidden.astype(BF), tup_ref[...]) + tub_ref[...])[0]
@@ -1185,7 +1304,7 @@
         row(tb_ref, 5),
     )[0]
 
-    context = jnp.concatenate([ctx_ref[j] for j in range(groups)], axis=1).astype(F32)
+    context = jnp.concatenate([ctx_ref[j, p] for j, p in pieces], axis=1).astype(F32)
     bent = jnp.tanh(context * (1.0 / clip_level))
     ctx_active = (clip_level * bent).astype(BF)
     ctx_slope = 1.0 - bent * bent
@@ -1205,7 +1324,26 @@
     )
     branch = dot(inner_active, bdown_ref[...]) + row(sb_ref, 4)
     output, normed_two, inverse_two = layer_norm(hidden + branch, row(sg_ref, 1), row(sb_ref, 5))
-    out_ref[...] = output.astype(BF)
+    out_box[step] = output.astype(BF)
+    per_tile = tile // shard
+    for n in range(per_tile):
+        block = turned * per_tile + n
+        source = out_box.at[step, pl.ds(n * shard, shard)]
+
+        @pl.when(block == s)
+        def _():
+            pltpu.make_async_copy(source, out_ref.at[s], have["out_s"].at[s]).start()
+
+        @pl.when(block != s)
+        def _():
+            remote(
+                source,
+                out_ref.at[s],
+                have["out_s"].at[block],
+                have["out_r"].at[s],
+                {"blk": block * groups + r},
+            ).start()
+
     upstream = cot_ref[...].astype(F32) + 0.5 * (output - t_out)
     d_two = norm_back(upstream, row(sg_ref, 1), normed_two, inverse_two)
     d_branch = d_two.astype(BF)
@@ -1218,8 +1356,19 @@
     d_attended = d_one.astype(BF)
     gout_acc[...] += dot(ctx_active, d_attended, TN)
     d_context = (dot(d_attended, bo_ref[...], NT) * ctx_slope).astype(BF)
+    place_rows = pl.ds(pl.multiple_of(r * n_steps * tile + start, tile), tile)
     for j in range(groups):
-        dctx_ref[j] = d_context[:, j * width : (j + 1) * width]
+        d_box[step, j] = d_context[:, j * width : (j + 1) * width]
+        piece, target = d_box.at[step, j], dctx_ref.at[place_rows]
+
+        @pl.when(r == j)
+        def _():
+            tiles.own(have, piece, target, 0, step).start()
+
+        @pl.when(r != j)
+        def _():
+            tiles.copy(have, piece, target, j, 0, step).start()
+
 
     def total(value):
         return jnp.sum(value, axis=0, keepdims=True)
@@ -1232,49 +1381,74 @@
     gbias_ref[5:6, :] += total(upstream)
     gub_ref[...] += total(d_inner.astype(F32))
 
-    @pl.when(step == pl.num_programs(0) - 1)
+    @pl.when(step == steps - 1)
     def _():
+        tiles.finish(have, d_box.at[0, 0], dctx_ref.at[place_rows])
+        source = out_box.at[0, pl.ds(0, shard)]
+        pltpu.make_async_copy(source, out_ref.at[s], have["out_s"].at[s]).wait()
+        for d, peer in enumerate(along_z, 1):
+            block = lax.rem(s + d, streams)
+            remote(
+                source, out_ref.at[block], have["out_s"].at[block], have["out_r"].at[block], peer
+            ).wait()
         gout_ref[...] = gout_acc[...].astype(BF)
         gup_ref[...] = gup_acc[...].astype(BF)
         gdown_ref[...] = gdown_acc[...].astype(BF)
 
 
-def middle(r, x, tx, cot, ctx, tctx, weights, teacher_weights, vectors):
+def row_tile(step, steps, streams, groups):
+    s, r = place(groups)
+    return lax.rem(s // (streams // steps) + 1 + step, steps)
+
+
+def middle(streams, groups, x, tx, cot, ctx, tctx, weights, teacher_weights, vectors, collective_id):
     rows, depth = cot.shape
     ff = weights[1].shape[1]
     tile = min(256, rows)
-    groups, unused, width = ctx.shape
+    pairs = ctx.shape[1]
+    width = pairs * 128
     steps = rows // tile
-    tall = pl.BlockSpec((tile, depth), lambda i, r: (i, 0))
-    of_stream = pl.BlockSpec((tile, depth), lambda i, r: (r[0] * steps + i, 0))
-    split_rows = pl.BlockSpec((groups, tile, width), lambda i, r: (0, i, 0))
+    shard = rows // streams
+
+    def turn(i):
+        return row_tile(i, steps, streams, groups)
+
+    def stream_tile(i):
+        return lax.rem(lax.axis_index("blk"), groups) * steps + turn(i)
+
+    tall = pl.BlockSpec((tile, depth), lambda i: (turn(i), 0))
+    of_stream = pl.BlockSpec((tile, depth), lambda i: (stream_tile(i), 0))
+    split_rows = pl.BlockSpec((groups, pairs, tile, 128), lambda i: (0, 0, turn(i), 0))
+    any_space = pl.BlockSpec(memory_space=pl.ANY)
 
     def full(shape):
-        return pl.BlockSpec(shape, lambda i, r: (0,) * len(shape))
-
-    def full_of(array):
-        return full(array.shape)
+        return pl.BlockSpec(shape, lambda i: (0,) * len(shape))
 
     out_full = [(depth, depth), (depth, ff), (ff, depth), (2, depth), (6, depth), (1, ff)]
+    bag = Bag()
+    for name, shape in zip(("gout", "gup", "gdown"), out_full):
+        bag.add(name, pltpu.VMEM(shape, F32))
+    bag.add("out_box", pltpu.VMEM((steps, tile, depth), BF))
+    bag.add("d_box", pltpu.VMEM((steps, groups, tile, width), BF))
+    bag.add("out_s", dma(streams))
+    bag.add("out_r", dma(streams))
+    tiles = Tiles(bag, "tiles", groups, 1, steps)
     return pl.pallas_call(
-        middle_kernel,
-        grid_spec=pltpu.PrefetchScalarGridSpec(
-            num_scalar_prefetch=1,
-            grid=(steps,),
-            in_specs=[of_stream, of_stream, tall, split_rows, split_rows]
-            + [full_of(a) for a in weights + teacher_weights + vectors],
-            out_specs=[tall, tall, split_rows] + [full(s) for s in out_full],
-            scratch_shapes=[pltpu.VMEM(s, F32) for s in out_full[:3]],
-        ),
+        functools.partial(middle_kernel, streams, groups, bag, tiles),
+        grid=(steps,),
+        in_specs=[of_stream, of_stream, tall, split_rows, split_rows]
+        + [full(a.shape) for a in weights + teacher_weights + vectors],
+        out_specs=[any_space, tall, any_space] + [full(s) for s in out_full],
         out_shape=[
-            jax.ShapeDtypeStruct((rows, depth), BF),
+            jax.ShapeDtypeStruct((streams, shard, depth), BF),
             jax.ShapeDtypeStruct((rows, depth), F32),
-            jax.ShapeDtypeStruct((groups, rows, width), BF),
+            jax.ShapeDtypeStruct((rows * groups, width), BF),
         ]
         + [jax.ShapeDtypeStruct(s, BF if i < 3 else F32) for i, s in enumerate(out_full)],
-        compiler_params=pltpu.CompilerParams(vmem_limit_bytes=VMEM_BYTES),
+        scratch_shapes=list(bag.items.values()),
+        compiler_params=remote_params(collective_id),
         name="middle",
-    )(r.reshape(1), x, tx, cot, ctx, tctx, *weights, *teacher_weights, *vectors)
+    )(x, tx, cot, ctx, tctx, *weights, *teacher_weights, *vectors)
 
 
 def latent_columns(latent, binary_grad):
@@ -1358,80 +1532,64 @@
     groups = blocks // streams
     seq = shard_len * blocks
     rows = seq // groups
-    width = depth // groups
-    s, r = place(groups)
     block = (shard_len, depth)
     gather, swap = Gather(streams, groups, block, BF), Swap(streams, groups, block, BF)
-    row_block = (rows, width)
-    by_rows = Rows(streams, groups, row_block, BF)
     doc_block = (shard_len // 128, 128)
-
-    def own_columns(matrices):
-        return lax.dynamic_slice_in_dim(matrices, r * width, width, axis=2)
-
-    def own_bias(bias):
-        return lax.dynamic_slice_in_dim(bias, r * width, width, axis=1)
-
-    latents = [own_columns(latent_qkv), latent_out, latent_up, latent_down]
-    taken = [
-        tokens,
-        segment_ids.reshape((streams,) + doc_block),
-        teacher_qkv,
-        teacher_out,
-    ]
-    bin_own, bin_out, bin_up, bin_down, token_blocks, docs, qkv_parts, out_parts = intake(
+    bin_own, bin_out, bin_up, bin_down, token_blocks, docs, qkv_parts = intake(
         Moves(
             gather,
             Gather(streams, groups, doc_block, jnp.int32),
             Spread(teacher_qkv.shape, BF),
-            Spread(teacher_out.shape, BF),
         ),
-        latents,
-        taken,
+        groups,
+        [latent_qkv, latent_out, latent_up, latent_down],
+        [tokens, segment_ids.reshape((streams,) + doc_block), teacher_qkv],
         1,
     )
-    docs = docs.reshape(seq)
-    big = docs[streams * shard_len] if groups > 1 else docs[shard_len]
-    in_big = docs == big
+    docs = docs.reshape(1, seq).astype(F32)
     stream_tokens = token_blocks.reshape(seq, depth)
-
-    def project(rows_in, matrices, bias):
-        q = dot(rows_in, matrices[0]) + own_bias(bias)[0]
-        k = dot(rows_in, matrices[1])
-        v = dot(rows_in, matrices[2]) + own_bias(bias)[1]
-        return jnp.concatenate(
-            [(q.astype(BF).astype(F32) * 0.125).astype(BF), k.astype(BF), v.astype(BF)], axis=1
-        )
-
-    active = squash(stream_tokens.astype(F32)).astype(BF)
-    qkv = project(active, bin_own, student_bias)
-    numerators, context, inverse, teacher_blocks, up_parts = attention(
-        qkv,
+    (
+        queries,
+        keys,
+        ctx_rows,
+        values,
+        numerators,
+        context,
+        inverse,
+        active,
+        teacher_blocks,
+        up_parts,
+        out_parts,
+    ) = attention(
+        stream_tokens,
+        bin_own,
+        student_bias,
         docs,
-        Moves(gather, Spread(teacher_up.shape, BF)),
-        [teacher_tokens, teacher_up],
+        streams,
+        groups,
+        Moves(gather, Spread(teacher_up.shape, BF), Spread(teacher_out.shape, BF)),
+        [teacher_tokens, teacher_up, teacher_out],
         True,
         2,
         "attention_student",
     )
     teacher_stream = teacher_blocks.reshape(seq, depth)
-    full_qkv = own_columns(qkv_parts.transpose(1, 0, 2, 3).reshape(3, depth, depth))
-    teacher_own = project(teacher_stream, full_qkv, teacher_bias)
-    row_shape = (groups,) + row_block
-    teacher_context, cot_blocks, down_parts, ctx_rows = attention(
-        teacher_own,
+    teacher_queries, teacher_keys, tctx_rows, cot_blocks, down_parts = attention(
+        teacher_stream,
+        qkv_parts,
+        teacher_bias,
         docs,
-        Moves(swap, Spread(teacher_down.shape, BF), by_rows),
-        [cotangent, teacher_down, context.reshape(row_shape)],
+        streams,
+        groups,
+        Moves(swap, Spread(teacher_down.shape, BF), others=[gather]),
+        [cotangent, teacher_down],
         False,
         3,
         "attention_teacher",
     )
-    (tctx_rows,) = move(
-        Moves(by_rows), [teacher_context.reshape(row_shape)], 4, "teacher_context_rows"
-    )
     output, d_one, d_context, g_out, g_up, g_down, g_gain, g_bias, g_ub = middle(
-        r,
+        streams,
+        groups,
         stream_tokens,
         teacher_stream,
         cot_blocks.reshape(rows, depth),
@@ -1451,30 +1609,31 @@
             teacher_bias,
             teacher_up_bias.reshape(1, -1),
         ],
+        4,
     )
     small = jnp.concatenate(
         [g_gain, g_bias, g_ub.reshape(-1, depth), jnp.zeros((4, depth), F32)], axis=0
     )
-    (d_ctx_rows,) = move(Moves(by_rows), [d_context], 5, "d_context_rows")
     grads = [[g_up], [g_down, g_out]]
     in_kernel = depth % (16 * blocks * lax.axis_size("dp")) == 0
-    output_blocks, grad_tokens, early, late, small = attention_back(
+    grad_tokens, early, late, small = attention_back(
         streams,
         groups,
         numerators,
-        qkv,
-        teacher_own,
-        d_ctx_rows.reshape(seq, width),
+        queries,
+        keys,
+        values,
+        teacher_queries,
+        teacher_keys,
+        d_context,
         context,
         inverse,
         docs,
-        in_big,
         small,
         active,
         bin_own,
         d_one,
         token_blocks,
-        output.reshape(streams, shard_len, depth),
         grads if in_kernel else [],
         6,
     )
@@ -1485,7 +1644,7 @@
         [latent_out, latent_up, latent_down], [early[2], early[0], early[1]]
     )
     return (
-        output_blocks,
+        output,
         grad_tokens,
         late_latents(latent_qkv, late),
         grad_out,

time: 336 us -> 310 us (0.923); the launches traced: 331 us -> 312 us
  other arithmetic: 12.7 us -> 4.07 us
  local copies, waits for them, and re-layouts: 13.3 us -> 5.65 us
  matrix products: 6.28 us -> 0 us
  Pallas kernels: 297 us -> 302 us
    pallas_call x6 -> x4, Pallas kernels: 165 us -> 171 us  [the longest x2 92.8 us: attention(): pl.pallas_call(functools.partial(forward_kernel, moves, keep, streams, gr...]
    dot_general x6 -> x0, matrix products: 6.28 us -> none  [dot(): return lax.dot_general(a, b, dims, preferred_element_type=F32)]
    convert_element_type x3 -> x1, other arithmetic: 6.19 us -> 1.3 us  [shards(): docs = docs.reshape(1, seq).astype(F32)]
    concatenate x2 -> x0, other arithmetic: 3.75 us -> none  [project(): jnp.concatenate([(q.astype(BF).astype(F32) * 0.125).astype(BF), k.astype(...]
where the time goes in v4:
time: 310 us; the launch traced here: 312 us
  Pallas kernels  302 us (97%)
  local copies, waits for them, and re-layouts  5.65 us (2%)
  other arithmetic  4.07 us (1%)
    pallas_call x1, Pallas kernels, attention_back(): pl.pallas_call(functools.partial(backward_kernel, streams, groups, tile,...  112 us
    pallas_call x2, Pallas kernels, attention(): pl.pallas_call(functools.partial(forward_kernel, moves, keep, streams, gr...  92.8 us
    pallas_call x1, Pallas kernels, middle(): pl.pallas_call(functools.partial(middle_kernel, streams, groups, bag, til...  41 us
    pallas_call x1, Pallas kernels, intake(): pl.pallas_call(functools.partial(intake_kernel, moves, groups), out_shape...  37.5 us
    pallas_call x1, Pallas kernels, early_latents(): pl.pallas_call(early_latents_kernel, grid=(steps,), in_specs=specs * 2, o...  12 us
    pallas_call x1, Pallas kernels, late_latents(): pl.pallas_call(functools.partial(late_latents_kernel, pairs), grid=(3, gr...  6.2 us

profile of v4, /device:TPU:0, one launch (start us, length us, event | category | flops | bytes accessed | tf_op | source)
XLA Modules:
  0.0 312.4 jit_solution(7295247421876959559)
XLA Ops:
  0.6 1.3 reshape.89.refs_1_
  1.9 37.5 %intake.1 = (bf16[1,3,512,256]{3,2,1,0:T(8,128)(2,1)}, bf16[512,512]{1,0:T(8,128)(2,1)}, bf16[512,2048]{1,0:T(8,128)(2,1)}, bf16[2048,512]{1,0:T(8,128)(2,1)}, b...) custom-call(bf16[3,512,512]{2,1,0:T(8,128)(2,1)} %latent.1, ...), custom_call_target="tpu_custom_call" | custom-call | tf_op jit(solution)/shard_map/intake/pallas_call | solution.py:539
  39.4 1.3 convert_element_type.5
  40.7 44.2 %attention_student.1 = (bf16[2048,256]{1,0:T(8,128)(2,1)}, bf16[2048,256]{1,0:T(8,128)(2,1)}, bf16[2,2,1024,128]{3,2,1,0:T(8,128)(2,1)}, bf16[2048,256]{1,0:T(8,...) custom-call(bf16[2048,512]{1,0:T(8,128)(2,1)} %bitcast.20, ...), custom_call_target="tpu_custom_call" | custom-call | tf_op jit(solution)/shard_map/attention_student/pallas_call | solution.py:755
  84.9 48.7 %attention_teacher.1 = (bf16[2048,256]{1,0:T(8,128)(2,1)}, bf16[2048,256]{1,0:T(8,128)(2,1)}, bf16[2,2,1024,128]{3,2,1,0:T(8,128)(2,1)}, bf16[4,256,512]{2,1,0:T(8,128)(2,1)}, bf16[4,512,512]{2,1,0:T(8,128)(2,1)}) custom-call(bf16[2048,512]{1,0:T(8,128)(2,1)} %bitcast.22, bf16[4,3,128,512]{3,2,1,0:T(8,128)(2,1)} %get-tuple-element.55.w_ref, ...), custom_call_target="tpu_custom_call" | custom-call | tf_op jit(solution)/shard_map/attention_teacher/pallas_call | solution.py:755
  133.6 41.0 %middle.1 = (bf16[4,256,512]{2,1,0:T(8,128)(2,1)}, f32[1024,512]{1,0:T(8,128)}, bf16[2048,256]{1,0:T(8,128)(2,1)}, bf16[512,512]{1,0:T(8,128)(2,1)}, bf16[512,20...) custom-call(bf16[2048,512]{1,0:T(8,128)(2,1)} %bitcast.21, ...), custom_call_target="tpu_custom_call" | custom-call | tf_op jit(solution)/shard_map/middle/pallas_call | solution.py:1436
  174.6 0.5 broadcast.5
  175.1 1.4 reduce.3
  176.5 0.1 pad.3.clone
  176.6 1.4 maximum_maximum_fusion.small_ref
  178.0 112.3 %attention_back.1 = (bf16[4,256,512]{2,1,0:T(8,128)(2,1)}, bf16[2,4,4,16,2048]{4,3,2,1,0:T(8,128)(2,1)}, bf16[2,4,4,64,512]{4,3,2,1,0:T(8,128)(2,1)}, bf16[2,4,4...) custom-call(bf16[4,2048,2048]{2,1,0:T(8,128)(2,1)} %get-tuple-elemen, ...), custom_call_target="tpu_custom_call" | custom-call | tf_op jit(solution)/shard_map/attention_back/pallas_call | solution.py:1181
  290.3 12.0 %early_latents.1 = (f32[512,512]{1,0:T(8,128)}, f32[512,2048]{1,0:T(8,128)}, f32[2048,512]{1,0:T(8,128)}) custom-call(bf16[512,512]{1,0:T(8,128)(2,1)} %lo.1, bf16[512,2048]{1,0:T(8,128)(2,1)} %lu.1, bf16[2048,512]{1,0:T(8,128)(2,1)} %ld.1, bf16[512,512]{1,0:T(8,128)(2,1)} %bitcast.35, bf16[512,2048]{1,0:T(8,128)(2,1)} %bitcast.28, bf16[2048,512]{1,0:T(8,128)(2,1)} %bitcast.29), custom_call_target="tpu_custom_call" | custom-call | tf_op jit(solution)/shard_map/early_latents/pallas_call | solution.py:1477
  302.3 0.0 copy-start.2
  302.3 0.0 copy-start
  302.3 6.2 %late_latents.1 = f32[3,512,512]{2,1,0:T(8,128)} custom-call(bf16[3,512,512]{2,1,0:T(8,128)(2,1)} %latent.1, bf16[2,512,384]{2,1,0:T(8,128)(2,1)} %bitcast.31, bf16[2,512,384]{2,1,0:T(8,128)(2,1)} %bitcast.32), custom_call_target="tpu_custom_call" | custom-call | tf_op jit(solution)/shard_map/late_latents/pallas_call | solution.py:1499
  308.5 0.0 copy-start.1
  308.5 0.0 copy-done.2
  308.5 0.6 copy.27
  309.1 0.6 slice.10
  309.7 0.6 slice.9
  310.3 0.0 copy-done
  310.3 1.0 copy.30
  311.3 0.0 copy-done.1
  311.3 1.0 copy.31
  (3 shorter events, 0.0 us)
Async XLA Ops:
  302.3 6.2 %copy-start.2 = (f32[16,512]{1,0:T(8,128)S(1)}, f32[16,512]{1,0:T(8,128)}, u32[]{:S(2)}) copy-start(f32[16,512]{1,0:T(8,128)} %get-tuple-element.92) | copy-start | bytes 98308
  302.3 8.0 %copy-start = (bf16[4,256,512]{2,1,0:T(8,128)(2,1)S(1)}, bf16[4,256,512]{2,1,0:T(8,128)(2,1)}, u32[]{:S(2)}) copy-start(bf16[4,256,512]{2,1,0:T(8,128)(2,1)} %get-tuple-element.102) | copy-start | bytes 3145732
  308.5 2.8 copy-start.1

commit v5 on v4

--- a/solution.py
+++ b/solution.py
@@ -181,13 +181,16 @@
         for copy in shares[0]:
             copy.start()
 
-    def last(self, *refs):
+    def middle(self, *refs):
         swaps, shares, own = self.parts(*refs)
-        own.last()
         for d in [1, 3, 2] if self.streams == 4 else range(1, self.streams):
             swaps[d - 1].wait_recv()
             for copy in shares[d]:
                 copy.start()
+
+    def last(self, *refs):
+        swaps, shares, own = self.parts(*refs)
+        own.last()
         for row in shares:
             for copy in row:
                 copy.wait()
@@ -311,10 +314,11 @@
 
 
 class Reduce:
-    def __init__(self, bag, name, streams, groups, shapes, over_cores):
+    def __init__(self, bag, name, streams, groups, shapes, over_cores, two_step):
         self.name, self.streams, self.groups = name, streams, groups
         self.size = lax.axis_size("dp")
         self.over_cores = over_cores
+        self.two_step = two_step and self.size == 4 and streams % 2 == 0
         self.count = len(shapes)
         share = self.size * (groups if over_cores else 1)
         self.shapes = [(rows // share, cols) for rows, cols in shapes]
@@ -324,18 +328,29 @@
             bag.add(f"{name}half{i}", pltpu.VMEM((self.size, chunk, cols), wire))
             if over_cores:
                 bag.add(f"{name}core{i}", pltpu.VMEM((groups - 1, self.size, chunk, cols), wire))
-            bag.add(f"{name}dp{i}", pltpu.VMEM((self.size - 1, chunk, cols), wire))
+            if self.two_step:
+                bag.add(f"{name}first{i}", pltpu.VMEM((4, chunk // 2, cols), wire))
+                bag.add(f"{name}second{i}", pltpu.VMEM((2, chunk // 2, cols), wire))
+            else:
+                bag.add(f"{name}dp{i}", pltpu.VMEM((self.size - 1, chunk, cols), wire))
             bag.add(f"{name}cut{i}", pltpu.VMEM((streams, slim, cols), wire))
             bag.add(f"{name}z{i}", pltpu.VMEM((streams - 1, slim, cols), wire))
             bag.add(f"{name}fin{i}", pltpu.VMEM((slim, cols), wire))
-            for kind, n in self.sem_counts().items():
-                bag.add(f"{name}{kind}s{i}", dma(n))
-                bag.add(f"{name}{kind}r{i}", dma(n))
+            for kind in self.kinds():
+                bag.add(f"{name}{kind}s{i}", dma(self.sem_count(kind)))
+                bag.add(f"{name}{kind}r{i}", dma(self.sem_count(kind)))
             bag.add(f"{name}local{i}", dma(2))
 
-    def sem_counts(self):
-        b, g, d = self.streams, self.groups, self.size
-        return {"a": g, "b": d, "c": b, "d": b, "e": d, "f": g}
+    def kinds(self):
+        along = ["b1", "b2", "c", "d", "e1", "e2"] if self.two_step else ["b", "c", "d", "e"]
+        return (["a"] if self.over_cores else []) + along + ["f"]
+
+    def sem_count(self, kind):
+        if kind in ("a", "f"):
+            return self.groups
+        if kind in ("c", "d"):
+            return self.streams
+        return max(self.size, 4)
 
     def out_shapes(self):
         return [
@@ -351,34 +366,59 @@
     def get(self, what, i):
         return self.scratch[f"{self.name}{what}{i}"]
 
-    def copies(self, kind, i):
+    def pairs(self, kind, i):
         s, r = place(self.groups)
         here = lax.axis_index("dp")
         b, g, size = self.streams, self.groups, self.size
+        x, y = lax.rem(here, 2), here // 2
+        beside_x, beside_y = {"dp": 2 * y + 1 - x}, {"dp": 2 * (1 - y) + x}
+        if kind == "a":
+            for d, peer in enumerate(core_peers(g), 1):
+                yield d, self.sources[i].at[lax.rem(r + d, g)], self.get("core", i).at[d - 1], peer
+        elif kind == "b":
+            half, box = self.get("half", i), self.get("dp", i)
+            for d, peer in enumerate(dp_peers(), 1):
+                yield d, half.at[lax.rem(here + d, size)], box.at[d - 1], peer
+        elif kind == "b1":
+            half, box, h = self.get("half", i), self.get("first", i), self.shapes[i][0] // 2
+            for n in range(2):
+                yield n, half.at[2 * n + 1 - x, pl.ds(0, h)], box.at[n], beside_x
+                yield 2 + n, half.at[2 * (1 - y) + n, pl.ds(h, h)], box.at[2 + n], beside_y
+        elif kind == "b2":
+            half, box, h = self.get("half", i), self.get("second", i), self.shapes[i][0] // 2
+            yield 0, half.at[2 * (1 - y) + x, pl.ds(0, h)], box.at[0], beside_y
+            yield 1, half.at[2 * y + 1 - x, pl.ds(h, h)], box.at[1], beside_x
+        elif kind in "cd":
+            peers = list(enumerate(stream_peers(b, g), 1))
+            for d, peer in [peers[1], peers[0], peers[2]] if b == 4 else peers:
+                if kind == "c":
+                    cut = self.get("cut", i)
+                    yield d, cut.at[lax.rem(s + d, b)], self.get("z", i).at[d - 1], peer
+                else:
+                    yield d, self.get("fin", i), self.targets[i].at[r, here, s], peer
+        elif kind == "e":
+            whole = self.targets[i].at[r, here]
+            for d, peer in enumerate(dp_peers(), 1):
+                yield d, whole, whole, peer
+        elif kind == "e1":
+            for n, peer in enumerate((beside_y, beside_x)):
+                part = self.targets[i].at[r, here, pl.ds(n * b // 2, b // 2)]
+                yield n, part, part, peer
+        elif kind == "e2":
+            for n in range(2):
+                part = self.targets[i].at[r, 2 * n + x, pl.ds(0, b // 2)]
+                yield n, part, part, beside_x
+                part = self.targets[i].at[r, 2 * y + n, pl.ds(b // 2, b // 2)]
+                yield 2 + n, part, part, beside_y
+        else:
+            whole = self.targets[i].at[r]
+            for d, peer in enumerate(core_peers(g), 1):
+                yield d, whole, whole, peer
+
+    def copies(self, kind, i):
         send, recv = self.get(kind + "s", i), self.get(kind + "r", i)
-        if kind in "af":
-            peers = core_peers(g)
-        elif kind in "be":
-            peers = dp_peers()
-        else:
-            peers = stream_peers(b, g)
-        order = list(enumerate(peers, 1))
-        if kind in "cd" and b == 4:
-            order = [order[1], order[0], order[2]]
-        for d, peer in order:
-            if kind == "a":
-                pair = self.sources[i].at[lax.rem(r + d, g)], self.get("core", i).at[d - 1]
-            elif kind == "b":
-                pair = self.get("half", i).at[lax.rem(here + d, size)], self.get("dp", i).at[d - 1]
-            elif kind == "c":
-                pair = self.get("cut", i).at[lax.rem(s + d, b)], self.get("z", i).at[d - 1]
-            elif kind == "d":
-                pair = self.get("fin", i), self.targets[i].at[r, here, s]
-            elif kind == "e":
-                pair = self.targets[i].at[r, here], self.targets[i].at[r, here]
-            else:
-                pair = self.targets[i].at[r], self.targets[i].at[r]
-            yield remote(*pair, send.at[d], recv.at[d], peer)
+        for n, source, target, peer in self.pairs(kind, i):
+            yield remote(source, target, send.at[n], recv.at[n], peer)
 
     def start(self, kind, i):
         for copy in self.copies(kind, i):
@@ -401,6 +441,11 @@
             self.targets[i].at[r, lax.axis_index("dp"), s],
             self.get("local", i).at[1],
         )
+
+    def stages(self):
+        middle = [self.dp_middle] if self.two_step else []
+        back = [self.dp_back_middle] if self.two_step else []
+        return [self.dp_start, *middle, self.z_start, self.z_back, self.dp_back, *back, self.core_back]
 
     def core_start(self):
         for i in range(self.count):
@@ -418,24 +463,37 @@
                     for j in range(self.groups - 1):
                         total = total + box[j, p].astype(F32)
                     half[p] = total.astype(wire)
-            self.start("b", i)
+            self.start("b1" if self.two_step else "b", i)
+
+    def dp_middle(self):
+        here = lax.axis_index("dp")
+        x, y = lax.rem(here, 2), here // 2
+        for i in range(self.count):
+            self.arrive("b1", i)
+            half, box, wire = self.get("half", i), self.get("first", i), self.wires[i]
+            h = self.shapes[i][0] // 2
+            for n in range(2):
+                for who, at, part in ((2 * n + x, pl.ds(0, h), n), (2 * y + n, pl.ds(h, h), 2 + n)):
+                    total = half[who, at, :].astype(F32) + box[part].astype(F32)
+                    half[who, at, :] = total.astype(wire)
+            self.start("b2", i)
 
     def z_start(self):
         here = lax.axis_index("dp")
         for i in range(self.count):
-            self.arrive("b", i)
-            half, box, cut, wire = (
-                self.get("half", i),
-                self.get("dp", i),
-                self.get("cut", i),
-                self.wires[i],
-            )
-            slim = self.shapes[i][0] // self.streams
+            self.arrive("b2" if self.two_step else "b", i)
+            half, cut, wire = self.get("half", i), self.get("cut", i), self.wires[i]
+            chunk = self.shapes[i][0]
+            slim = chunk // self.streams
             for z in range(self.streams):
                 at = slice(z * slim, (z + 1) * slim)
                 total = half[here, at, :].astype(F32)
-                for d in range(self.size - 1):
-                    total = total + box[d, at, :].astype(F32)
+                if self.two_step:
+                    which, first = divmod(z * slim, chunk // 2)
+                    total = total + self.get("second", i)[which, first : first + slim].astype(F32)
+                else:
+                    for d in range(self.size - 1):
+                        total = total + self.get("dp", i)[d, at, :].astype(F32)
                 cut[z] = total.astype(wire)
             self.start("c", i)
 
@@ -455,17 +513,22 @@
         for i in range(self.count):
             self.keep(i).wait()
             self.arrive("d", i)
-            self.start("e", i)
+            self.start("e1" if self.two_step else "e", i)
+
+    def dp_back_middle(self):
+        for i in range(self.count):
+            self.arrive("e1", i)
+            self.start("e2", i)
 
     def core_back(self):
         for i in range(self.count):
-            self.arrive("e", i)
+            self.arrive("e2" if self.two_step else "e", i)
             self.start("f", i)
 
     def end(self):
         for i in range(self.count):
             self.arrive("f", i)
-            for kind in "abcdef" if self.over_cores else "bcdef":
+            for kind in self.kinds():
                 for copy in self.copies(kind, i):
                     copy.wait_send()
 
@@ -494,6 +557,11 @@
         greet(unique(self.jobs + self.others))
         for job, refs in self.each(sources, targets, scratch):
             job.first(*refs)
+
+    def middle(self, sources, targets, scratch):
+        for job, refs in self.each(sources, targets, scratch):
+            if isinstance(job, Gather):
+                job.middle(*refs)
 
     def last(self, sources, targets, scratch):
         for job, refs in self.each(sources, targets, scratch):
@@ -529,6 +597,7 @@
         up_bin[:, i : i + 512] = binary_columns(up_ref[:, i : i + 512])
     for i in range(0, down_ref.shape[1], 128):
         down_bin[:, i : i + 128] = binary_columns(down_ref[:, i : i + 128])
+    moves.middle(sources, targets, scratch)
     moves.last(sources, targets, scratch)
 
 
@@ -593,6 +662,10 @@
         if keep:
             for i in range(0, seq, 256):
                 active_ref[i : i + 256, :] = squash(x_ref[i : i + 256, :].astype(F32)).astype(BF)
+
+    @pl.when((pair == pairs - 1) & (step == steps - 2))
+    def _():
+        moves.middle(sources, targets, scratch)
 
     @pl.when(step == 0)
     def _():
@@ -799,7 +872,7 @@
     sources, rest = rest[:n_early], rest[n_early:]
     grad_ref, *rest = rest
     early_out, rest = rest[:n_early], rest[n_early:]
-    late_out, (sum_ref, *rest) = rest[: len(late)], rest[len(late) :]
+    late_out, (gain_ref, bias_ref, shift_ref, *rest) = rest[: len(late)], rest[len(late) :]
     have = bag.bind(rest)
     at = 0
     for job in early:
@@ -822,7 +895,7 @@
     v_aug, dk_acc, dv_acc, grams = have["v_aug"], have["dk_acc"], have["dv_acc"], have["grams"]
     dq_all, d_act, active, weights = have["dq_all"], have["d_act"], have["active"], have["weights"]
     d_one, x_rows = have["d_one"], have["x_rows"]
-    edges, in_big = have["edges"], have["in_big"]
+    edges, in_big, pair_box = have["edges"], have["in_big"], have["pair_box"]
     along_z, cores, along_dp = stream_peers(streams, groups), core_peers(groups), dp_peers()
 
     def loads():
@@ -866,13 +939,25 @@
 
     at_time(0, begin)
     unit = total_time / 16
+    left = []
     for n, job in enumerate(early):
-        for when, work in zip(EARLY_TIMES[n], (job.dp_start, job.z_start, job.z_back, job.dp_back)):
+        stages, times = job.stages(), EARLY_TIMES[n]
+        if not job.two_step:
+            times = times[:1] + times[2:5] + times[6:]
+        for when, work in zip(times, stages):
             at_time(int(when * unit), work)
+        left.append(stages[len(times) :])
     for p, job in enumerate(late[:-1]):
         first = (p + 1) * steps
-        for when, work in zip(LATE_TIMES, (job.dp_start, job.z_start, job.z_back, job.dp_back)):
+        for when, work in zip(LATE_TIMES, job.stages()):
             at_time(first + when, work)
+        left.append(job.stages()[len(LATE_TIMES) :])
+
+    def go_on(count):
+        for unused in range(count):
+            for queue in left:
+                if queue:
+                    queue.pop(0)()
 
     @pl.when(step == 0)
     def _():
@@ -972,16 +1057,23 @@
                 copy.wait()
         columns = slice(p * 128, (p + 1) * 128)
         bins = jnp.concatenate([weights[0, i, :, columns] for i in range(3)], axis=1)
-        if p == 0:
-            d_act[...] = dot(d_pair, bins, NT)
+        if p < pairs - 1:
+            if p == 0:
+                d_act[...] = dot(d_pair, bins, NT)
+            else:
+                d_act[...] += dot(d_pair, bins, NT)
         else:
-            d_act[...] += dot(d_pair, bins, NT)
-        if p == pairs - 1:
-            for j in range(1, groups):
-                other = pl.multiple_of(lax.rem(r + j, groups) * rows, rows)
-                have["outbox"][j - 1] = d_act[pl.ds(other, rows), :].astype(BF)
-            for copy in core_copies():
-                copy.start()
+            pair_box[...] = d_pair
+            for j in range(1, groups + 1):
+                at = pl.ds(pl.multiple_of(lax.rem(r + j, groups) * rows, rows), rows)
+                total = dot(pair_box[at, :], bins, NT)
+                if p > 0:
+                    total = total + d_act[at, :]
+                if j < groups:
+                    have["outbox"][j - 1] = total.astype(BF)
+                    core_copies()[j - 1].start()
+                else:
+                    d_act[at, :] = total
         partial = dot(active[...], d_pair, TN)
         chunk = depth // size
         half = job.get("half", 0)
@@ -1046,6 +1138,9 @@
                 [jnp.where(r == j, vector, 0.0) for j in range(groups)], axis=1
             )
         small_start(0, along_dp, 0)
+        go_on(TAIL[0])
+        last.z_start()
+        last.z_back()
         for copy in core_copies():
             copy.wait_recv()
         shard = rows // streams
@@ -1072,21 +1167,21 @@
                 copy = pltpu.make_async_copy(blocks.at[s], grad_ref.at[s], have["grad_s"].at[0])
             copy.start()
             back_copies.append(copy)
-        for job in early[:1]:
-            job.core_back()
-        last.z_start()
         small[1] = small_sum(0, along_dp, 0)
         small_start(1, along_z, size)
-        for job in late[:-1]:
-            job.core_back()
-        last.z_back()
-        for job in early[1:]:
-            job.core_back()
+        go_on(TAIL[1])
         small[2] = small_sum(1, along_z, size)
         small_start(2, cores, size + streams)
+        go_on(TAIL[2])
         last.dp_back()
-        sum_ref[...] = small_sum(2, cores, size + streams)
+        summed = small_sum(2, cores, size + streams)
+        gain_ref[...] = summed[0:2, :]
+        bias_ref[...] = summed[2:8, :]
+        for i in range(shift_ref.shape[1] // depth):
+            shift_ref[:, i * depth : (i + 1) * depth] = summed[8 + i : 9 + i, :]
+        go_on(TAIL[3])
         last.core_back()
+        go_on(8)
         for copy in back_copies:
             copy.wait()
         for job in early + late:
@@ -1100,8 +1195,10 @@
             copy.wait_send()
 
 
-EARLY_TIMES = ((1, 7, 10, 12), (2, 11, 13, 15))
-LATE_TIMES = (0, 3, 5, 7)
+TWO_STEP = False
+TAIL = (1, 1, 0, 0)
+EARLY_TIMES = ((2, 0, 7, 9, 12), (4, 0, 12, 14))
+LATE_TIMES = (0, 5, 7)
 
 
 def attention_back(
@@ -1123,6 +1220,7 @@
     d_one,
     tokens,
     early_arrays,
+    up_width,
     collective_id,
 ):
     seq, width = queries.shape
@@ -1156,17 +1254,19 @@
     bag.add("small_box", pltpu.VMEM((count,) + small.shape, F32))
     bag.add("small_s", dma(count))
     bag.add("small_r", dma(count))
+    bag.add("pair_box", pltpu.VMEM((seq, 3 * 128), BF))
     bag.add("edges", pltpu.VMEM((2, tile, 128), F32))
     bag.add("in_big", pltpu.VMEM((2, tile, 128), F32))
     early, flat = [], []
     for n, arrays in enumerate(early_arrays):
-        job = Reduce(bag, f"early{n}", streams, groups, [a.shape for a in arrays], True)
+        job = Reduce(bag, f"early{n}", streams, groups, [a.shape for a in arrays], True, TWO_STEP)
         early.append(job)
         flat += [
             a.reshape(groups, size, chunk, cols) for a, (chunk, cols) in zip(arrays, job.shapes)
         ]
     late = [
-        Reduce(bag, f"late{p}", streams, groups, [(depth, 3 * 128)], False) for p in range(pairs)
+        Reduce(bag, f"late{p}", streams, groups, [(depth, 3 * 128)], False, False)
+        for p in range(pairs)
     ]
     part = pl.BlockSpec((tile, 128), lambda p, i: (i, p))
     any_space = pl.BlockSpec(memory_space=pl.ANY)
@@ -1176,6 +1276,7 @@
     def constant(shape):
         return pl.BlockSpec(shape, lambda p, i: (0,) * len(shape))
 
+    small_shapes = [(2, depth), (6, depth), (1, up_width)]
     early_shapes = [shape for job in early for shape in job.out_shapes()]
     late_shapes = [shape for job in late for shape in job.out_shapes()]
     results = pl.pallas_call(
@@ -1196,11 +1297,11 @@
         ]
         + [any_space] * (4 + len(flat)),
         out_specs=[any_space] * (1 + len(early_shapes) + len(late_shapes))
-        + [constant(small.shape)],
+        + [constant(shape) for shape in small_shapes],
         out_shape=[jax.ShapeDtypeStruct((streams, shard, depth), BF)]
         + early_shapes
         + late_shapes
-        + [jax.ShapeDtypeStruct(small.shape, F32)],
+        + [jax.ShapeDtypeStruct(shape, F32) for shape in small_shapes],
         scratch_shapes=list(bag.items.values()),
         compiler_params=remote_params(collective_id),
         name="attention_back",
@@ -1224,13 +1325,13 @@
     )
     grad_tokens, *rest = results
     early_sums = rest[: len(flat)]
-    late_sums = rest[len(flat) : -1]
+    late_sums = rest[len(flat) : -3]
     shapes = [a.shape for arrays in early_arrays for a in arrays]
     return (
         grad_tokens,
         [e.reshape(shape) for e, shape in zip(early_sums, shapes)],
         [l.reshape(groups, depth, 3 * 128) for l in late_sums],
-        rest[-1],
+        rest[-3:],
     )
 
 
@@ -1262,9 +1363,7 @@
     gout_ref,
     gup_ref,
     gdown_ref,
-    ggain_ref,
-    gbias_ref,
-    gub_ref,
+    small_ref,
     *rest,
 ):
     have = bag.bind(rest)
@@ -1287,7 +1386,7 @@
 
     @pl.when(step == 0)
     def _():
-        for ref in (gout_acc, gup_acc, gdown_acc, ggain_ref, gbias_ref, gub_ref):
+        for ref in (gout_acc, gup_acc, gdown_acc, small_ref):
             ref[...] = jnp.zeros_like(ref)
 
     def row(ref, i):
@@ -1373,13 +1472,19 @@
     def total(value):
         return jnp.sum(value, axis=0, keepdims=True)
 
-    ggain_ref[0:1, :] += total(d_hidden * normed_one)
-    ggain_ref[1:2, :] += total(upstream * normed_two)
-    gbias_ref[2:3, :] += total(d_attended.astype(F32))
-    gbias_ref[3:4, :] += total(d_hidden)
-    gbias_ref[4:5, :] += total(d_branch.astype(F32))
-    gbias_ref[5:6, :] += total(upstream)
-    gub_ref[...] += total(d_inner.astype(F32))
+    sums = [
+        (0, d_hidden * normed_one),
+        (1, upstream * normed_two),
+        (4, d_attended.astype(F32)),
+        (5, d_hidden),
+        (6, d_branch.astype(F32)),
+        (7, upstream),
+    ]
+    for i, value in sums:
+        small_ref[i : i + 1, :] += total(value)
+    d_shift = total(d_inner.astype(F32))
+    for i in range(d_shift.shape[1] // depth):
+        small_ref[8 + i : 9 + i, :] += d_shift[:, i * depth : (i + 1) * depth]
 
     @pl.when(step == steps - 1)
     def _():
@@ -1424,7 +1529,7 @@
     def full(shape):
         return pl.BlockSpec(shape, lambda i: (0,) * len(shape))
 
-    out_full = [(depth, depth), (depth, ff), (ff, depth), (2, depth), (6, depth), (1, ff)]
+    out_full = [(depth, depth), (depth, ff), (ff, depth), (16, depth)]
     bag = Bag()
     for name, shape in zip(("gout", "gup", "gdown"), out_full):
         bag.add(name, pltpu.VMEM(shape, F32))
@@ -1463,48 +1568,40 @@
     return 2.0 * grad * slope + matrix * factor
 
 
-def early_latents_kernel(lo, lu, ld, go, gu, gd, oo, ou, od):
+def latent_grads_kernel(pairs, lq, lo, lu, ld, *refs):
+    late, (go, gu, gd, oq, oo, ou, od) = refs[:pairs], refs[pairs:]
+    for p in range(pairs):
+
+        @pl.when(lax.rem(pl.program_id(0), pairs) == p)
+        def _():
+            for i in range(3):
+                oq[i] = latent_columns(lq[i], late[p][0, :, i * 128 : (i + 1) * 128])
+
     oo[...] = latent_columns(lo[...], go[...])
-    ou[...] = latent_columns(lu[...], gu[...])
     od[...] = latent_columns(ld[...], gd[...])
-
-
-def early_latents(latents, grads):
-    steps = 4
-    specs = [
-        pl.BlockSpec((a.shape[0], a.shape[1] // steps), lambda i: (0, i)) for a in latents
-    ]
+    for i in range(0, lu.shape[1], 128):
+        at = slice(i, i + 128)
+        ou[:, at] = latent_columns(lu[:, at], gu[:, at])
+
+
+def latent_grads(latents, late, early):
+    pairs = len(late)
+    groups, depth, wide = late[0].shape
+    steps = groups * pairs
+    qkv = pl.BlockSpec((3, depth, depth // steps), lambda i: (0, 0, i))
+    flat = [pl.BlockSpec((a.shape[0], a.shape[1] // steps), lambda i: (0, i)) for a in latents[1:]]
     return pl.pallas_call(
-        early_latents_kernel,
+        functools.partial(latent_grads_kernel, pairs),
         grid=(steps,),
-        in_specs=specs * 2,
-        out_specs=specs,
+        in_specs=[qkv]
+        + flat
+        + [pl.BlockSpec((1, depth, wide), lambda i: (i // pairs, 0, 0))] * pairs
+        + flat,
+        out_specs=[qkv] + flat,
         out_shape=[jax.ShapeDtypeStruct(a.shape, F32) for a in latents],
         compiler_params=pltpu.CompilerParams(vmem_limit_bytes=VMEM_BYTES),
-        name="early_latents",
-    )(*latents, *grads)
-
-
-def late_latents_kernel(pairs, latent, *refs):
-    grads, out = refs[:pairs], refs[pairs]
-    for p in range(pairs):
-        columns = slice(p * 128, (p + 1) * 128)
-        out[0, :, columns] = latent_columns(latent[0, :, columns], grads[p][0])
-
-
-def late_latents(latent, grads):
-    pairs = len(grads)
-    groups, depth, wide = grads[0].shape
-    spec = pl.BlockSpec((1, depth, pairs * 128), lambda m, j: (m, 0, j))
-    return pl.pallas_call(
-        functools.partial(late_latents_kernel, pairs),
-        grid=(3, groups),
-        in_specs=[spec] + [pl.BlockSpec((1, depth, 128), lambda m, j: (j, 0, m))] * pairs,
-        out_specs=spec,
-        out_shape=jax.ShapeDtypeStruct(latent.shape, F32),
-        compiler_params=pltpu.CompilerParams(vmem_limit_bytes=VMEM_BYTES),
-        name="late_latents",
-    )(latent, *grads)
+        name="latent_grads",
+    )(*latents, *late, *early)
 
 
 def shards(
@@ -1587,7 +1684,7 @@
         3,
         "attention_teacher",
     )
-    output, d_one, d_context, g_out, g_up, g_down, g_gain, g_bias, g_ub = middle(
+    output, d_one, d_context, g_out, g_up, g_down, small = middle(
         streams,
         groups,
         stream_tokens,
@@ -1611,9 +1708,6 @@
         ],
         4,
     )
-    small = jnp.concatenate(
-        [g_gain, g_bias, g_ub.reshape(-1, depth), jnp.zeros((4, depth), F32)], axis=0
-    )
     grads = [[g_up], [g_down, g_out]]
     in_kernel = depth % (16 * blocks * lax.axis_size("dp")) == 0
     grad_tokens, early, late, small = attention_back(
@@ -1635,24 +1729,24 @@
         d_one,
         token_blocks,
         grads if in_kernel else [],
+        latent_up.shape[1],
         6,
     )
     if not in_kernel:
         early = lax.psum((g_up, g_down, g_out), ("dp", "blk"))
-    up_rows = latent_up.shape[1] // depth
-    grad_out, grad_up, grad_down = early_latents(
-        [latent_out, latent_up, latent_down], [early[2], early[0], early[1]]
+    grad_qkv, grad_out, grad_up, grad_down = latent_grads(
+        [latent_qkv, latent_out, latent_up, latent_down], late, [early[2], early[0], early[1]]
     )
     return (
         output,
         grad_tokens,
-        late_latents(latent_qkv, late),
+        grad_qkv,
         grad_out,
         grad_up,
         grad_down,
-        small[0:2],
-        small[2:8],
-        small[8 : 8 + up_rows].reshape(-1),
+        small[0],
+        small[1],
+        small[2].reshape(-1),
     )
 
 

time: 310 us -> 295 us (0.952)
  Pallas kernels: 302 us -> 290 us
    pallas_call x1, Pallas kernels: 112 us -> 106 us  [attention_back(): pl.pallas_call(functools.partial(backward_kernel, streams, groups, tile,...]
    pallas_call x2 -> x1, Pallas kernels: 18.2 us -> 13.8 us  [latent_grads(): pl.pallas_call(functools.partial(latent_grads_kernel, pairs), grid=(steps...]
where the time goes in v5:
time: 295 us; the launch traced here: 298 us
  Pallas kernels  290 us (98%)
  local copies, waits for them, and re-layouts  5.63 us (2%)
    pallas_call x1, Pallas kernels, attention_back(): pl.pallas_call(functools.partial(backward_kernel, streams, groups, tile,...  106 us
    pallas_call x2, Pallas kernels, attention(): pl.pallas_call(functools.partial(forward_kernel, moves, keep, streams, gr...  90.9 us
    pallas_call x1, Pallas kernels, middle(): pl.pallas_call(functools.partial(middle_kernel, streams, groups, bag, til...  41.6 us
    pallas_call x1, Pallas kernels, intake(): pl.pallas_call(functools.partial(intake_kernel, moves, groups), out_shape...  37.7 us
    pallas_call x1, Pallas kernels, latent_grads(): pl.pallas_call(functools.partial(latent_grads_kernel, pairs), grid=(steps...  13.8 us

profile of v5, /device:TPU:0, one launch (start us, length us, event | category | flops | bytes accessed | tf_op | source)
XLA Modules:
  0.0 298.3 jit_solution(10153861314679169293)
XLA Ops:
  0.6 1.3 reshape.86.refs_1_
  1.9 37.7 %intake.1 = (bf16[1,3,512,256]{3,2,1,0:T(8,128)(2,1)}, bf16[512,512]{1,0:T(8,128)(2,1)}, bf16[512,2048]{1,0:T(8,128)(2,1)}, bf16[2048,512]{1,0:T(8,128)(2,1)}, b...) custom-call(bf16[3,512,512]{2,1,0:T(8,128)(2,1)} %lq.1, bf16[512,512]{1,0:T(8,128)(2,1)} %lo.1, ...), custom_call_target="tpu_custom_call" | custom-call | tf_op jit(solution)/shard_map/intake/pallas_call | solution.py:608
  39.6 1.3 convert_element_type.5
  40.9 40.9 %attention_student.1 = (bf16[2048,256]{1,0:T(8,128)(2,1)}, bf16[2048,256]{1,0:T(8,128)(2,1)}, bf16[2,2,1024,128]{3,2,1,0:T(8,128)(2,1)}, bf16[2048,256]{1,0:T(8,...) custom-call(bf16[2048,512]{1,0:T(8,128)(2,1)} %bitcast.18, ...), custom_call_target="tpu_custom_call" | custom-call | tf_op jit(solution)/shard_map/attention_student/pallas_call | solution.py:828
  81.8 50.0 %attention_teacher.1 = (bf16[2048,256]{1,0:T(8,128)(2,1)}, bf16[2048,256]{1,0:T(8,128)(2,1)}, bf16[2,2,1024,128]{3,2,1,0:T(8,128)(2,1)}, bf16[4,256,512]{2,1,0:T(8,128)(2,1)}, bf16[4,512,512]{2,1,0:T(8,128)(2,1)}) custom-call(bf16[2048,512]{1,0:T(8,128)(2,1)} %bitcast.20, bf16[4,3,128,512]{3,2,1,0:T(8,128)(2,1)} %get-tuple-element.56.w_ref, ...), custom_call_target="tpu_custom_call" | custom-call | tf_op jit(solution)/shard_map/attention_teacher/pallas_call | solution.py:828
  131.8 41.6 %middle.1 = (bf16[4,256,512]{2,1,0:T(8,128)(2,1)}, f32[1024,512]{1,0:T(8,128)}, bf16[2048,256]{1,0:T(8,128)(2,1)}, bf16[512,512]{1,0:T(8,128)(2,1)}, bf16[512,20...) custom-call(bf16[2048,512]{1,0:T(8,128)(2,1)} %bitcast.19, bf16[2048,512]{1,0:T(8,128)(2,1)} %bitcast.21, ...), custom_call_target="tpu_custom_call" | custom-call | tf_op jit(solution)/shard_map/middle/pallas_call | solution.py:1541
  173.4 106.5 %attention_back.1 = (bf16[4,256,512]{2,1,0:T(8,128)(2,1)}, bf16[2,4,4,16,2048]{4,3,2,1,0:T(8,128)(2,1)}, bf16[2,4,4,64,512]{4,3,2,1,0:T(8,128)(2,1)}, bf16[2,4,4...) custom-call(bf16[4,2048,2048]{2,1,0:T(8,128)(2,1)} %get-tuple-elemen, ...), custom_call_target="tpu_custom_call" | custom-call | tf_op jit(solution)/shard_map/attention_back/pallas_call | solution.py:1282
  279.9 0.0 copy-start
  279.9 13.8 %latent_grads.1 = (f32[3,512,512]{2,1,0:T(8,128)}, f32[512,512]{1,0:T(8,128)}, f32[512,2048]{1,0:T(8,128)}, f32[2048,512]{1,0:T(8,128)}) custom-call(bf16[3,512,512]{2,1,0:T(8,128)(2,1)} %lq.1, bf16[512,512]{1,0:T(8,128)(2,1)} %lo.1, bf16[512,2048]{1,0:T(8,128)(2,1)} %lu.1, bf16[2048,512]{1,0:T(8,128)(2,1)} %ld.1, bf16[2,512,384]{2,1,0:T(8,128)(2,1)} %bitcast.29, ...), custom_call_target="tpu_custom_call" | custom-call | tf_op jit(solution)/shard_map/latent_grads/pallas_call | solution.py:1593
  293.7 0.0 copy-start.1
  293.7 0.0 copy-done
  293.7 0.0 copy-start.4
  293.7 0.0 copy-start.2
  293.7 0.0 copy-start.3
  293.7 1.0 copy.32
  294.7 0.6 copy-done.1
  295.3 1.0 copy.33
  296.3 0.0 copy-done.4
  296.3 0.6 copy.34
  296.9 0.0 copy-done.2
  296.9 0.6 copy.35
  297.5 0.0 copy-done.3
  297.5 0.6 copy.36
Async XLA Ops:
  279.9 13.8 %copy-start = (bf16[4,256,512]{2,1,0:T(8,128)(2,1)S(1)}, bf16[4,256,512]{2,1,0:T(8,128)(2,1)}, u32[]{:S(2)}) copy-start(bf16[4,256,512]{2,1,0:T(8,128)(2,1)} %get-tuple-element.104) | copy-start | bytes 3145732
  293.7 1.6 copy-start.1
  293.7 2.6 copy-start.4
  293.7 3.1 %copy-start.2 = (f32[6,512]{1,0:T(8,128)S(1)}, f32[6,512]{1,0:T(8,128)}, u32[]{:S(2)}) copy-start(f32[6,512]{1,0:T(8,128)} %get-tuple-element.111) | copy-start | bytes 36868
  293.7 3.7 %copy-start.3 = (f32[1,2048]{1,0:T(1,128)S(1)}, f32[1,2048]{1,0:T(1,128)}, u32[]{:S(2)}) copy-start(f32[1,2048]{1,0:T(1,128)} %get-tuple-element.94) | copy-start | bytes 24580
